TPU v7x, 32 devices: a whole 2x2x4 slice. The times are simulated.
32 devices in a mesh: gz: 8 (over z, x), xy: 4 (over y, core).
Axes of the slice: x: 2, y: 2, z: 4, core: 2. Of those that a mesh axis runs over, the one named last changes fastest.
Arguments:
- images: bfloat16 [8, 640, 640], P('gz', 'xy'), may hold values from -6 to 6
- peak_code: int32 [8, 4, 4], P('gz', 'xy'), may hold values from 0 to 24
- cell_block: int32 [8, 4, 4], P('gz', 'xy'), may hold values from 0 to 27
- cell_offset: int32 [8, 4, 4], P('gz', 'xy'), may hold values from 0 to 1599
- valid_patch: int32 [8, 4, 4], P('gz', 'xy'), may hold values from 0 to 1, as said below
Outputs:
- flow: float32 [2, 8, 4, 4], P(None, 'gz', 'xy')
- node_shift: float32 [2, 8, 16, 8], P(None, 'gz', 'xy')
Inputs may be any that keep to these rules, and one draw needn't show every extreme that they name: `valid_patch`: 1 where the patch lies on tissue, 0 elsewhere; coverage rises with the patch row.
All inputs are finite; a program needn't handle non-finite values.
Results may differ from a plain program's by a relative error of at most 0.0003.
Values may be sent and summed in bfloat16 or wider, within the bound.
No kernel may reach another device: no remote copies, remote signals or barrier semaphores. Data moves between devices by JAX's collectives and lax.ppermute only.
A program may use at most 64 MiB of HBM per device.

v0:
```python
import math

import jax
import jax.numpy as jnp
from jax import lax
from jax.sharding import PartitionSpec as P

PATCH_SIZE = 160
BAND_ROWS = 4
NODE_COLS = 8
CELL_SUBDIV = 40
SPRING_STEPS = 4


rest_length = 40.0
spring_stiff = 1.0
flow_stiff = 0.5
time_step = 0.5
damping = 0.6
highest = lax.Precision.HIGHEST


def shifted(block, axis, distance):
    devices = range(lax.axis_size(axis))
    route = [(i - distance, i) for i in devices if i - distance in devices]
    return lax.ppermute(block, axis, route)


def carried_in(x, axis, combine, identity):
    size, place = (lax.axis_size(axis), lax.axis_index(axis))
    everything = lax.all_gather(x, axis)
    start = jnp.broadcast_to(jnp.asarray(identity, x.dtype), x.shape)

    def step(k, before):
        reached = k < place
        new = combine(before, everything[k])
        return jnp.where(reached, new, before)

    return lax.fori_loop(0, size, step, start)


def with_halo(x, sides, width):
    for axis, dim in sides:
        size, length = (lax.axis_size(axis), x.shape[dim])
        up = [(i, (i + 1) % size) for i in range(size - 1)]
        down = [(j, i) for i, j in up]
        last = lax.slice_in_dim(x, length - width, length, axis=dim)
        initial = lax.slice_in_dim(x, 0, width, axis=dim)
        before = lax.ppermute(last, axis, up)
        after = lax.ppermute(initial, axis, down)
        x = jnp.concatenate([before, x, after], axis=dim)
    return x


def spring_force(field, live):
    cols = field.shape[3]
    zero_row = jnp.zeros_like(field[:, :, :1])
    zero_col = jnp.zeros_like(field[:, :, :, :1])
    nothing = jnp.zeros((1,), field.dtype)
    above = jnp.concatenate([zero_row, field[:, :, :-1]], axis=2)
    below = jnp.concatenate([field[:, :, 1:], zero_row], axis=2)
    left = jnp.concatenate([zero_col, field[:, :, :, :-1]], axis=3)
    right = jnp.concatenate([field[:, :, :, 1:], zero_col], axis=3)
    live_above = jnp.concatenate([nothing, live[:-1]])
    live_below = jnp.concatenate([live[1:], nothing])
    column = jnp.arange(cols, dtype=jnp.int32)
    live_left = (column > 0).astype(field.dtype)
    live_right = (column < cols - 1).astype(field.dtype)
    rest_zero = math.sqrt(rest_length * rest_length + 1.0)
    push_y = jnp.zeros_like(field[0])
    push_x = jnp.zeros_like(field[0])
    pairs = (
        (above, live_above[:, None], -rest_length, 0.0),
        (below, live_below[:, None], rest_length, 0.0),
        (left, live_left[None, :], 0.0, -rest_length),
        (right, live_right[None, :], 0.0, rest_length),
    )
    for neighbour, present, rest_y, rest_x in pairs:
        gap_y = rest_y + neighbour[0] - field[0]
        gap_x = rest_x + neighbour[1] - field[1]
        length = jnp.sqrt(gap_y * gap_y + gap_x * gap_x + 1.0)
        tension = spring_stiff * (length - rest_zero) / length * present
        push_y = push_y + tension * gap_y
        push_x = push_x + tension * gap_x
    return jnp.stack([push_y, push_x])


def cut_patches(block, size):
    depth, pixels, breadth = block.shape
    rows_here = pixels // size
    cols_here = breadth // size
    shaped = block.reshape(depth, rows_here, size, cols_here, size).transpose(0, 1, 3, 2, 4)
    return shaped.reshape(depth * rows_here * cols_here, size, size)


def correlate(first, second, code, size):
    source = jnp.arange(size, dtype=jnp.int32)[:, None]
    dest = jnp.arange(size, dtype=jnp.int32)[None, :]
    lags = jnp.arange(7, dtype=jnp.int32) - 3
    diagonals = (((dest - source)[None] - lags[:, None, None]) % size == 0).astype(jnp.float32)
    sums = []
    for lag_row in range(-3, 4):
        rolled = jnp.roll(second, -lag_row, axis=1)
        cross = jnp.einsum("nyx,nyz->nxz", first, rolled, preferred_element_type=jnp.float32)
        sums.append(jnp.einsum("nxz,dxz->nd", cross, diagonals, precision=highest))
    table = jnp.stack(sums, axis=1) / float(size)
    steps = jnp.arange(3, dtype=jnp.int32) - 1
    seven = jnp.arange(7, dtype=jnp.int32)
    lag_y = code[:, None] // 5 - 2 + steps[None, :] + 3
    lag_x = code[:, None] % 5 - 2 + steps[None, :] + 3
    pick_y = (lag_y[:, :, None] == seven).astype(jnp.float32)
    pick_x = (lag_x[:, :, None] == seven).astype(jnp.float32)
    return jnp.einsum("nay,nyx,nbx->nab", pick_y, table, pick_x, precision=highest)


def on_device(images, peak_code, cell_block, cell_offset, valid_patch):
    slab, strip_pixels, width = images.shape
    size = PATCH_SIZE
    rows_local = strip_pixels // size
    cols_local = width // size
    count = rows_local * cols_local
    cells = cut_patches(images, size).reshape(slab, count, size, size)
    code_all = peak_code.reshape(slab, count)
    following = shifted(images[0], "gz", -1)
    tail = correlate(cells[-1], cut_patches(following[None], size), code_all[-1], size)
    pieces_done = tail[None]
    corr = pieces_done.reshape(slab * count, 3, 3)
    code = code_all.reshape(slab * count)
    num_y = jnp.sum(corr[:, 2, :] - corr[:, 0, :], axis=-1)
    num_x = jnp.sum(corr[:, :, 2] - corr[:, :, 0], axis=-1)
    energy = 1.0 + jnp.sum(corr * corr, axis=(-2, -1))
    flow_y = (code // 5 - 2).astype(jnp.float32) + num_y / energy
    flow_x = (code % 5 - 2).astype(jnp.float32) + num_x / energy
    flow = jnp.stack([flow_y, flow_x]).reshape(2, slab, rows_local, cols_local)
    block = cell_block.reshape(slab, count)
    offset = cell_offset.reshape(slab, count)
    valid = valid_patch.reshape(slab, count).astype(jnp.float32)
    cell_row = block // (NODE_COLS - 1)
    cell_col = block % (NODE_COLS - 1)
    frac_y = (offset // CELL_SUBDIV).astype(jnp.float32) / CELL_SUBDIV
    frac_x = (offset % CELL_SUBDIV).astype(jnp.float32) / CELL_SUBDIV
    row_index = jnp.arange(BAND_ROWS + 1, dtype=jnp.int32)
    col_index = jnp.arange(NODE_COLS, dtype=jnp.int32)
    weight_y = (cell_row[..., None] == row_index).astype(jnp.float32) * (1.0 - frac_y)[
        ..., None
    ] + (cell_row[..., None] + 1 == row_index).astype(jnp.float32) * frac_y[..., None]
    weight_x = (cell_col[..., None] == col_index).astype(jnp.float32) * (1.0 - frac_x)[
        ..., None
    ] + (cell_col[..., None] + 1 == col_index).astype(jnp.float32) * frac_x[..., None]
    values = jnp.stack(
        [flow_y.reshape(slab, count) * valid, flow_x.reshape(slab, count) * valid, valid]
    )
    gathered = jnp.einsum("qsp,spi,spj->qsij", values, weight_y, weight_x, precision=highest)
    spill = shifted(gathered[:, :, BAND_ROWS], "xy", 1)
    summed = gathered[:, :, :BAND_ROWS].at[:, :, 0].add(spill)
    target = summed[:2] / (1.0 + summed[2])
    totals = jnp.sum(target, axis=1)
    carry = carried_in(totals, "gz", lambda earlier, later: earlier + later, jnp.zeros_like(totals))
    cumulative = carry[:, None] + jnp.cumsum(target, axis=1) - target
    band = lax.axis_index("xy")
    grid_rows = BAND_ROWS * lax.axis_size("xy")
    global_row = band * BAND_ROWS + jnp.arange(-1, BAND_ROWS + 1, dtype=jnp.int32)
    live = ((global_row >= 0) & (global_row < grid_rows)).astype(jnp.float32)
    moving = cumulative
    velocity = jnp.zeros_like(cumulative)
    for step in range(SPRING_STEPS):
        padded = with_halo(moving, (("xy", 2),), 1)
        force = spring_force(padded, live)[:, :, 1:-1] + flow_stiff * (cumulative - moving)
        velocity = damping * velocity + time_step * force
        moving = moving + time_step * velocity
    return (flow, moving)


def solution(mesh):
    return jax.shard_map(
        on_device,
        mesh=mesh,
        in_specs=(
            P("gz", "xy", None),
            P("gz", "xy", None),
            P("gz", "xy", None),
            P("gz", "xy", None),
            P("gz", "xy", None),
        ),
        out_specs=(P(None, "gz", "xy", None), P(None, "gz", "xy", None)),
        check_vma=False,
    )
```

profile of v0, /device:TPU:0, one launch (start us, length us, event | category | flops | bytes accessed | tf_op | source)
XLA Modules:
  0.0 103.3 jit_solution(2221307481037804851)
XLA Ops:
  0.7 1.4 %collective-permute-start = (bf16[160,640]{1,0:T(8,128)(2,1)}, bf16[160,640]{1,0:T(8,128)(2,1)S(1)}, u32[]{:S(2)}, u32[]{:S(2)}) collective-permute-start(bf16[160,640]{1,0:T(8,128)(2,1)} %bitcast.178), channel_id=1, source_target_pairs={{4,0},{8,4},{12,8},{16,12},{20,16},{24,20},{28,24},{5,1},{9,5},{13... | collective-permute-start | bytes 614408 | tf_op jit(solution)/shard_map/ppermute | solution.py:26
  4.4 6.5 %collective-permute-done = bf16[160,640]{1,0:T(8,128)(2,1)S(1)} collective-permute-done((bf16[160,640]{1,0:T(8,128)(2,1)}, bf16[160,640]{1,0:T(8,128)(2,1)S(1)}, u32[]{:S(2)}, u32[]{:S(2)}) %collective-permute-start) | collective-permute-done | bytes 204832 | tf_op jit(solution)/shard_map/ppermute | solution.py:26
  15.3 1.2 %copy.22 = f32[4,160,160]{2,0,1:T(4,128)} copy(f32[4,160,160]{1,2,0:T(8,128)S(1)} %convolution_bitcast_fusion.4) | data formatting | bytes 819200 | tf_op jit(solution)/shard_map/nyx,nyz->nxz/dot_general | solution.py:104
  17.9 2.2 %fusion.148 = f32[4,7,1]{1,0,2:T(4,128)S(1)} fusion(f32[4,160,160]{2,0,1:T(4,128)S(1)} %copy-done.1, s32[7]{0:T(128)S(1)} %iota_add_fusion.1, s32[160,160]{1,0:T(8,128)S(1)} %copy-done.6), kind=kOutput, calls=%fused_computation.281 | convolution fusion | flops 10035200 | bytes 512140 | tf_op jit(solution)/shard_map/nxz,dxz->nd/dot_general | solution.py:105
  20.1 2.2 %fusion.146 = f32[4,7,1]{1,0,2:T(4,128)S(1)} fusion(f32[4,160,160]{2,0,1:T(4,128)S(1)} %copy-done.2, s32[7]{0:T(128)S(1)} %iota_add_fusion.1, s32[160,160]{1,0:T(8,128)S(1)} %copy-done.6), kind=kOutput, calls=%fused_computation.280 | convolution fusion | flops 10035200 | bytes 512140 | tf_op jit(solution)/shard_map/nxz,dxz->nd/dot_general | solution.py:105
  23.0 2.2 %fusion.143 = f32[4,7,1]{1,0,2:T(4,128)S(1)} fusion(f32[4,160,160]{2,0,1:T(4,128)S(1)} %copy.27, s32[7]{0:T(128)S(1)} %iota_add_fusion.1, s32[160,160]{1,0:T(8,128)S(1)} %copy-done.6), kind=kOutput, calls=%fused_computation.279 | convolution fusion | flops 10035200 | bytes 512140 | tf_op jit(solution)/shard_map/nxz,dxz->nd/dot_general | solution.py:105
  25.8 2.2 %fusion.141 = f32[4,7,1]{1,0,2:T(4,128)S(1)} fusion(f32[4,160,160]{2,0,1:T(4,128)S(1)} %copy.28, s32[7]{0:T(128)S(1)} %iota_add_fusion.1, s32[160,160]{1,0:T(8,128)S(1)} %copy-done.6), kind=kOutput, calls=%fused_computation.278 | convolution fusion | flops 10035200 | bytes 512140 | tf_op jit(solution)/shard_map/nxz,dxz->nd/dot_general | solution.py:105
  28.7 2.3 %fusion.139 = f32[4,7,1]{1,0,2:T(4,128)S(1)} fusion(f32[4,160,160]{2,0,1:T(4,128)S(1)} %copy.29, s32[7]{0:T(128)S(1)} %iota_add_fusion.1, s32[160,160]{1,0:T(8,128)S(1)} %copy-done.6), kind=kOutput, calls=%fused_computation.277 | convolution fusion | flops 10035200 | bytes 512140 | tf_op jit(solution)/shard_map/nxz,dxz->nd/dot_general | solution.py:105
  32.3 2.2 %fusion.150 = f32[4,7,1]{1,0,2:T(4,128)S(1)} fusion(f32[4,160,160]{2,0,1:T(4,128)S(1)} %copy.21, s32[7]{0:T(128)S(1)} %iota_add_fusion.1, s32[160,160]{1,0:T(8,128)S(1)} %copy-done.7), kind=kOutput, calls=%fused_computation.282 | convolution fusion | flops 10035200 | bytes 512140 | tf_op jit(solution)/shard_map/nxz,dxz->nd/dot_general | solution.py:105
  34.4 2.3 %fusion.4 = f32[4,7,1]{1,0,2:T(4,128)S(1)} fusion(f32[4,160,160]{2,1,0:T(8,128)S(1)} %copy-done, s32[7]{0:T(128)S(1)} %iota_add_fusion.1, s32[160,160]{1,0:T(8,128)S(1)} %copy-done.7), kind=kOutput, calls=%fused_computation.14 | convolution fusion | flops 10035200 | bytes 512140 | tf_op jit(solution)/shard_map/nxz,dxz->nd/dot_general | solution.py:105
  38.1 1.3 %collective-permute-start.1 = (f32[3,1,8]{2,1,0:T(1,128)S(1)}, f32[3,1,8]{2,1,0:T(1,128)S(1)}, u32[]{:S(2)}, u32[]{:S(2)}) collective-permute-start(f32[3,1,8]{2,1,0:T(1,128)S(1)} %squeeze.12), channel_id=1, source_target_pairs={{0,1},{1,2},{2,3},{4,5},{5,6},{6,7},{8,9},{9,10},{10,11},{12,13},{... | collective-permute-start | bytes 296 | tf_op jit(solution)/shard_map/ppermute | solution.py:26
  40.3 31.0 %all-gather = f32[16,1,4,8]{3,2,1,0:T(4,128)S(1)} all-gather(f32[2,1,4,8]{3,2,1,0:T(4,128)S(1)} %copy.39), channel_id=2, replica_groups=mesh['gz'=8,'xy'=4] {'gz'}, dimensions={0}, use_global_device_ids=true | all-gather | bytes 2304 | tf_op jit(solution)/shard_map/all_gather | solution.py:31
  71.6 1.3 %collective-permute-start.2 = (f32[2,1,1,8]{3,0,2,1:T(2,128)S(1)}, f32[2,1,1,8]{3,0,2,1:T(2,128)S(1)}, u32[]{:S(2)}, u32[]{:S(2)}) collective-permute-start(f32[2,1,1,8]{3,0,2,1:T(2,128)S(1)} %get-tuple-element.207), channel_id=1, source_target_pairs={{0,1},{1,2},{2,3},{4,5},{5,6},{6,7},{8,9},{9,10},{10,11},{12,13},{... | collective-permute-start | bytes 200 | tf_op jit(solution)/shard_map/ppermute | solution.py:49
  72.9 1.3 %collective-permute-start.3 = (f32[2,1,1,8]{3,0,2,1:T(2,128)S(1)}, f32[2,1,1,8]{3,0,2,1:T(2,128)S(1)}, u32[]{:S(2)}, u32[]{:S(2)}) collective-permute-start(f32[2,1,1,8]{3,0,2,1:T(2,128)S(1)} %get-tuple-element.208), channel_id=1, source_target_pairs={{1,0},{2,1},{3,2},{5,4},{6,5},{7,6},{9,8},{10,9},{11,10},{13,12},{... | collective-permute-start | bytes 200 | tf_op jit(solution)/shard_map/ppermute | solution.py:50
  74.2 6.3 %collective-permute-done.3 = f32[2,1,1,8]{3,0,2,1:T(2,128)S(1)} collective-permute-done((f32[2,1,1,8]{3,0,2,1:T(2,128)S(1)}, f32[2,1,1,8]{3,0,2,1:T(2,128)S(1)}, u32[]{:S(2)}, u32[]{:S(2)}) %collective-permute-start.3) | collective-permute-done | bytes 96 | tf_op jit(solution)/shard_map/ppermute | solution.py:50
  80.8 4.3 %collective-permute-start.4 = (f32[2,1,1,8]{3,0,2,1:T(2,128)S(1)}, f32[2,1,1,8]{3,0,2,1:T(2,128)S(1)}, u32[]{:S(2)}, u32[]{:S(2)}) collective-permute-start(f32[2,1,1,8]{3,0,2,1:T(2,128)S(1)} %get-tuple-element.205), channel_id=1, source_target_pairs={{0,1},{1,2},{2,3},{4,5},{5,6},{6,7},{8,9},{9,10},{10,11},{12,13},{... | collective-permute-start | bytes 200 | tf_op jit(solution)/shard_map/ppermute | solution.py:49
  85.0 1.3 %collective-permute-start.5 = (f32[2,1,1,8]{3,0,2,1:T(2,128)S(1)}, f32[2,1,1,8]{3,0,2,1:T(2,128)S(1)}, u32[]{:S(2)}, u32[]{:S(2)}) collective-permute-start(f32[2,1,1,8]{3,0,2,1:T(2,128)S(1)} %get-tuple-element.206), channel_id=1, source_target_pairs={{1,0},{2,1},{3,2},{5,4},{6,5},{7,6},{9,8},{10,9},{11,10},{13,12},{... | collective-permute-start | bytes 200 | tf_op jit(solution)/shard_map/ppermute | solution.py:50
  86.4 1.7 %collective-permute-done.5 = f32[2,1,1,8]{3,0,2,1:T(2,128)S(1)} collective-permute-done((f32[2,1,1,8]{3,0,2,1:T(2,128)S(1)}, f32[2,1,1,8]{3,0,2,1:T(2,128)S(1)}, u32[]{:S(2)}, u32[]{:S(2)}) %collective-permute-start.5) | collective-permute-done | bytes 96 | tf_op jit(solution)/shard_map/ppermute | solution.py:50
  88.4 3.8 %collective-permute-start.6 = (f32[2,1,1,8]{3,0,2,1:T(2,128)S(1)}, f32[2,1,1,8]{3,0,2,1:T(2,128)S(1)}, u32[]{:S(2)}, u32[]{:S(2)}) collective-permute-start(f32[2,1,1,8]{3,0,2,1:T(2,128)S(1)} %get-tuple-element.203), channel_id=1, source_target_pairs={{0,1},{1,2},{2,3},{4,5},{5,6},{6,7},{8,9},{9,10},{10,11},{12,13},{... | collective-permute-start | bytes 200 | tf_op jit(solution)/shard_map/ppermute | solution.py:49
  92.2 1.3 %collective-permute-start.7 = (f32[2,1,1,8]{3,0,2,1:T(2,128)S(1)}, f32[2,1,1,8]{3,0,2,1:T(2,128)S(1)}, u32[]{:S(2)}, u32[]{:S(2)}) collective-permute-start(f32[2,1,1,8]{3,0,2,1:T(2,128)S(1)} %get-tuple-element.204), channel_id=1, source_target_pairs={{1,0},{2,1},{3,2},{5,4},{6,5},{7,6},{9,8},{10,9},{11,10},{13,12},{... | collective-permute-start | bytes 200 | tf_op jit(solution)/shard_map/ppermute | solution.py:50
  93.5 1.7 %collective-permute-done.7 = f32[2,1,1,8]{3,0,2,1:T(2,128)S(1)} collective-permute-done((f32[2,1,1,8]{3,0,2,1:T(2,128)S(1)}, f32[2,1,1,8]{3,0,2,1:T(2,128)S(1)}, u32[]{:S(2)}, u32[]{:S(2)}) %collective-permute-start.7) | collective-permute-done | bytes 96 | tf_op jit(solution)/shard_map/ppermute | solution.py:50
  95.6 3.8 %collective-permute-start.8 = (f32[2,1,1,8]{3,0,2,1:T(2,128)S(1)}, f32[2,1,1,8]{3,0,2,1:T(2,128)S(1)}, u32[]{:S(2)}, u32[]{:S(2)}) collective-permute-start(f32[2,1,1,8]{3,0,2,1:T(2,128)S(1)} %get-tuple-element.201), channel_id=1, source_target_pairs={{0,1},{1,2},{2,3},{4,5},{5,6},{6,7},{8,9},{9,10},{10,11},{12,13},{... | collective-permute-start | bytes 200 | tf_op jit(solution)/shard_map/ppermute | solution.py:49
  99.4 1.3 %collective-permute-start.9 = (f32[2,1,1,8]{3,0,2,1:T(2,128)S(1)}, f32[2,1,1,8]{3,0,2,1:T(2,128)S(1)}, u32[]{:S(2)}, u32[]{:S(2)}) collective-permute-start(f32[2,1,1,8]{3,0,2,1:T(2,128)S(1)} %get-tuple-element.202), channel_id=1, source_target_pairs={{1,0},{2,1},{3,2},{5,4},{6,5},{7,6},{9,8},{10,9},{11,10},{13,12},{... | collective-permute-start | bytes 200 | tf_op jit(solution)/shard_map/ppermute | solution.py:50
  100.7 1.7 %collective-permute-done.9 = f32[2,1,1,8]{3,0,2,1:T(2,128)S(1)} collective-permute-done((f32[2,1,1,8]{3,0,2,1:T(2,128)S(1)}, f32[2,1,1,8]{3,0,2,1:T(2,128)S(1)}, u32[]{:S(2)}, u32[]{:S(2)}) %collective-permute-start.9) | collective-permute-done | bytes 96 | tf_op jit(solution)/shard_map/ppermute | solution.py:50
  (118 shorter events, 15.6 us)
Async XLA Ops:
  0.6 3.3 %copy-start.8 = (s32[1,1,4]{2,1,0:T(1,128)S(1)}, s32[1,1,4]{2,1,0:T(1,128)}, u32[]{:S(2)}) copy-start(s32[1,1,4]{2,1,0:T(1,128)} %param.10) | copy-start | bytes 52
  0.6 3.4 %copy-start.11 = (s32[1,1,4]{2,1,0:T(1,128)S(1)}, s32[1,1,4]{2,1,0:T(1,128)}, u32[]{:S(2)}) copy-start(s32[1,1,4]{2,1,0:T(1,128)} %param.13) | copy-start | bytes 52
  0.7 3.4 %copy-start.9 = (s32[1,1,4]{2,1,0:T(1,128)S(1)}, s32[1,1,4]{2,1,0:T(1,128)}, u32[]{:S(2)}) copy-start(s32[1,1,4]{2,1,0:T(1,128)} %param.11) | copy-start | bytes 52
  0.7 3.4 %copy-start.10 = (s32[1,1,4]{2,1,0:T(1,128)S(1)}, s32[1,1,4]{2,1,0:T(1,128)}, u32[]{:S(2)}) copy-start(s32[1,1,4]{2,1,0:T(1,128)} %param.12) | copy-start | bytes 52
  0.7 10.3 %collective-permute-start = (bf16[160,640]{1,0:T(8,128)(2,1)}, bf16[160,640]{1,0:T(8,128)(2,1)S(1)}, u32[]{:S(2)}, u32[]{:S(2)}) collective-permute-start(bf16[160,640]{1,0:T(8,128)(2,1)} %bitcast.178), channel_id=1, source_target_pairs={{4,0},{8,4},{12,8},{16,12},{20,16},{24,20},{28,24},{5,1},{9,5},{13... | collective-permute-start | bytes 614408 | tf_op jit(solution)/shard_map/ppermute | solution.py:26
  16.7 1.2 %copy-start.1 = (f32[4,160,160]{2,0,1:T(4,128)S(1)}, f32[4,160,160]{2,0,1:T(4,128)}, u32[]{:S(2)}) copy-start(f32[4,160,160]{2,0,1:T(4,128)} %copy.22) | copy-start | bytes 1228804
  16.7 1.2 %copy-start.6 = (s32[160,160]{1,0:T(8,128)S(1)}, s32[160,160]{1,0:T(8,128)}, u32[]{:S(2)}) copy-start(s32[160,160]{1,0:T(8,128)} %iota_subtract_fusion) | copy-start | bytes 307204
  17.9 2.2 %copy-start.2 = (f32[4,160,160]{2,0,1:T(4,128)S(1)}, f32[4,160,160]{2,0,1:T(4,128)}, u32[]{:S(2)}) copy-start(f32[4,160,160]{2,0,1:T(4,128)} %copy.23) | copy-start | bytes 1228804
  20.1 2.2 %copy-start.5 = (bf16[4,1,160]{1,2,0:T(8,128)(2,1)S(1)}, bf16[4,1,160]{1,2,0:T(8,128)(2,1)}, u32[]{:S(2)}) copy-start(bf16[4,1,160]{1,2,0:T(8,128)(2,1)} %get-tuple-element.179) | copy-start | bytes 3844
  23.0 2.2 %copy-start.3 = (bf16[4,2,160]{1,2,0:T(8,128)(2,1)S(1)}, bf16[4,2,160]{1,2,0:T(8,128)(2,1)}, u32[]{:S(2)}) copy-start(bf16[4,2,160]{1,2,0:T(8,128)(2,1)} %get-tuple-element.175) | copy-start | bytes 7684
  25.8 2.2 %copy-start.4 = (bf16[4,3,160]{1,2,0:T(8,128)(2,1)S(1)}, bf16[4,3,160]{1,2,0:T(8,128)(2,1)}, u32[]{:S(2)}) copy-start(bf16[4,3,160]{1,2,0:T(8,128)(2,1)} %get-tuple-element.171) | copy-start | bytes 11524
  31.3 0.9 copy-start.7
  32.3 2.2 %copy-start = (f32[4,160,160]{2,1,0:T(8,128)S(1)}, f32[4,160,160]{2,1,0:T(8,128)}, u32[]{:S(2)}) copy-start(f32[4,160,160]{2,1,0:T(8,128)} %fusion.24) | copy-start | bytes 1228804
  38.1 2.1 %collective-permute-start.1 = (f32[3,1,8]{2,1,0:T(1,128)S(1)}, f32[3,1,8]{2,1,0:T(1,128)S(1)}, u32[]{:S(2)}, u32[]{:S(2)}) collective-permute-start(f32[3,1,8]{2,1,0:T(1,128)S(1)} %squeeze.12), channel_id=1, source_target_pairs={{0,1},{1,2},{2,3},{4,5},{5,6},{6,7},{8,9},{9,10},{10,11},{12,13},{... | collective-permute-start | bytes 296 | tf_op jit(solution)/shard_map/ppermute | solution.py:26
  71.6 2.6 %collective-permute-start.2 = (f32[2,1,1,8]{3,0,2,1:T(2,128)S(1)}, f32[2,1,1,8]{3,0,2,1:T(2,128)S(1)}, u32[]{:S(2)}, u32[]{:S(2)}) collective-permute-start(f32[2,1,1,8]{3,0,2,1:T(2,128)S(1)} %get-tuple-element.207), channel_id=1, source_target_pairs={{0,1},{1,2},{2,3},{4,5},{5,6},{6,7},{8,9},{9,10},{10,11},{12,13},{... | collective-permute-start | bytes 200 | tf_op jit(solution)/shard_map/ppermute | solution.py:49
  72.9 7.6 %collective-permute-start.3 = (f32[2,1,1,8]{3,0,2,1:T(2,128)S(1)}, f32[2,1,1,8]{3,0,2,1:T(2,128)S(1)}, u32[]{:S(2)}, u32[]{:S(2)}) collective-permute-start(f32[2,1,1,8]{3,0,2,1:T(2,128)S(1)} %get-tuple-element.208), channel_id=1, source_target_pairs={{1,0},{2,1},{3,2},{5,4},{6,5},{7,6},{9,8},{10,9},{11,10},{13,12},{... | collective-permute-start | bytes 200 | tf_op jit(solution)/shard_map/ppermute | solution.py:50
  80.8 5.6 %collective-permute-start.4 = (f32[2,1,1,8]{3,0,2,1:T(2,128)S(1)}, f32[2,1,1,8]{3,0,2,1:T(2,128)S(1)}, u32[]{:S(2)}, u32[]{:S(2)}) collective-permute-start(f32[2,1,1,8]{3,0,2,1:T(2,128)S(1)} %get-tuple-element.205), channel_id=1, source_target_pairs={{0,1},{1,2},{2,3},{4,5},{5,6},{6,7},{8,9},{9,10},{10,11},{12,13},{... | collective-permute-start | bytes 200 | tf_op jit(solution)/shard_map/ppermute | solution.py:49
  85.0 3.0 %collective-permute-start.5 = (f32[2,1,1,8]{3,0,2,1:T(2,128)S(1)}, f32[2,1,1,8]{3,0,2,1:T(2,128)S(1)}, u32[]{:S(2)}, u32[]{:S(2)}) collective-permute-start(f32[2,1,1,8]{3,0,2,1:T(2,128)S(1)} %get-tuple-element.206), channel_id=1, source_target_pairs={{1,0},{2,1},{3,2},{5,4},{6,5},{7,6},{9,8},{10,9},{11,10},{13,12},{... | collective-permute-start | bytes 200 | tf_op jit(solution)/shard_map/ppermute | solution.py:50
  88.4 5.1 %collective-permute-start.6 = (f32[2,1,1,8]{3,0,2,1:T(2,128)S(1)}, f32[2,1,1,8]{3,0,2,1:T(2,128)S(1)}, u32[]{:S(2)}, u32[]{:S(2)}) collective-permute-start(f32[2,1,1,8]{3,0,2,1:T(2,128)S(1)} %get-tuple-element.203), channel_id=1, source_target_pairs={{0,1},{1,2},{2,3},{4,5},{5,6},{6,7},{8,9},{9,10},{10,11},{12,13},{... | collective-permute-start | bytes 200 | tf_op jit(solution)/shard_map/ppermute | solution.py:49
  92.2 3.0 %collective-permute-start.7 = (f32[2,1,1,8]{3,0,2,1:T(2,128)S(1)}, f32[2,1,1,8]{3,0,2,1:T(2,128)S(1)}, u32[]{:S(2)}, u32[]{:S(2)}) collective-permute-start(f32[2,1,1,8]{3,0,2,1:T(2,128)S(1)} %get-tuple-element.204), channel_id=1, source_target_pairs={{1,0},{2,1},{3,2},{5,4},{6,5},{7,6},{9,8},{10,9},{11,10},{13,12},{... | collective-permute-start | bytes 200 | tf_op jit(solution)/shard_map/ppermute | solution.py:50
  95.6 5.1 %collective-permute-start.8 = (f32[2,1,1,8]{3,0,2,1:T(2,128)S(1)}, f32[2,1,1,8]{3,0,2,1:T(2,128)S(1)}, u32[]{:S(2)}, u32[]{:S(2)}) collective-permute-start(f32[2,1,1,8]{3,0,2,1:T(2,128)S(1)} %get-tuple-element.201), channel_id=1, source_target_pairs={{0,1},{1,2},{2,3},{4,5},{5,6},{6,7},{8,9},{9,10},{10,11},{12,13},{... | collective-permute-start | bytes 200 | tf_op jit(solution)/shard_map/ppermute | solution.py:49
  99.4 3.0 %collective-permute-start.9 = (f32[2,1,1,8]{3,0,2,1:T(2,128)S(1)}, f32[2,1,1,8]{3,0,2,1:T(2,128)S(1)}, u32[]{:S(2)}, u32[]{:S(2)}) collective-permute-start(f32[2,1,1,8]{3,0,2,1:T(2,128)S(1)} %get-tuple-element.202), channel_id=1, source_target_pairs={{1,0},{2,1},{3,2},{5,4},{6,5},{7,6},{9,8},{10,9},{11,10},{13,12},{... | collective-permute-start | bytes 200 | tf_op jit(solution)/shard_map/ppermute | solution.py:50
where the time goes:
time: 105 us; the launch traced here: 103 us
  blocking collectives  31 us (30%)
  starting transfers between devices  21.1 us (20%)
  matrix products  19.3 us (18%)
  waiting for transfers between devices  18.2 us (17%)
  local copies, waits for them, and re-layouts  9.5 us (9%)
  other arithmetic  3.01 us (3%)
  between operations  1.16 us (1%)
    all_gather x1, blocking collectives, carried_in(): everything = lax.all_gather(x, axis)  31 us
    dot_general x7, matrix products, correlate(): sums.append(jnp.einsum('nxz,dxz->nd', cross, diagonals, precision=highest))  15.5 us
    ppermute x4, starting transfers between devices, with_halo(): before = lax.ppermute(last, axis, up)  13.2 us
    ppermute x4, waiting for transfers between devices, with_halo(): after = lax.ppermute(initial, axis, down)  11.4 us
    ppermute x2, waiting for transfers between devices, shifted(): return lax.ppermute(block, axis, route)  6.73 us
    ppermute x4, starting transfers between devices, with_halo(): after = lax.ppermute(initial, axis, down)  5.17 us
    dot_general x6, local copies, waits for them, and re-layouts, correlate(): jnp.einsum('nyx,nyz->nxz', first, rolled, preferred_element_type=jnp.floa...  3.73 us
    dot_general x7, matrix products, correlate(): jnp.einsum('nyx,nyz->nxz', first, rolled, preferred_element_type=jnp.floa...  3.05 us
  transfers between devices with their start and end apart: 10, of which 6 were waited for; matrix products, arithmetic and copies ran while one was open for 3% of the time, Pallas kernels for 0%

commit v1 on v0

v1 whole, which is shorter than its diff:
```python
import functools
import math

import jax
import jax.numpy as jnp
from jax import lax
from jax.experimental import pallas as pl
from jax.experimental.pallas import tpu as pltpu
from jax.sharding import PartitionSpec as P

PATCH_SIZE = 160
BAND_ROWS = 4
NODE_COLS = 8
CELL_SUBDIV = 40
SPRING_STEPS = 4

LANES = 128
SUBLANES = 8
LAGS = 9
BAND = BAND_ROWS * NODE_COLS
SPLAT = BAND + NODE_COLS

rest_length = 40.0
flow_stiff = 0.5
time_step = 0.5
damping = 0.6

VMEM = pl.BlockSpec(memory_space=pltpu.VMEM)
SMEM = pl.BlockSpec(memory_space=pltpu.SMEM)


def iota(shape, dim):
    return lax.broadcasted_iota(jnp.int32, shape, dim)


def wrapped(index, size):
    index = jnp.where(index < 0, index + size, index)
    return jnp.where(index >= size, index - size, index)


def windows(cols, size):
    for j in range(cols):
        start = j * size
        base = start // LANES * LANES
        stop = -(-(start + size) // LANES) * LANES
        yield j, base, stop - base, start - base


def prepare(code_ref, block_ref, offset_ref, valid_ref, image_ref, moved_ref, aux_ref):
    size = PATCH_SIZE
    cols = code_ref.shape[2]
    filled = 0
    for j, base, width, begin in windows(cols, size):
        code = code_ref[0, 0, j]
        shift_y = code // 5 - 2
        shift_x = code % 5 - 2
        lane = iota((1, width), 1) - begin
        inside = (lane >= 0) & (lane < size)
        source = iota((width, width), 0)
        row = iota((size, 1), 0)
        column = iota((size, size), 1)
        pick_y = jnp.concatenate(
            [(column == wrapped(row - shift_y - a, size)).astype(jnp.bfloat16) for a in (-1, 0, 1)]
        )
        window = image_ref[0, :, base : base + width]
        for b in range(3):
            wanted = jnp.where(inside, wrapped(lane - shift_x - (b - 1), size) + begin, -1)
            pick_x = (source == wanted).astype(jnp.bfloat16)
            across = jnp.dot(window, pick_x, preferred_element_type=jnp.float32)
            both = jnp.dot(pick_y, across.astype(jnp.bfloat16), preferred_element_type=jnp.float32)
            for a in range(3):
                piece = both[a * size : (a + 1) * size]
                for tile in range(0, width, LANES):
                    part = piece[:, tile : tile + LANES]
                    where = (a * 3 + b, slice(None), slice(base + tile, base + tile + LANES))
                    if base + tile < filled:
                        part = part + moved_ref[where]
                    moved_ref[where] = part
        filled = base + width
    sub = iota((SUBLANES, LANES), 0)
    lane = iota((SUBLANES, LANES), 1)
    zero = jnp.zeros((SUBLANES, LANES), jnp.int32)
    rows = [zero] * 7
    for p in range(cols):
        code, block = code_ref[0, 0, p], block_ref[0, 0, p]
        offset = offset_ref[0, 0, p]
        held = (
            code // 5 - 2,
            code % 5 - 2,
            block // (NODE_COLS - 1),
            block % (NODE_COLS - 1),
            offset // CELL_SUBDIV,
            offset % CELL_SUBDIV,
            valid_ref[0, 0, p],
        )
        rows = [jnp.where(sub == p, value, before) for value, before in zip(held, rows)]
    shift_y, shift_x, cell_row, cell_col, part_y, part_x, valid = rows
    frac_y = part_y.astype(jnp.float32) / CELL_SUBDIV
    frac_x = part_x.astype(jnp.float32) / CELL_SUBDIV
    spot = jnp.where(lane >= 2 * SPLAT, lane - 2 * SPLAT, jnp.where(lane >= SPLAT, lane - SPLAT, lane))
    node_row = spot >> 3
    node_col = spot & (NODE_COLS - 1)
    weight_y = jnp.where(cell_row == node_row, 1.0 - frac_y, 0.0) + jnp.where(
        cell_row + 1 == node_row, frac_y, 0.0
    )
    weight_x = jnp.where(cell_col == node_col, 1.0 - frac_x, 0.0) + jnp.where(
        cell_col + 1 == node_col, frac_x, 0.0
    )
    weight = weight_y * weight_x * valid.astype(jnp.float32)
    aux_ref[0] = jnp.where(lane < 3 * SPLAT, weight, 0.0)
    aux_ref[1] = shift_y.astype(jnp.float32)
    aux_ref[2] = shift_x.astype(jnp.float32)


def correlate(moved_ref, aux_ref, second_ref, flow_ref, splat_ref):
    size = PATCH_SIZE
    cols = flow_ref.shape[3]
    sub = iota((SUBLANES, LANES), 0)
    lane = iota((SUBLANES, LANES), 1)
    total = [jnp.zeros((SUBLANES, LANES), jnp.float32) for _ in range(LAGS)]
    for base in range(0, cols * size, LANES):
        sums = [None] * LAGS
        for top in range(0, size, 16):
            later = second_ref[0, top : top + 16, base : base + LANES].astype(jnp.float32)
            for k in range(LAGS):
                part = moved_ref[k, top : top + 16, base : base + LANES] * later
                part = part[:SUBLANES] + part[SUBLANES:]
                sums[k] = part if sums[k] is None else sums[k] + part
        own = (lane + base >= sub * size) & (lane + base < (sub + 1) * size)
        for k in range(LAGS):
            part = sums[k]
            for step in (4, 2, 1):
                part = part + pltpu.roll(part, step, 0)
            total[k] = total[k] + jnp.where(own, part, 0.0)
    corr = [jnp.sum(t, axis=1, keepdims=True) / float(size) for t in total]
    energy = 1.0
    for value in corr:
        energy = energy + value * value
    num_y = (corr[6] - corr[0]) + (corr[7] - corr[1]) + (corr[8] - corr[2])
    num_x = (corr[2] - corr[0]) + (corr[5] - corr[3]) + (corr[8] - corr[6])
    flow_y = aux_ref[1] + num_y / energy
    flow_x = aux_ref[2] + num_x / energy
    value = jnp.where(lane < SPLAT, flow_y, jnp.where(lane < 2 * SPLAT, flow_x, 1.0))
    row = jnp.sum(aux_ref[0] * value, axis=0, keepdims=True)
    splat_ref[...] = jnp.broadcast_to(row, splat_ref.shape)
    for q, flow in enumerate((flow_y, flow_x)):
        flow_ref[q, 0] = jnp.sum(jnp.where(lane == sub, flow, 0.0), axis=0, keepdims=True)[:, :cols]


def relax(strips, splat_ref, out_ref):
    sections = splat_ref.shape[0] // strips
    section, strip = lax.axis_index("gz"), lax.axis_index("xy")
    length = strips * BAND
    tiles = -(-length // LANES)
    lane = iota((sections, LANES), 1)
    grid = [[jnp.zeros((sections, LANES), jnp.float32)] * tiles for _ in range(3)]
    for r in range(strips):
        rows = splat_ref[pl.ds(r, sections, stride=strips), :]
        tile, start = divmod(r * BAND, LANES)
        for q in range(3):
            moved = pltpu.roll(rows, (start - q * SPLAT) % LANES, 1)
            here = (lane >= start) & (lane < start + SPLAT)
            grid[q][tile] = grid[q][tile] + jnp.where(here, moved, 0.0)
            if start + SPLAT > LANES and tile + 1 < tiles:
                spill = lane < start + SPLAT - LANES
                grid[q][tile + 1] = grid[q][tile + 1] + jnp.where(spill, moved, 0.0)
    below = iota((sections, LANES), 0) < section
    fixed = []
    for q in range(2):
        parts = []
        for tile in range(tiles):
            target = jnp.where(below, grid[q][tile] / (1.0 + grid[2][tile]), 0.0)
            part = jnp.sum(target, axis=0, keepdims=True)
            parts.append(jnp.broadcast_to(part, (SUBLANES, LANES)))
        fixed.append(parts[0] if tiles == 1 else jnp.concatenate(parts, axis=1))
    width = tiles * LANES
    node = iota((SUBLANES, width), 1)
    col = node & (NODE_COLS - 1)
    one, none = 1.0, 0.0
    springs = (
        (NODE_COLS, jnp.where(node >= NODE_COLS, one, none), -rest_length, 0.0),
        (width - NODE_COLS, jnp.where(node < length - NODE_COLS, one, none), rest_length, 0.0),
        (1, jnp.where(col > 0, one, none), 0.0, -rest_length),
        (width - 1, jnp.where(col < NODE_COLS - 1, one, none), 0.0, rest_length),
    )
    rest_zero = math.sqrt(rest_length * rest_length + 1.0)
    now_y, now_x = fixed
    speed_y = speed_x = jnp.zeros((SUBLANES, width), jnp.float32)
    for _ in range(SPRING_STEPS):
        push_y = flow_stiff * (fixed[0] - now_y)
        push_x = flow_stiff * (fixed[1] - now_x)
        for turn, present, rest_y, rest_x in springs:
            gap_y = rest_y + pltpu.roll(now_y, turn, 1) - now_y
            gap_x = rest_x + pltpu.roll(now_x, turn, 1) - now_x
            inverse = lax.rsqrt(gap_y * gap_y + gap_x * gap_x + 1.0)
            tension = (1.0 - rest_zero * inverse) * present
            push_y = push_y + tension * gap_y
            push_x = push_x + tension * gap_x
        speed_y = damping * speed_y + time_step * push_y
        speed_x = damping * speed_x + time_step * push_x
        now_y = now_y + time_step * speed_y
        now_x = now_x + time_step * speed_x
    for q, now in enumerate((now_y, now_x)):
        for i in range(BAND_ROWS):
            turn = lax.rem(2 * width - strip * BAND - i * NODE_COLS, width)
            out_ref[q, 0, i : i + 1, :] = pltpu.roll(now, turn, 1)[:1, :NODE_COLS]


def on_device(images, peak_code, cell_block, cell_offset, valid_patch):
    _, size, breadth = images.shape
    cols = breadth // PATCH_SIZE
    sections, strips = lax.axis_size("gz"), lax.axis_size("xy")
    devices = sections * strips
    following = lax.ppermute(images, "gz", [(i + 1, i) for i in range(sections - 1)])
    moved, aux = pl.pallas_call(
        prepare,
        out_shape=(
            pltpu.VMEM((LAGS, size, breadth), jnp.float32),
            pltpu.VMEM((3, SUBLANES, LANES), jnp.float32),
        ),
        in_specs=[SMEM] * 4 + [VMEM],
        out_specs=[VMEM, VMEM],
        compiler_params=pltpu.CompilerParams(vmem_limit_bytes=24 << 20),
        cost_estimate=pl.CostEstimate(flops=2_000_000_000, bytes_accessed=4_000_000, transcendentals=0),
        name="prepare",
    )(peak_code, cell_block, cell_offset, valid_patch, images)
    flow, splat = pl.pallas_call(
        correlate,
        out_shape=(
            jax.ShapeDtypeStruct((2, 1, 1, cols), jnp.float32),
            jax.ShapeDtypeStruct((devices, LANES), jnp.float32),
        ),
        in_specs=[VMEM, VMEM, VMEM],
        out_specs=[VMEM, VMEM],
        compiler_params=pltpu.CompilerParams(vmem_limit_bytes=24 << 20),
        name="correlate",
    )(moved, aux, following)
    gathered = lax.all_to_all(splat, ("gz", "xy"), 0, 0, tiled=True)
    node_shift = pl.pallas_call(
        functools.partial(relax, strips),
        out_shape=jax.ShapeDtypeStruct((2, 1, BAND_ROWS, NODE_COLS), jnp.float32),
        in_specs=[VMEM],
        out_specs=VMEM,
        compiler_params=pltpu.CompilerParams(vmem_limit_bytes=24 << 20),
        name="relax",
    )(gathered)
    return (flow, node_shift)


def solution(mesh):
    return jax.shard_map(
        on_device,
        mesh=mesh,
        in_specs=(P("gz", "xy", None),) * 5,
        out_specs=(P(None, "gz", "xy", None), P(None, "gz", "xy", None)),
        check_vma=False,
    )
```

time: 105 us -> 26.1 us (0.25); the launches traced: 103 us -> 25.9 us
  starting transfers between devices: 21.1 us -> 1.29 us
  matrix products: 19.3 us -> 0 us
  blocking collectives: 31 us -> 12.9 us
  waiting for transfers between devices: 18.2 us -> 2.69 us
  local copies, waits for them, and re-layouts: 9.5 us -> 3.54 us
  Pallas kernels: 0 us -> 4.8 us
  other arithmetic: 3.01 us -> 0 us
    all_gather x1 -> x0, blocking collectives: 31 us -> none  [carried_in(): everything = lax.all_gather(x, axis)]
    ppermute x10 -> x1, starting transfers between devices: 21.1 us -> 1.29 us  [on_device(): lax.ppermute(images, 'gz', [(i + 1, i) for i in range(sections - 1)])]
    dot_general x17 -> x0, matrix products: 19.3 us -> none  [the longest x7 15.5 us: correlate(): sums.append(jnp.einsum('nxz,dxz->nd', cross, diagonals, precision=highest))]
    ppermute x10 -> x1, waiting for transfers between devices: 18.2 us -> 2.69 us  [on_device(): lax.ppermute(images, 'gz', [(i + 1, i) for i in range(sections - 1)])]
    all_to_all x0 -> x1, blocking collectives: none -> 12.9 us  [on_device(): gathered = lax.all_to_all(splat, ('gz', 'xy'), 0, 0, tiled=True)]
    pallas_call x0 -> x3, Pallas kernels: none -> 4.8 us  [the longest x1 2.58 us: on_device(): pl.pallas_call(prepare, out_shape=(pltpu.VMEM((LAGS, size, breadth), jnp....]
    dot_general x7 -> x0, local copies, waits for them, and re-layouts: 3.84 us -> none  [the longest x6 3.73 us: correlate(): jnp.einsum('nyx,nyz->nxz', first, rolled, preferred_element_type=jnp.floa...]
    slice x17 -> x0, local copies, waits for them, and re-layouts: 3.05 us -> none  [the longest x6 2.66 us: correlate(): rolled = jnp.roll(second, -lag_row, axis=1)]
  transfers between devices with their start and end apart: 10 -> 1, of which waited for: 6 -> 1; matrix products, arithmetic and copies ran while one was open for 3% -> 0% of each run, Pallas kernels for 0% -> 10%
where the time goes in v1:
time: 26.1 us; the launch traced here: 25.9 us
  blocking collectives  12.9 us (49%)
  Pallas kernels  4.8 us (18%)
  local copies, waits for them, and re-layouts  3.54 us (14%)
  waiting for transfers between devices  2.69 us (10%)
  starting transfers between devices  1.29 us (5%)
  between operations  0.66 us (3%)
    all_to_all x1, blocking collectives, on_device(): gathered = lax.all_to_all(splat, ('gz', 'xy'), 0, 0, tiled=True)  12.9 us
    unnamed x10, local copies, waits for them, and re-layouts  3.54 us
    ppermute x1, waiting for transfers between devices, on_device(): lax.ppermute(images, 'gz', [(i + 1, i) for i in range(sections - 1)])  2.69 us
    pallas_call x1, Pallas kernels, on_device(): pl.pallas_call(prepare, out_shape=(pltpu.VMEM((LAGS, size, breadth), jnp....  2.58 us
    ppermute x1, starting transfers between devices, on_device(): lax.ppermute(images, 'gz', [(i + 1, i) for i in range(sections - 1)])  1.29 us
    pallas_call x1, Pallas kernels, on_device(): pl.pallas_call(functools.partial(relax, strips), out_shape=jax.ShapeDtype...  1.13 us
    pallas_call x1, Pallas kernels, on_device(): pl.pallas_call(correlate, out_shape=(jax.ShapeDtypeStruct((2, 1, 1, cols)...  1.09 us
  transfers between devices with their start and end apart: 1, of which 1 were waited for; matrix products, arithmetic and copies ran while one was open for 0% of the time, Pallas kernels for 10%

profile of v1, /device:TPU:0, one launch (start us, length us, event | category | flops | bytes accessed | tf_op | source)
XLA Modules:
  0.0 25.9 jit_solution(14005768585435340073)
XLA Ops:
  0.6 1.3 %collective-permute-start = (bf16[1,160,640]{2,1,0:T(8,128)(2,1)}, bf16[1,160,640]{2,1,0:T(8,128)(2,1)S(1)}, u32[]{:S(2)}, u32[]{:S(2)}) collective-permute-start(bf16[1,160,640]{2,1,0:T(8,128)(2,1)} %image_ref.1), channel_id=1, source_target_pairs={{4,0},{8,4},{12,8},{16,12},{20,16},{24,20},{28,24},{5,1},{9,5},{13... | collective-permute-start | bytes 614408 | tf_op jit(solution)/shard_map/ppermute | solution.py:214
  1.9 0.0 copy-start
  1.9 0.9 %copy-done = bf16[1,160,640]{2,1,0:T(8,128)(2,1)S(1)} copy-done((bf16[1,160,640]{2,1,0:T(8,128)(2,1)S(1)}, bf16[1,160,640]{2,1,0:T(8,128)(2,1)}, u32[]{:S(2)}) %copy-start) | copy-done | bytes 204824
  2.9 0.0 copy-start.1
  2.9 0.7 %copy-done.1 = s32[1,1,4]{2,1,0:T(1,128)S(1)} copy-done((s32[1,1,4]{2,1,0:T(1,128)S(1)}, s32[1,1,4]{2,1,0:T(1,128)}, u32[]{:S(2)}) %copy-start.1) | copy-done | bytes 40
  3.5 0.0 copy-start.2
  3.5 0.7 %copy-done.2 = s32[1,1,4]{2,1,0:T(1,128)S(1)} copy-done((s32[1,1,4]{2,1,0:T(1,128)S(1)}, s32[1,1,4]{2,1,0:T(1,128)}, u32[]{:S(2)}) %copy-start.2) | copy-done | bytes 40
  4.2 0.0 copy-start.3
  4.2 0.7 %copy-done.3 = s32[1,1,4]{2,1,0:T(1,128)S(1)} copy-done((s32[1,1,4]{2,1,0:T(1,128)S(1)}, s32[1,1,4]{2,1,0:T(1,128)}, u32[]{:S(2)}) %copy-start.3) | copy-done | bytes 40
  4.8 0.0 copy-start.4
  4.8 0.7 %copy-done.4 = s32[1,1,4]{2,1,0:T(1,128)S(1)} copy-done((s32[1,1,4]{2,1,0:T(1,128)S(1)}, s32[1,1,4]{2,1,0:T(1,128)}, u32[]{:S(2)}) %copy-start.4) | copy-done | bytes 40
  5.5 2.6 %prepare.1 = (f32[9,160,640]{2,1,0:T(8,128)S(1)}, f32[3,8,128]{2,1,0:T(8,128)S(1)}) custom-call(s32[1,1,4]{2,1,0:T(1,128)S(1)} %copy-done.1, s32[1,1,4]{2,1,0:T(1,128)S(1)} %copy-done.2, s32[1,1,4]{2,1,0:T(1,128)S(1)} %copy-done.3, s32[1,1,4]{2,1,0:T(1,128)S(1)} %copy-done.4, bf16[1,160,640]{2,1,0:T(8,128)(2,1)S(1)} %copy-done), custom_call_target="tpu_custom_call" | custom-call | flops 2000000000 | bytes 4000000 | tf_op jit(solution)/shard_map/prepare/pallas_call | solution.py:215
  8.1 2.7 %collective-permute-done.second_ref = bf16[1,160,640]{2,1,0:T(8,128)(2,1)S(1)} collective-permute-done((bf16[1,160,640]{2,1,0:T(8,128)(2,1)}, bf16[1,160,640]{2,1,0:T(8,128)(2,1)S(1)}, u32[]{:S(2)}, u32[]{:S(2)}) %collective-permute-start) | collective-permute-done | bytes 204832 | tf_op jit(solution)/shard_map/ppermute | solution.py:214
  10.8 1.1 %correlate.1 = (f32[2,1,1,4]{3,2,1,0:T(1,128)}, f32[32,128]{1,0:T(8,128)S(1)}) custom-call(f32[9,160,640]{2,1,0:T(8,128)S(1)} %get-tuple-element.6.moved_ref, f32[3,8,128]{2,1,0:T(8,128)S(1)} %get-tuple-element.7.aux_ref, bf16[1,160,640]{2,1,0:T(8,128)(2,1)S(1)} %collective-permute-done.second_ref), custom_call_target="tpu_custom_call" | custom-call | tf_op jit(solution)/shard_map/correlate/pallas_call | solution.py:227
  11.8 12.9 %all_to_all.11 = f32[32,1,128]{2,1,0:T(1,128)S(1)} all-to-all(f32[32,1,128]{2,1,0:T(1,128)S(1)} %bitcast.5), channel_id=1, replica_groups=mesh['gz'=8,'xy'=4] {'gz','xy'}, dimensions={0} | all-to-all | bytes 32768 | tf_op jit(solution)/shard_map/all_to_all | solution.py:238
  24.8 1.1 %relax.1 = f32[2,1,4,8]{3,2,1,0:T(4,128)} custom-call(f32[32,128]{1,0:T(8,128)S(1)} %bitcast.4), custom_call_target="tpu_custom_call" | custom-call | tf_op jit(solution)/shard_map/relax/pallas_call | solution.py:239
Async XLA Ops:
  0.6 10.1 %collective-permute-start = (bf16[1,160,640]{2,1,0:T(8,128)(2,1)}, bf16[1,160,640]{2,1,0:T(8,128)(2,1)S(1)}, u32[]{:S(2)}, u32[]{:S(2)}) collective-permute-start(bf16[1,160,640]{2,1,0:T(8,128)(2,1)} %image_ref.1), channel_id=1, source_target_pairs={{4,0},{8,4},{12,8},{16,12},{20,16},{24,20},{28,24},{5,1},{9,5},{13... | collective-permute-start | bytes 614408 | tf_op jit(solution)/shard_map/ppermute | solution.py:214
  1.9 0.9 %copy-start = (bf16[1,160,640]{2,1,0:T(8,128)(2,1)S(1)}, bf16[1,160,640]{2,1,0:T(8,128)(2,1)}, u32[]{:S(2)}) copy-start(bf16[1,160,640]{2,1,0:T(8,128)(2,1)} %image_ref.1) | copy-start | bytes 614404
  2.9 0.7 %copy-start.1 = (s32[1,1,4]{2,1,0:T(1,128)S(1)}, s32[1,1,4]{2,1,0:T(1,128)}, u32[]{:S(2)}) copy-start(s32[1,1,4]{2,1,0:T(1,128)} %code_ref.1) | copy-start | bytes 52
  3.5 0.7 %copy-start.2 = (s32[1,1,4]{2,1,0:T(1,128)S(1)}, s32[1,1,4]{2,1,0:T(1,128)}, u32[]{:S(2)}) copy-start(s32[1,1,4]{2,1,0:T(1,128)} %block_ref.1) | copy-start | bytes 52
  4.2 0.7 %copy-start.3 = (s32[1,1,4]{2,1,0:T(1,128)S(1)}, s32[1,1,4]{2,1,0:T(1,128)}, u32[]{:S(2)}) copy-start(s32[1,1,4]{2,1,0:T(1,128)} %offset_ref.1) | copy-start | bytes 52
  4.8 0.7 %copy-start.4 = (s32[1,1,4]{2,1,0:T(1,128)S(1)}, s32[1,1,4]{2,1,0:T(1,128)}, u32[]{:S(2)}) copy-start(s32[1,1,4]{2,1,0:T(1,128)} %valid_ref.1) | copy-start | bytes 52

commit v2 on v1

--- a/solution.py
+++ b/solution.py
@@ -27,6 +27,7 @@
 
 VMEM = pl.BlockSpec(memory_space=pltpu.VMEM)
 SMEM = pl.BlockSpec(memory_space=pltpu.SMEM)
+HBM = pl.BlockSpec(memory_space=pltpu.HBM)
 
 
 def iota(shape, dim):
@@ -46,12 +47,12 @@
         yield j, base, stop - base, start - base
 
 
-def prepare(code_ref, block_ref, offset_ref, valid_ref, image_ref, moved_ref, aux_ref):
+def prepare(codes_ref, image_ref, moved_ref, aux_ref):
     size = PATCH_SIZE
-    cols = code_ref.shape[2]
+    cols = codes_ref.shape[2]
     filled = 0
     for j, base, width, begin in windows(cols, size):
-        code = code_ref[0, 0, j]
+        code = codes_ref[0, 0, j]
         shift_y = code // 5 - 2
         shift_x = code % 5 - 2
         lane = iota((1, width), 1) - begin
@@ -82,8 +83,7 @@
     zero = jnp.zeros((SUBLANES, LANES), jnp.int32)
     rows = [zero] * 7
     for p in range(cols):
-        code, block = code_ref[0, 0, p], block_ref[0, 0, p]
-        offset = offset_ref[0, 0, p]
+        code, block, offset, valid = (codes_ref[0, q, p] for q in range(4))
         held = (
             code // 5 - 2,
             code % 5 - 2,
@@ -91,7 +91,7 @@
             block % (NODE_COLS - 1),
             offset // CELL_SUBDIV,
             offset % CELL_SUBDIV,
-            valid_ref[0, 0, p],
+            valid,
         )
         rows = [jnp.where(sub == p, value, before) for value, before in zip(held, rows)]
     shift_y, shift_x, cell_row, cell_col, part_y, part_x, valid = rows
@@ -147,7 +147,9 @@
         flow_ref[q, 0] = jnp.sum(jnp.where(lane == sub, flow, 0.0), axis=0, keepdims=True)[:, :cols]
 
 
-def relax(strips, splat_ref, out_ref):
+def relax(strips, splat_ref, held_ref, flow_ref, out_ref, sem):
+    keep = pltpu.make_async_copy(held_ref, flow_ref, sem)
+    keep.start()
     sections = splat_ref.shape[0] // strips
     section, strip = lax.axis_index("gz"), lax.axis_index("xy")
     length = strips * BAND
@@ -204,6 +206,7 @@
         for i in range(BAND_ROWS):
             turn = lax.rem(2 * width - strip * BAND - i * NODE_COLS, width)
             out_ref[q, 0, i : i + 1, :] = pltpu.roll(now, turn, 1)[:1, :NODE_COLS]
+    keep.wait()
 
 
 def on_device(images, peak_code, cell_block, cell_offset, valid_patch):
@@ -212,23 +215,24 @@
     sections, strips = lax.axis_size("gz"), lax.axis_size("xy")
     devices = sections * strips
     following = lax.ppermute(images, "gz", [(i + 1, i) for i in range(sections - 1)])
+    codes = jnp.concatenate([peak_code, cell_block, cell_offset, valid_patch], axis=1)
     moved, aux = pl.pallas_call(
         prepare,
         out_shape=(
             pltpu.VMEM((LAGS, size, breadth), jnp.float32),
             pltpu.VMEM((3, SUBLANES, LANES), jnp.float32),
         ),
-        in_specs=[SMEM] * 4 + [VMEM],
+        in_specs=[SMEM, VMEM],
         out_specs=[VMEM, VMEM],
         compiler_params=pltpu.CompilerParams(vmem_limit_bytes=24 << 20),
         cost_estimate=pl.CostEstimate(flops=2_000_000_000, bytes_accessed=4_000_000, transcendentals=0),
         name="prepare",
-    )(peak_code, cell_block, cell_offset, valid_patch, images)
-    flow, splat = pl.pallas_call(
+    )(codes, images)
+    held, splat = pl.pallas_call(
         correlate,
         out_shape=(
-            jax.ShapeDtypeStruct((2, 1, 1, cols), jnp.float32),
-            jax.ShapeDtypeStruct((devices, LANES), jnp.float32),
+            pltpu.VMEM((2, 1, 1, cols), jnp.float32),
+            pltpu.VMEM((devices, LANES), jnp.float32),
         ),
         in_specs=[VMEM, VMEM, VMEM],
         out_specs=[VMEM, VMEM],
@@ -236,14 +240,18 @@
         name="correlate",
     )(moved, aux, following)
     gathered = lax.all_to_all(splat, ("gz", "xy"), 0, 0, tiled=True)
-    node_shift = pl.pallas_call(
+    flow, node_shift = pl.pallas_call(
         functools.partial(relax, strips),
-        out_shape=jax.ShapeDtypeStruct((2, 1, BAND_ROWS, NODE_COLS), jnp.float32),
-        in_specs=[VMEM],
-        out_specs=VMEM,
+        out_shape=(
+            jax.ShapeDtypeStruct(held.shape, jnp.float32),
+            jax.ShapeDtypeStruct((2, 1, BAND_ROWS, NODE_COLS), jnp.float32),
+        ),
+        in_specs=[VMEM, VMEM],
+        out_specs=[HBM, VMEM],
+        scratch_shapes=[pltpu.SemaphoreType.DMA],
         compiler_params=pltpu.CompilerParams(vmem_limit_bytes=24 << 20),
         name="relax",
-    )(gathered)
+    )(gathered, held)
     return (flow, node_shift)
 
 

time: 26.1 us -> 25.6 us (0.981)
  local copies, waits for them, and re-layouts: 3.54 us -> 0.93 us
  waiting for transfers between devices: 2.69 us -> 4.59 us
  other arithmetic: 0 us -> 0.72 us
  Pallas kernels: 4.8 us -> 4.31 us
    unnamed x10 -> x2, local copies, waits for them, and re-layouts: 3.54 us -> 0.93 us
    ppermute x1, waiting for transfers between devices: 2.69 us -> 4.59 us  [on_device(): lax.ppermute(images, 'gz', [(i + 1, i) for i in range(sections - 1)])]
    concatenate x0 -> x1, other arithmetic: none -> 0.72 us  [on_device(): jnp.concatenate([peak_code, cell_block, cell_offset, valid_patch], axis=1)]
    pallas_call x2, Pallas kernels: 2.22 us -> 1.72 us  [the longest x1 1.17 us: on_device(): pl.pallas_call(functools.partial(relax, strips), out_shape=(jax.ShapeDtyp...]
  transfers between devices with their start and end apart: 1 -> 1, of which waited for: 1 -> 1; matrix products, arithmetic and copies ran while one was open for 0% -> 3% of each run, Pallas kernels for 10% -> 10%
where the time goes in v2:
time: 25.6 us; the launch traced here: 25.4 us
  blocking collectives  12.9 us (50%)
  waiting for transfers between devices  4.59 us (18%)
  Pallas kernels  4.31 us (17%)
  starting transfers between devices  1.29 us (5%)
  local copies, waits for them, and re-layouts  0.93 us (4%)
  other arithmetic  0.72 us (3%)
  between operations  0.66 us (3%)
    all_to_all x1, blocking collectives, on_device(): gathered = lax.all_to_all(splat, ('gz', 'xy'), 0, 0, tiled=True)  12.9 us
    ppermute x1, waiting for transfers between devices, on_device(): lax.ppermute(images, 'gz', [(i + 1, i) for i in range(sections - 1)])  4.59 us
    pallas_call x1, Pallas kernels, on_device(): pl.pallas_call(prepare, out_shape=(pltpu.VMEM((LAGS, size, breadth), jnp....  2.59 us
    ppermute x1, starting transfers between devices, on_device(): lax.ppermute(images, 'gz', [(i + 1, i) for i in range(sections - 1)])  1.29 us
    pallas_call x1, Pallas kernels, on_device(): pl.pallas_call(functools.partial(relax, strips), out_shape=(jax.ShapeDtyp...  1.17 us
    unnamed x2, local copies, waits for them, and re-layouts  0.93 us
    concatenate x1, other arithmetic, on_device(): jnp.concatenate([peak_code, cell_block, cell_offset, valid_patch], axis=1)  0.72 us
    pallas_call x1, Pallas kernels, on_device(): pl.pallas_call(correlate, out_shape=(pltpu.VMEM((2, 1, 1, cols), jnp.floa...  0.55 us
  transfers between devices with their start and end apart: 1, of which 1 were waited for; matrix products, arithmetic and copies ran while one was open for 3% of the time, Pallas kernels for 10%

profile of v2, /device:TPU:0, one launch (start us, length us, event | category | flops | bytes accessed | tf_op | source)
XLA Modules:
  0.0 25.4 jit_solution(9315062168746090412)
XLA Ops:
  0.6 1.3 %collective-permute-start = (bf16[1,160,640]{2,1,0:T(8,128)(2,1)}, bf16[1,160,640]{2,1,0:T(8,128)(2,1)S(1)}, u32[]{:S(2)}, u32[]{:S(2)}) collective-permute-start(bf16[1,160,640]{2,1,0:T(8,128)(2,1)} %image_ref.1), channel_id=1, source_target_pairs={{4,0},{8,4},{12,8},{16,12},{20,16},{24,20},{28,24},{5,1},{9,5},{13... | collective-permute-start | bytes 614408 | tf_op jit(solution)/shard_map/ppermute | solution.py:217
  1.9 0.7 %pad_add_fusion.codes_ref = s32[1,4,4]{2,1,0:T(4,128)S(1)} fusion(s32[1,1,4]{2,1,0:T(1,128)} %param.9, s32[1,1,4]{2,1,0:T(1,128)} %param.8, s32[1,1,4]{2,1,0:T(1,128)} %param.7, s32[1,1,4]{2,1,0:T(1,128)} %param.6), kind=kLoop, calls=%fused_computation | loop fusion | flops 48 | bytes 128 | tf_op jit(solution)/shard_map/concatenate | solution.py:218
  2.6 0.0 copy-start
  2.7 0.9 %copy-done = bf16[1,160,640]{2,1,0:T(8,128)(2,1)S(1)} copy-done((bf16[1,160,640]{2,1,0:T(8,128)(2,1)S(1)}, bf16[1,160,640]{2,1,0:T(8,128)(2,1)}, u32[]{:S(2)}) %copy-start) | copy-done | bytes 204824
  3.6 2.6 %prepare.1 = (f32[9,160,640]{2,1,0:T(8,128)S(1)}, f32[3,8,128]{2,1,0:T(8,128)S(1)}) custom-call(s32[1,4,4]{2,1,0:T(4,128)S(1)} %pad_add_fusion.codes_ref, bf16[1,160,640]{2,1,0:T(8,128)(2,1)S(1)} %copy-done), custom_call_target="tpu_custom_call" | custom-call | flops 2000000000 | bytes 4000000 | tf_op jit(solution)/shard_map/prepare/pallas_call | solution.py:219
  6.2 4.6 %collective-permute-done.second_ref = bf16[1,160,640]{2,1,0:T(8,128)(2,1)S(1)} collective-permute-done((bf16[1,160,640]{2,1,0:T(8,128)(2,1)}, bf16[1,160,640]{2,1,0:T(8,128)(2,1)S(1)}, u32[]{:S(2)}, u32[]{:S(2)}) %collective-permute-start) | collective-permute-done | bytes 204832 | tf_op jit(solution)/shard_map/ppermute | solution.py:217
  10.8 0.5 %correlate.1 = (f32[2,1,1,4]{3,2,1,0:T(1,128)S(1)}, f32[32,128]{1,0:T(8,128)S(1)}) custom-call(f32[9,160,640]{2,1,0:T(8,128)S(1)} %get-tuple-element.6.moved_ref, f32[3,8,128]{2,1,0:T(8,128)S(1)} %get-tuple-element.7.aux_ref, bf16[1,160,640]{2,1,0:T(8,128)(2,1)S(1)} %collective-permute-done.second_ref), custom_call_target="tpu_custom_call" | custom-call | tf_op jit(solution)/shard_map/correlate/pallas_call | solution.py:231
  11.3 12.9 %all_to_all.11 = f32[32,1,128]{2,1,0:T(1,128)S(1)} all-to-all(f32[32,1,128]{2,1,0:T(1,128)S(1)} %bitcast.5), channel_id=1, replica_groups=mesh['gz'=8,'xy'=4] {'gz','xy'}, dimensions={0} | all-to-all | bytes 32768 | tf_op jit(solution)/shard_map/all_to_all | solution.py:242
  24.3 1.2 %relax.1 = (f32[2,1,1,4]{3,2,1,0:T(1,128)}, f32[2,1,4,8]{3,2,1,0:T(4,128)}) custom-call(f32[32,128]{1,0:T(8,128)S(1)} %bitcast.4, f32[2,1,1,4]{3,2,1,0:T(1,128)S(1)} %get-tuple-element.9.held_ref), custom_call_target="tpu_custom_call" | custom-call | tf_op jit(solution)/shard_map/relax/pallas_call | solution.py:243
Async XLA Ops:
  0.6 10.1 %collective-permute-start = (bf16[1,160,640]{2,1,0:T(8,128)(2,1)}, bf16[1,160,640]{2,1,0:T(8,128)(2,1)S(1)}, u32[]{:S(2)}, u32[]{:S(2)}) collective-permute-start(bf16[1,160,640]{2,1,0:T(8,128)(2,1)} %image_ref.1), channel_id=1, source_target_pairs={{4,0},{8,4},{12,8},{16,12},{20,16},{24,20},{28,24},{5,1},{9,5},{13... | collective-permute-start | bytes 614408 | tf_op jit(solution)/shard_map/ppermute | solution.py:217
  2.6 0.9 %copy-start = (bf16[1,160,640]{2,1,0:T(8,128)(2,1)S(1)}, bf16[1,160,640]{2,1,0:T(8,128)(2,1)}, u32[]{:S(2)}) copy-start(bf16[1,160,640]{2,1,0:T(8,128)(2,1)} %image_ref.1) | copy-start | bytes 614404

commit v3 on v2

--- a/solution.py
+++ b/solution.py
@@ -17,6 +17,7 @@
 LANES = 128
 SUBLANES = 8
 LAGS = 9
+PEAK = 2
 BAND = BAND_ROWS * NODE_COLS
 SPLAT = BAND + NODE_COLS
 
@@ -27,7 +28,6 @@
 
 VMEM = pl.BlockSpec(memory_space=pltpu.VMEM)
 SMEM = pl.BlockSpec(memory_space=pltpu.SMEM)
-HBM = pl.BlockSpec(memory_space=pltpu.HBM)
 
 
 def iota(shape, dim):
@@ -47,37 +47,27 @@
         yield j, base, stop - base, start - base
 
 
-def prepare(codes_ref, image_ref, moved_ref, aux_ref):
+def bank(rows_ref, across_ref):
     size = PATCH_SIZE
-    cols = codes_ref.shape[2]
-    filled = 0
-    for j, base, width, begin in windows(cols, size):
-        code = codes_ref[0, 0, j]
-        shift_y = code // 5 - 2
-        shift_x = code % 5 - 2
+    for k in range(rows_ref.shape[0]):
+        row = iota((size, 1), 0)
+        move = iota((size, size), 1) == wrapped(row - (k - PEAK), size)
+        rows_ref[k] = move.astype(jnp.bfloat16)
+    reach = 2 * PEAK + 3
+    width = across_ref.shape[2]
+    source = iota((width, width), 0).astype(jnp.float32).astype(jnp.bfloat16)
+    one, none = jnp.ones((), jnp.bfloat16), jnp.zeros((), jnp.bfloat16)
+    for j, _, _, begin in windows(across_ref.shape[0] // reach, size):
         lane = iota((1, width), 1) - begin
         inside = (lane >= 0) & (lane < size)
-        source = iota((width, width), 0)
-        row = iota((size, 1), 0)
-        column = iota((size, size), 1)
-        pick_y = jnp.concatenate(
-            [(column == wrapped(row - shift_y - a, size)).astype(jnp.bfloat16) for a in (-1, 0, 1)]
-        )
-        window = image_ref[0, :, base : base + width]
-        for b in range(3):
-            wanted = jnp.where(inside, wrapped(lane - shift_x - (b - 1), size) + begin, -1)
-            pick_x = (source == wanted).astype(jnp.bfloat16)
-            across = jnp.dot(window, pick_x, preferred_element_type=jnp.float32)
-            both = jnp.dot(pick_y, across.astype(jnp.bfloat16), preferred_element_type=jnp.float32)
-            for a in range(3):
-                piece = both[a * size : (a + 1) * size]
-                for tile in range(0, width, LANES):
-                    part = piece[:, tile : tile + LANES]
-                    where = (a * 3 + b, slice(None), slice(base + tile, base + tile + LANES))
-                    if base + tile < filled:
-                        part = part + moved_ref[where]
-                    moved_ref[where] = part
-        filled = base + width
+        for k in range(reach):
+            wanted = jnp.where(inside, wrapped(lane - (k - PEAK - 1), size) + begin, -1)
+            wanted = wanted.astype(jnp.float32).astype(jnp.bfloat16)
+            across_ref[j * reach + k] = jnp.where(source == wanted, one, none)
+
+
+def splat_weights(codes_ref, aux_ref):
+    cols = codes_ref.shape[2]
     sub = iota((SUBLANES, LANES), 0)
     lane = iota((SUBLANES, LANES), 1)
     zero = jnp.zeros((SUBLANES, LANES), jnp.int32)
@@ -112,20 +102,65 @@
     aux_ref[2] = shift_x.astype(jnp.float32)
 
 
-def correlate(moved_ref, aux_ref, second_ref, flow_ref, splat_ref):
+def move(codes_ref, rows_ref, across_ref, first_ref, moved_ref, aux_ref):
     size = PATCH_SIZE
-    cols = flow_ref.shape[3]
+    cols = codes_ref.shape[2]
+    splat_weights(codes_ref, aux_ref)
+    downs = []
+    for j, base, width, _ in windows(cols, size):
+        window = first_ref[0, :, base : base + width]
+        down = jnp.dot(
+            rows_ref[codes_ref[0, 0, j] // 5], window, preferred_element_type=jnp.float32
+        )
+        downs.append(down.astype(jnp.bfloat16))
+    for b in range(3):
+        kept = {}
+        for j, base, width, _ in windows(cols, size):
+            pick = across_ref[j * (2 * PEAK + 3) + codes_ref[0, 0, j] % 5 + b]
+            across = jnp.dot(downs[j], pick, preferred_element_type=jnp.float32)
+            for tile in range(0, width, LANES):
+                part = across[:, tile : tile + LANES]
+                kept[base + tile] = kept[base + tile] + part if base + tile in kept else part
+        for tile, part in kept.items():
+            moved_ref[b, :, tile : tile + LANES] = part
+
+
+def correlate(moved_ref, aux_ref, own_ref, even_ref, late_ref, splat_ref, held_ref):
+    size = PATCH_SIZE
+    cols = own_ref.shape[2] // size
+    section = lax.axis_index("gz")
+
+    def stage(second_ref):
+        for tile in range(cols * size // LANES):
+            lanes = slice(tile * LANES, (tile + 1) * LANES)
+            for top in range(0, size, 16):
+                later = second_ref[0, top : top + 16, lanes].astype(jnp.float32)
+                held_ref[tile, SUBLANES + top : SUBLANES + top + 16, :] = later
+                if top == 0:
+                    held_ref[tile, SUBLANES + size : 2 * SUBLANES + size, :] = later[:SUBLANES]
+                if top + 16 == size:
+                    held_ref[tile, :SUBLANES, :] = later[SUBLANES:]
+
+    odd = lax.rem(section, 2) == 1
+    four = lax.rem(section, 4) == 0
+    pl.when(odd)(lambda: stage(own_ref))
+    pl.when(four)(lambda: stage(even_ref))
+    pl.when(jnp.logical_not(jnp.logical_or(odd, four)))(lambda: stage(late_ref))
     sub = iota((SUBLANES, LANES), 0)
     lane = iota((SUBLANES, LANES), 1)
     total = [jnp.zeros((SUBLANES, LANES), jnp.float32) for _ in range(LAGS)]
-    for base in range(0, cols * size, LANES):
+    for tile in range(cols * size // LANES):
+        base = tile * LANES
         sums = [None] * LAGS
-        for top in range(0, size, 16):
-            later = second_ref[0, top : top + 16, base : base + LANES].astype(jnp.float32)
-            for k in range(LAGS):
-                part = moved_ref[k, top : top + 16, base : base + LANES] * later
-                part = part[:SUBLANES] + part[SUBLANES:]
-                sums[k] = part if sums[k] is None else sums[k] + part
+        for top in range(0, size, SUBLANES):
+            first = [moved_ref[b, top : top + SUBLANES, base : base + LANES] for b in range(3)]
+            for a in range(3):
+                start = SUBLANES + top + a - 1
+                later = held_ref[tile, start : start + SUBLANES, :]
+                for b in range(3):
+                    part = first[b] * later
+                    k = a * 3 + b
+                    sums[k] = part if sums[k] is None else sums[k] + part
         own = (lane + base >= sub * size) & (lane + base < (sub + 1) * size)
         for k in range(LAGS):
             part = sums[k]
@@ -141,17 +176,20 @@
     flow_y = aux_ref[1] + num_y / energy
     flow_x = aux_ref[2] + num_x / energy
     value = jnp.where(lane < SPLAT, flow_y, jnp.where(lane < 2 * SPLAT, flow_x, 1.0))
-    row = jnp.sum(aux_ref[0] * value, axis=0, keepdims=True)
+    value = aux_ref[0] * value
+    value = jnp.where(lane == 3 * SPLAT + sub, flow_y, value)
+    value = jnp.where(lane == 3 * SPLAT + cols + sub, flow_x, value)
+    row = jnp.sum(jnp.where(sub < cols, value, 0.0), axis=0, keepdims=True)
     splat_ref[...] = jnp.broadcast_to(row, splat_ref.shape)
-    for q, flow in enumerate((flow_y, flow_x)):
-        flow_ref[q, 0] = jnp.sum(jnp.where(lane == sub, flow, 0.0), axis=0, keepdims=True)[:, :cols]
-
-
-def relax(strips, splat_ref, held_ref, flow_ref, out_ref, sem):
-    keep = pltpu.make_async_copy(held_ref, flow_ref, sem)
-    keep.start()
+
+
+def relax(strips, splat_ref, flow_ref, out_ref):
     sections = splat_ref.shape[0] // strips
     section, strip = lax.axis_index("gz"), lax.axis_index("xy")
+    cols = flow_ref.shape[3]
+    home = splat_ref[pl.ds((section ^ 1) * strips + strip, 1), :]
+    for q in range(2):
+        flow_ref[q, 0] = pltpu.roll(home, LANES - 3 * SPLAT - q * cols, 1)[:, :cols]
     length = strips * BAND
     tiles = -(-length // LANES)
     lane = iota((sections, LANES), 1)
@@ -166,7 +204,7 @@
             if start + SPLAT > LANES and tile + 1 < tiles:
                 spill = lane < start + SPLAT - LANES
                 grid[q][tile + 1] = grid[q][tile + 1] + jnp.where(spill, moved, 0.0)
-    below = iota((sections, LANES), 0) < section
+    below = (iota((sections, LANES), 0) ^ 1) < section
     fixed = []
     for q in range(2):
         parts = []
@@ -206,7 +244,18 @@
         for i in range(BAND_ROWS):
             turn = lax.rem(2 * width - strip * BAND - i * NODE_COLS, width)
             out_ref[q, 0, i : i + 1, :] = pltpu.roll(now, turn, 1)[:1, :NODE_COLS]
-    keep.wait()
+
+
+def call(kernel, out_shape, in_specs, flops=0, **settings):
+    return pl.pallas_call(
+        kernel,
+        out_shape=out_shape,
+        in_specs=in_specs,
+        out_specs=jax.tree.map(lambda _: VMEM, out_shape),
+        compiler_params=pltpu.CompilerParams(vmem_limit_bytes=24 << 20),
+        cost_estimate=pl.CostEstimate(flops=flops, bytes_accessed=4_000_000, transcendentals=0),
+        **settings,
+    )
 
 
 def on_device(images, peak_code, cell_block, cell_offset, valid_patch):
@@ -214,44 +263,52 @@
     cols = breadth // PATCH_SIZE
     sections, strips = lax.axis_size("gz"), lax.axis_size("xy")
     devices = sections * strips
-    following = lax.ppermute(images, "gz", [(i + 1, i) for i in range(sections - 1)])
+    pair = [(i ^ 1, i) for i in range(sections)]
+    two = [(i ^ 2, i) for i in range(sections)]
+    late = [(i + 2, i) for i in range(2, sections - 2, 4)]
     codes = jnp.concatenate([peak_code, cell_block, cell_offset, valid_patch], axis=1)
-    moved, aux = pl.pallas_call(
-        prepare,
-        out_shape=(
-            pltpu.VMEM((LAGS, size, breadth), jnp.float32),
+    first = lax.ppermute(images, "gz", pair)
+    codes = lax.ppermute(codes, "gz", pair)
+    even = lax.ppermute(images, "gz", two)
+    late = lax.ppermute(images, "gz", late)
+    width = max(w for _, _, w, _ in windows(cols, PATCH_SIZE))
+    rows, across = call(
+        bank,
+        (
+            pltpu.VMEM((2 * PEAK + 1, size, size), jnp.bfloat16),
+            pltpu.VMEM((cols * (2 * PEAK + 3), width, width), jnp.bfloat16),
+        ),
+        [],
+        flops=1_000_000_000,
+        name="bank",
+    )()
+    moved, aux = call(
+        move,
+        (
+            pltpu.VMEM((3, size, breadth), jnp.float32),
             pltpu.VMEM((3, SUBLANES, LANES), jnp.float32),
         ),
-        in_specs=[SMEM, VMEM],
-        out_specs=[VMEM, VMEM],
-        compiler_params=pltpu.CompilerParams(vmem_limit_bytes=24 << 20),
-        cost_estimate=pl.CostEstimate(flops=2_000_000_000, bytes_accessed=4_000_000, transcendentals=0),
-        name="prepare",
-    )(codes, images)
-    held, splat = pl.pallas_call(
+        [SMEM] + [VMEM] * 3,
+        flops=1_000_000_000,
+        name="move",
+    )(codes, rows, across, first)
+    splat = call(
         correlate,
-        out_shape=(
-            pltpu.VMEM((2, 1, 1, cols), jnp.float32),
-            pltpu.VMEM((devices, LANES), jnp.float32),
-        ),
-        in_specs=[VMEM, VMEM, VMEM],
-        out_specs=[VMEM, VMEM],
-        compiler_params=pltpu.CompilerParams(vmem_limit_bytes=24 << 20),
+        pltpu.VMEM((devices, LANES), jnp.float32),
+        [VMEM] * 5,
+        scratch_shapes=[pltpu.VMEM((breadth // LANES, size + 2 * SUBLANES, LANES), jnp.float32)],
         name="correlate",
-    )(moved, aux, following)
+    )(moved, aux, images, even, late)
     gathered = lax.all_to_all(splat, ("gz", "xy"), 0, 0, tiled=True)
-    flow, node_shift = pl.pallas_call(
+    flow, node_shift = call(
         functools.partial(relax, strips),
-        out_shape=(
-            jax.ShapeDtypeStruct(held.shape, jnp.float32),
+        (
+            jax.ShapeDtypeStruct((2, 1, 1, cols), jnp.float32),
             jax.ShapeDtypeStruct((2, 1, BAND_ROWS, NODE_COLS), jnp.float32),
         ),
-        in_specs=[VMEM, VMEM],
-        out_specs=[HBM, VMEM],
-        scratch_shapes=[pltpu.SemaphoreType.DMA],
-        compiler_params=pltpu.CompilerParams(vmem_limit_bytes=24 << 20),
+        [VMEM],
         name="relax",
-    )(gathered, held)
+    )(gathered)
     return (flow, node_shift)
 
 

time: 25.6 us -> 25.1 us (0.980)
  starting transfers between devices: 1.29 us -> 5.84 us
  waiting for transfers between devices: 4.59 us -> 2.56 us
  blocking collectives: 12.9 us -> 11.8 us
  Pallas kernels: 4.31 us -> 3.38 us
  local copies, waits for them, and re-layouts: 0.93 us -> 0.01 us
    ppermute x1 -> x4, starting transfers between devices: 1.29 us -> 5.84 us  [the longest x1 3 us: on_device(): first = lax.ppermute(images, 'gz', pair)]
    ppermute x1 -> x4, waiting for transfers between devices: 4.59 us -> 2.56 us  [the longest x1 2.55 us: on_device(): codes = lax.ppermute(codes, 'gz', pair)]
    all_to_all x1, blocking collectives: 12.9 us -> 11.8 us  [on_device(): gathered = lax.all_to_all(splat, ('gz', 'xy'), 0, 0, tiled=True)]
    pallas_call x3 -> x4, Pallas kernels: 4.31 us -> 3.38 us  [the longest x1 1.16 us: on_device(): call(move, (pltpu.VMEM((3, size, breadth), jnp.float32), pltpu.VMEM((3, S...]
    unnamed x2, local copies, waits for them, and re-layouts: 0.93 us -> 0.01 us
  transfers between devices with their start and end apart: 1 -> 4, of which waited for: 1 -> 1; matrix products, arithmetic and copies ran while one was open for 3% -> 3% of each run, Pallas kernels for 10% -> 7%
where the time goes in v3:
time: 25.1 us; the launch traced here: 24.9 us
  blocking collectives  11.8 us (47%)
  starting transfers between devices  5.84 us (23%)
  Pallas kernels  3.38 us (13%)
  waiting for transfers between devices  2.56 us (10%)
  other arithmetic  0.72 us (3%)
  between operations  0.68 us (3%)
    all_to_all x1, blocking collectives, on_device(): gathered = lax.all_to_all(splat, ('gz', 'xy'), 0, 0, tiled=True)  11.8 us
    ppermute x1, starting transfers between devices, on_device(): first = lax.ppermute(images, 'gz', pair)  3 us
    ppermute x1, waiting for transfers between devices, on_device(): codes = lax.ppermute(codes, 'gz', pair)  2.55 us
    ppermute x1, starting transfers between devices, on_device(): even = lax.ppermute(images, 'gz', two)  1.58 us
    pallas_call x1, Pallas kernels, on_device(): call(move, (pltpu.VMEM((3, size, breadth), jnp.float32), pltpu.VMEM((3, S...  1.16 us
    pallas_call x1, Pallas kernels, on_device(): call(functools.partial(relax, strips), (jax.ShapeDtypeStruct((2, 1, 1, co...  1.13 us
    concatenate x1, other arithmetic, on_device(): jnp.concatenate([peak_code, cell_block, cell_offset, valid_patch], axis=1)  0.72 us
    ppermute x1, starting transfers between devices, on_device(): late = lax.ppermute(images, 'gz', late)  0.66 us
  transfers between devices with their start and end apart: 4, of which 1 were waited for; matrix products, arithmetic and copies ran while one was open for 3% of the time, Pallas kernels for 7%

profile of v3, /device:TPU:0, one launch (start us, length us, event | category | flops | bytes accessed | tf_op | source)
XLA Modules:
  0.0 24.9 jit_solution(15042976947099358845)
XLA Ops:
  0.6 3.0 %collective-permute-start.1 = (bf16[1,160,640]{2,1,0:T(8,128)(2,1)}, bf16[1,160,640]{2,1,0:T(8,128)(2,1)S(1)}, u32[]{:S(2)}, u32[]{:S(2)}) collective-permute-start(bf16[1,160,640]{2,1,0:T(8,128)(2,1)} %own_ref.1), channel_id=1, source_target_pairs={{4,0},{0,4},{12,8},{8,12},{20,16},{16,20},{28,24},{24,28},{5,1},{1... | collective-permute-start | bytes 614408 | tf_op jit(solution)/shard_map/ppermute | solution.py:270
  3.6 1.6 %collective-permute-start.2 = (bf16[1,160,640]{2,1,0:T(8,128)(2,1)}, bf16[1,160,640]{2,1,0:T(8,128)(2,1)S(1)}, u32[]{:S(2)}, u32[]{:S(2)}) collective-permute-start(bf16[1,160,640]{2,1,0:T(8,128)(2,1)} %own_ref.1), channel_id=1, source_target_pairs={{8,0},{12,4},{0,8},{4,12},{24,16},{28,20},{16,24},{20,28},{9,1},{1... | collective-permute-start | bytes 614408 | tf_op jit(solution)/shard_map/ppermute | solution.py:272
  5.2 0.7 %collective-permute-start.3 = (bf16[1,160,640]{2,1,0:T(8,128)(2,1)}, bf16[1,160,640]{2,1,0:T(8,128)(2,1)S(1)}, u32[]{:S(2)}, u32[]{:S(2)}) collective-permute-start(bf16[1,160,640]{2,1,0:T(8,128)(2,1)} %own_ref.1), channel_id=1, source_target_pairs={{16,8},{17,9},{18,10},{19,11}} | collective-permute-start | bytes 614408 | tf_op jit(solution)/shard_map/ppermute | solution.py:273
  5.9 0.7 %pad_add_fusion = s32[1,4,4]{2,1,0:T(4,128)S(1)} fusion(s32[1,1,4]{2,1,0:T(1,128)} %param.9, s32[1,1,4]{2,1,0:T(1,128)} %param.8, s32[1,1,4]{2,1,0:T(1,128)} %param.7, s32[1,1,4]{2,1,0:T(1,128)} %param.6), kind=kLoop, calls=%fused_computation | loop fusion | flops 48 | bytes 128 | tf_op jit(solution)/shard_map/concatenate | solution.py:269
  6.6 0.0 copy-start
  6.6 0.6 %collective-permute-start = (s32[1,4,4]{2,1,0:T(4,128)S(1)}, s32[1,4,4]{2,1,0:T(4,128)S(1)}, u32[]{:S(2)}, u32[]{:S(2)}) collective-permute-start(s32[1,4,4]{2,1,0:T(4,128)S(1)} %pad_add_fusion), channel_id=1, source_target_pairs={{4,0},{0,4},{12,8},{8,12},{20,16},{16,20},{28,24},{24,28},{5,1},{1... | collective-permute-start | bytes 200 | tf_op jit(solution)/shard_map/ppermute | solution.py:271
  7.2 0.5 %bank.1 = (bf16[5,160,160]{2,1,0:T(8,128)(2,1)S(1)}, bf16[28,256,256]{2,1,0:T(8,128)(2,1)S(1)}) custom-call(), custom_call_target="tpu_custom_call" | custom-call | flops 1000000000 | bytes 4000000 | tf_op jit(solution)/shard_map/bank/pallas_call | solution.py:275
  7.7 2.5 %collective-permute-done.codes_ref = s32[1,4,4]{2,1,0:T(4,128)S(1)} collective-permute-done((s32[1,4,4]{2,1,0:T(4,128)S(1)}, s32[1,4,4]{2,1,0:T(4,128)S(1)}, u32[]{:S(2)}, u32[]{:S(2)}) %collective-permute-start) | collective-permute-done | bytes 96 | tf_op jit(solution)/shard_map/ppermute | solution.py:271
  10.3 0.0 collective-permute-done.1.first_ref
  10.3 1.2 %move.1 = (f32[3,160,640]{2,1,0:T(8,128)S(1)}, f32[3,8,128]{2,1,0:T(8,128)S(1)}) custom-call(s32[1,4,4]{2,1,0:T(4,128)S(1)} %collective-permute-done.codes_ref, bf16[5,160,160]{2,1,0:T(8,128)(2,1)S(1)} %get-tuple-element.6.rows_ref, bf16[28,256,256]{2,1,0:T(8,128)(2,1)S(1)} %get-tuple-element.7.across_ref, ...), custom_call_target="tpu_custom_call" | custom-call | flops 1000000000 | bytes 4000000 | tf_op jit(solution)/shard_map/move/pallas_call | solution.py:285
  11.4 0.0 collective-permute-done.2.even_ref
  11.4 0.0 collective-permute-done.3.late_ref
  11.4 0.0 copy-done
  11.5 0.6 %correlate.1 = f32[32,128]{1,0:T(8,128)S(1)} custom-call(f32[3,160,640]{2,1,0:T(8,128)S(1)} %get-tuple-element.8.moved_ref, f32[3,8,128]{2,1,0:T(8,128)S(1)} %get-tuple-element.9.aux_ref, bf16[1,160,640]{2,1,0:T(8,128)(2,1)S(1)} %copy-done, bf16[1,160,640]{2,1,0:T(8,128)(2,1)S(1)} %collective-permute-done.2.even_ref, ...), custom_call_target="tpu_custom_call" | custom-call | bytes 4000000 | tf_op jit(solution)/shard_map/correlate/pallas_call | solution.py:295
  12.0 11.8 %all_to_all.11 = f32[32,1,128]{2,1,0:T(1,128)S(1)} all-to-all(f32[32,1,128]{2,1,0:T(1,128)S(1)} %bitcast.4), channel_id=1, replica_groups=mesh['gz'=8,'xy'=4] {'gz','xy'}, dimensions={0} | all-to-all | bytes 32768 | tf_op jit(solution)/shard_map/all_to_all | solution.py:302
  23.8 1.1 %relax.1 = (f32[2,1,1,4]{3,2,1,0:T(1,128)}, f32[2,1,4,8]{3,2,1,0:T(4,128)}) custom-call(f32[32,128]{1,0:T(8,128)S(1)} %bitcast.5), custom_call_target="tpu_custom_call" | custom-call | bytes 4000000 | tf_op jit(solution)/shard_map/relax/pallas_call | solution.py:303
Async XLA Ops:
  0.6 9.6 %collective-permute-start.1 = (bf16[1,160,640]{2,1,0:T(8,128)(2,1)}, bf16[1,160,640]{2,1,0:T(8,128)(2,1)S(1)}, u32[]{:S(2)}, u32[]{:S(2)}) collective-permute-start(bf16[1,160,640]{2,1,0:T(8,128)(2,1)} %own_ref.1), channel_id=1, source_target_pairs={{4,0},{0,4},{12,8},{8,12},{20,16},{16,20},{28,24},{24,28},{5,1},{1... | collective-permute-start | bytes 614408 | tf_op jit(solution)/shard_map/ppermute | solution.py:270
  3.6 7.8 %collective-permute-start.2 = (bf16[1,160,640]{2,1,0:T(8,128)(2,1)}, bf16[1,160,640]{2,1,0:T(8,128)(2,1)S(1)}, u32[]{:S(2)}, u32[]{:S(2)}) collective-permute-start(bf16[1,160,640]{2,1,0:T(8,128)(2,1)} %own_ref.1), channel_id=1, source_target_pairs={{8,0},{12,4},{0,8},{4,12},{24,16},{28,20},{16,24},{20,28},{9,1},{1... | collective-permute-start | bytes 614408 | tf_op jit(solution)/shard_map/ppermute | solution.py:272
  5.2 6.2 %collective-permute-start.3 = (bf16[1,160,640]{2,1,0:T(8,128)(2,1)}, bf16[1,160,640]{2,1,0:T(8,128)(2,1)S(1)}, u32[]{:S(2)}, u32[]{:S(2)}) collective-permute-start(bf16[1,160,640]{2,1,0:T(8,128)(2,1)} %own_ref.1), channel_id=1, source_target_pairs={{16,8},{17,9},{18,10},{19,11}} | collective-permute-start | bytes 614408 | tf_op jit(solution)/shard_map/ppermute | solution.py:273
  6.6 4.8 %copy-start = (bf16[1,160,640]{2,1,0:T(8,128)(2,1)S(1)}, bf16[1,160,640]{2,1,0:T(8,128)(2,1)}, u32[]{:S(2)}) copy-start(bf16[1,160,640]{2,1,0:T(8,128)(2,1)} %own_ref.1) | copy-start | bytes 614404
  6.6 3.7 %collective-permute-start = (s32[1,4,4]{2,1,0:T(4,128)S(1)}, s32[1,4,4]{2,1,0:T(4,128)S(1)}, u32[]{:S(2)}, u32[]{:S(2)}) collective-permute-start(s32[1,4,4]{2,1,0:T(4,128)S(1)} %pad_add_fusion), channel_id=1, source_target_pairs={{4,0},{0,4},{12,8},{8,12},{20,16},{16,20},{28,24},{24,28},{5,1},{1... | collective-permute-start | bytes 200 | tf_op jit(solution)/shard_map/ppermute | solution.py:271

commit v4 on v3

--- a/solution.py
+++ b/solution.py
@@ -27,7 +27,6 @@
 damping = 0.6
 
 VMEM = pl.BlockSpec(memory_space=pltpu.VMEM)
-SMEM = pl.BlockSpec(memory_space=pltpu.SMEM)
 
 
 def iota(shape, dim):
@@ -66,57 +65,56 @@
             across_ref[j * reach + k] = jnp.where(source == wanted, one, none)
 
 
-def splat_weights(codes_ref, aux_ref):
-    cols = codes_ref.shape[2]
-    sub = iota((SUBLANES, LANES), 0)
+def split(value, parts):
+    over = jnp.floor((value + 0.5) * (1.0 / parts))
+    return over, value - over * parts
+
+
+def splat_weights(codes, aux_ref):
+    cols = codes.shape[1]
+    sub = iota((SUBLANES, cols), 0)
+    lane = iota((SUBLANES, cols), 1)
+    code, block, offset, valid = (
+        jnp.sum(jnp.where(lane == sub, codes[q : q + 1], 0.0), axis=1, keepdims=True)
+        for q in range(4)
+    )
+    shift_y, shift_x = (part - PEAK for part in split(code, 2 * PEAK + 1))
+    cell_row, cell_col = split(block, NODE_COLS - 1)
+    part_y, part_x = split(offset, CELL_SUBDIV)
     lane = iota((SUBLANES, LANES), 1)
-    zero = jnp.zeros((SUBLANES, LANES), jnp.int32)
-    rows = [zero] * 7
-    for p in range(cols):
-        code, block, offset, valid = (codes_ref[0, q, p] for q in range(4))
-        held = (
-            code // 5 - 2,
-            code % 5 - 2,
-            block // (NODE_COLS - 1),
-            block % (NODE_COLS - 1),
-            offset // CELL_SUBDIV,
-            offset % CELL_SUBDIV,
-            valid,
-        )
-        rows = [jnp.where(sub == p, value, before) for value, before in zip(held, rows)]
-    shift_y, shift_x, cell_row, cell_col, part_y, part_x, valid = rows
-    frac_y = part_y.astype(jnp.float32) / CELL_SUBDIV
-    frac_x = part_x.astype(jnp.float32) / CELL_SUBDIV
+    frac_y = part_y / CELL_SUBDIV
+    frac_x = part_x / CELL_SUBDIV
     spot = jnp.where(lane >= 2 * SPLAT, lane - 2 * SPLAT, jnp.where(lane >= SPLAT, lane - SPLAT, lane))
-    node_row = spot >> 3
-    node_col = spot & (NODE_COLS - 1)
+    node_row = (spot >> 3).astype(jnp.float32)
+    node_col = (spot & (NODE_COLS - 1)).astype(jnp.float32)
     weight_y = jnp.where(cell_row == node_row, 1.0 - frac_y, 0.0) + jnp.where(
         cell_row + 1 == node_row, frac_y, 0.0
     )
     weight_x = jnp.where(cell_col == node_col, 1.0 - frac_x, 0.0) + jnp.where(
         cell_col + 1 == node_col, frac_x, 0.0
     )
-    weight = weight_y * weight_x * valid.astype(jnp.float32)
+    weight = weight_y * weight_x * valid
     aux_ref[0] = jnp.where(lane < 3 * SPLAT, weight, 0.0)
-    aux_ref[1] = shift_y.astype(jnp.float32)
-    aux_ref[2] = shift_x.astype(jnp.float32)
+    aux_ref[1] = jnp.broadcast_to(shift_y, (SUBLANES, LANES))
+    aux_ref[2] = jnp.broadcast_to(shift_x, (SUBLANES, LANES))
 
 
 def move(codes_ref, rows_ref, across_ref, first_ref, moved_ref, aux_ref):
     size = PATCH_SIZE
     cols = codes_ref.shape[2]
-    splat_weights(codes_ref, aux_ref)
+    codes = codes_ref[0]
+    lane = iota((1, cols), 1)
+    peaks = [jnp.sum(jnp.where(lane == j, codes[:1], 0)) for j in range(cols)]
+    splat_weights(codes.astype(jnp.float32), aux_ref)
     downs = []
     for j, base, width, _ in windows(cols, size):
         window = first_ref[0, :, base : base + width]
-        down = jnp.dot(
-            rows_ref[codes_ref[0, 0, j] // 5], window, preferred_element_type=jnp.float32
-        )
+        down = jnp.dot(rows_ref[peaks[j] // 5], window, preferred_element_type=jnp.float32)
         downs.append(down.astype(jnp.bfloat16))
     for b in range(3):
         kept = {}
         for j, base, width, _ in windows(cols, size):
-            pick = across_ref[j * (2 * PEAK + 3) + codes_ref[0, 0, j] % 5 + b]
+            pick = across_ref[j * (2 * PEAK + 3) + peaks[j] % 5 + b]
             across = jnp.dot(downs[j], pick, preferred_element_type=jnp.float32)
             for tile in range(0, width, LANES):
                 part = across[:, tile : tile + LANES]
@@ -288,7 +286,7 @@
             pltpu.VMEM((3, size, breadth), jnp.float32),
             pltpu.VMEM((3, SUBLANES, LANES), jnp.float32),
         ),
-        [SMEM] + [VMEM] * 3,
+        [VMEM] * 4,
         flops=1_000_000_000,
         name="move",
     )(codes, rows, across, first)

time: 25.1 us -> 24.6 us (0.980)
  Pallas kernels: 3.38 us -> 2.87 us
    pallas_call x1, Pallas kernels: 1.16 us -> 0.66 us  [on_device(): call(move, (pltpu.VMEM((3, size, breadth), jnp.float32), pltpu.VMEM((3, S...]
  transfers between devices with their start and end apart: 4 -> 4, of which waited for: 1 -> 1; matrix products, arithmetic and copies ran while one was open for 3% -> 3% of each run, Pallas kernels for 7% -> 5%
where the time goes in v4:
time: 24.6 us; the launch traced here: 24.4 us
  blocking collectives  11.8 us (48%)
  starting transfers between devices  5.84 us (24%)
  Pallas kernels  2.87 us (12%)
  waiting for transfers between devices  2.56 us (10%)
  other arithmetic  0.72 us (3%)
  between operations  0.68 us (3%)
    all_to_all x1, blocking collectives, on_device(): gathered = lax.all_to_all(splat, ('gz', 'xy'), 0, 0, tiled=True)  11.8 us
    ppermute x1, starting transfers between devices, on_device(): first = lax.ppermute(images, 'gz', pair)  3 us
    ppermute x1, waiting for transfers between devices, on_device(): codes = lax.ppermute(codes, 'gz', pair)  2.55 us
    ppermute x1, starting transfers between devices, on_device(): even = lax.ppermute(images, 'gz', two)  1.58 us
    pallas_call x1, Pallas kernels, on_device(): call(functools.partial(relax, strips), (jax.ShapeDtypeStruct((2, 1, 1, co...  1.13 us
    concatenate x1, other arithmetic, on_device(): jnp.concatenate([peak_code, cell_block, cell_offset, valid_patch], axis=1)  0.72 us
    ppermute x1, starting transfers between devices, on_device(): late = lax.ppermute(images, 'gz', late)  0.66 us
    pallas_call x1, Pallas kernels, on_device(): call(move, (pltpu.VMEM((3, size, breadth), jnp.float32), pltpu.VMEM((3, S...  0.66 us
  transfers between devices with their start and end apart: 4, of which 1 were waited for; matrix products, arithmetic and copies ran while one was open for 3% of the time, Pallas kernels for 5%

profile of v4, /device:TPU:0, one launch (start us, length us, event | category | flops | bytes accessed | tf_op | source)
XLA Modules:
  0.0 24.4 jit_solution(10653523981876570500)
XLA Ops:
  0.6 3.0 %collective-permute-start.1 = (bf16[1,160,640]{2,1,0:T(8,128)(2,1)}, bf16[1,160,640]{2,1,0:T(8,128)(2,1)S(1)}, u32[]{:S(2)}, u32[]{:S(2)}) collective-permute-start(bf16[1,160,640]{2,1,0:T(8,128)(2,1)} %own_ref.1), channel_id=1, source_target_pairs={{4,0},{0,4},{12,8},{8,12},{20,16},{16,20},{28,24},{24,28},{5,1},{1... | collective-permute-start | bytes 614408 | tf_op jit(solution)/shard_map/ppermute | solution.py:268
  3.6 1.6 %collective-permute-start.2 = (bf16[1,160,640]{2,1,0:T(8,128)(2,1)}, bf16[1,160,640]{2,1,0:T(8,128)(2,1)S(1)}, u32[]{:S(2)}, u32[]{:S(2)}) collective-permute-start(bf16[1,160,640]{2,1,0:T(8,128)(2,1)} %own_ref.1), channel_id=1, source_target_pairs={{8,0},{12,4},{0,8},{4,12},{24,16},{28,20},{16,24},{20,28},{9,1},{1... | collective-permute-start | bytes 614408 | tf_op jit(solution)/shard_map/ppermute | solution.py:270
  5.2 0.7 %collective-permute-start.3 = (bf16[1,160,640]{2,1,0:T(8,128)(2,1)}, bf16[1,160,640]{2,1,0:T(8,128)(2,1)S(1)}, u32[]{:S(2)}, u32[]{:S(2)}) collective-permute-start(bf16[1,160,640]{2,1,0:T(8,128)(2,1)} %own_ref.1), channel_id=1, source_target_pairs={{16,8},{17,9},{18,10},{19,11}} | collective-permute-start | bytes 614408 | tf_op jit(solution)/shard_map/ppermute | solution.py:271
  5.9 0.7 %pad_add_fusion = s32[1,4,4]{2,1,0:T(4,128)S(1)} fusion(s32[1,1,4]{2,1,0:T(1,128)} %param.9, s32[1,1,4]{2,1,0:T(1,128)} %param.8, s32[1,1,4]{2,1,0:T(1,128)} %param.7, s32[1,1,4]{2,1,0:T(1,128)} %param.6), kind=kLoop, calls=%fused_computation | loop fusion | flops 48 | bytes 128 | tf_op jit(solution)/shard_map/concatenate | solution.py:267
  6.6 0.0 copy-start
  6.6 0.6 %collective-permute-start = (s32[1,4,4]{2,1,0:T(4,128)S(1)}, s32[1,4,4]{2,1,0:T(4,128)S(1)}, u32[]{:S(2)}, u32[]{:S(2)}) collective-permute-start(s32[1,4,4]{2,1,0:T(4,128)S(1)} %pad_add_fusion), channel_id=1, source_target_pairs={{4,0},{0,4},{12,8},{8,12},{20,16},{16,20},{28,24},{24,28},{5,1},{1... | collective-permute-start | bytes 200 | tf_op jit(solution)/shard_map/ppermute | solution.py:269
  7.2 0.5 %bank.1 = (bf16[5,160,160]{2,1,0:T(8,128)(2,1)S(1)}, bf16[28,256,256]{2,1,0:T(8,128)(2,1)S(1)}) custom-call(), custom_call_target="tpu_custom_call" | custom-call | flops 1000000000 | bytes 4000000 | tf_op jit(solution)/shard_map/bank/pallas_call | solution.py:273
  7.7 2.5 %collective-permute-done.codes_ref = s32[1,4,4]{2,1,0:T(4,128)S(1)} collective-permute-done((s32[1,4,4]{2,1,0:T(4,128)S(1)}, s32[1,4,4]{2,1,0:T(4,128)S(1)}, u32[]{:S(2)}, u32[]{:S(2)}) %collective-permute-start) | collective-permute-done | bytes 96 | tf_op jit(solution)/shard_map/ppermute | solution.py:269
  10.3 0.0 collective-permute-done.1.first_ref
  10.3 0.7 %move.1 = (f32[3,160,640]{2,1,0:T(8,128)S(1)}, f32[3,8,128]{2,1,0:T(8,128)S(1)}) custom-call(s32[1,4,4]{2,1,0:T(4,128)S(1)} %collective-permute-done.codes_ref, bf16[5,160,160]{2,1,0:T(8,128)(2,1)S(1)} %get-tuple-element.6.rows_ref, bf16[28,256,256]{2,1,0:T(8,128)(2,1)S(1)} %get-tuple-element.7.across_ref, ...), custom_call_target="tpu_custom_call" | custom-call | flops 1000000000 | bytes 4000000 | tf_op jit(solution)/shard_map/move/pallas_call | solution.py:283
  10.9 0.0 collective-permute-done.2.even_ref
  10.9 0.0 collective-permute-done.3.late_ref
  10.9 0.0 copy-done
  11.0 0.6 %correlate.1 = f32[32,128]{1,0:T(8,128)S(1)} custom-call(f32[3,160,640]{2,1,0:T(8,128)S(1)} %get-tuple-element.8.moved_ref, f32[3,8,128]{2,1,0:T(8,128)S(1)} %get-tuple-element.9.aux_ref, bf16[1,160,640]{2,1,0:T(8,128)(2,1)S(1)} %copy-done, bf16[1,160,640]{2,1,0:T(8,128)(2,1)S(1)} %collective-permute-done.2.even_ref, ...), custom_call_target="tpu_custom_call" | custom-call | bytes 4000000 | tf_op jit(solution)/shard_map/correlate/pallas_call | solution.py:293
  11.5 11.8 %all_to_all.11 = f32[32,1,128]{2,1,0:T(1,128)S(1)} all-to-all(f32[32,1,128]{2,1,0:T(1,128)S(1)} %bitcast.4), channel_id=1, replica_groups=mesh['gz'=8,'xy'=4] {'gz','xy'}, dimensions={0} | all-to-all | bytes 32768 | tf_op jit(solution)/shard_map/all_to_all | solution.py:300
  23.3 1.1 %relax.1 = (f32[2,1,1,4]{3,2,1,0:T(1,128)}, f32[2,1,4,8]{3,2,1,0:T(4,128)}) custom-call(f32[32,128]{1,0:T(8,128)S(1)} %bitcast.5), custom_call_target="tpu_custom_call" | custom-call | bytes 4000000 | tf_op jit(solution)/shard_map/relax/pallas_call | solution.py:301
Async XLA Ops:
  0.6 9.6 %collective-permute-start.1 = (bf16[1,160,640]{2,1,0:T(8,128)(2,1)}, bf16[1,160,640]{2,1,0:T(8,128)(2,1)S(1)}, u32[]{:S(2)}, u32[]{:S(2)}) collective-permute-start(bf16[1,160,640]{2,1,0:T(8,128)(2,1)} %own_ref.1), channel_id=1, source_target_pairs={{4,0},{0,4},{12,8},{8,12},{20,16},{16,20},{28,24},{24,28},{5,1},{1... | collective-permute-start | bytes 614408 | tf_op jit(solution)/shard_map/ppermute | solution.py:268
  3.6 7.3 %collective-permute-start.2 = (bf16[1,160,640]{2,1,0:T(8,128)(2,1)}, bf16[1,160,640]{2,1,0:T(8,128)(2,1)S(1)}, u32[]{:S(2)}, u32[]{:S(2)}) collective-permute-start(bf16[1,160,640]{2,1,0:T(8,128)(2,1)} %own_ref.1), channel_id=1, source_target_pairs={{8,0},{12,4},{0,8},{4,12},{24,16},{28,20},{16,24},{20,28},{9,1},{1... | collective-permute-start | bytes 614408 | tf_op jit(solution)/shard_map/ppermute | solution.py:270
  5.2 5.7 %collective-permute-start.3 = (bf16[1,160,640]{2,1,0:T(8,128)(2,1)}, bf16[1,160,640]{2,1,0:T(8,128)(2,1)S(1)}, u32[]{:S(2)}, u32[]{:S(2)}) collective-permute-start(bf16[1,160,640]{2,1,0:T(8,128)(2,1)} %own_ref.1), channel_id=1, source_target_pairs={{16,8},{17,9},{18,10},{19,11}} | collective-permute-start | bytes 614408 | tf_op jit(solution)/shard_map/ppermute | solution.py:271
  6.6 4.3 %copy-start = (bf16[1,160,640]{2,1,0:T(8,128)(2,1)S(1)}, bf16[1,160,640]{2,1,0:T(8,128)(2,1)}, u32[]{:S(2)}) copy-start(bf16[1,160,640]{2,1,0:T(8,128)(2,1)} %own_ref.1) | copy-start | bytes 614404
  6.6 3.7 %collective-permute-start = (s32[1,4,4]{2,1,0:T(4,128)S(1)}, s32[1,4,4]{2,1,0:T(4,128)S(1)}, u32[]{:S(2)}, u32[]{:S(2)}) collective-permute-start(s32[1,4,4]{2,1,0:T(4,128)S(1)} %pad_add_fusion), channel_id=1, source_target_pairs={{4,0},{0,4},{12,8},{8,12},{20,16},{16,20},{28,24},{24,28},{5,1},{1... | collective-permute-start | bytes 200 | tf_op jit(solution)/shard_map/ppermute | solution.py:269

commit v5 on v4

--- a/solution.py
+++ b/solution.py
@@ -188,60 +188,76 @@
     home = splat_ref[pl.ds((section ^ 1) * strips + strip, 1), :]
     for q in range(2):
         flow_ref[q, 0] = pltpu.roll(home, LANES - 3 * SPLAT - q * cols, 1)[:, :cols]
-    length = strips * BAND
-    tiles = -(-length // LANES)
     lane = iota((sections, LANES), 1)
-    grid = [[jnp.zeros((sections, LANES), jnp.float32)] * tiles for _ in range(3)]
-    for r in range(strips):
-        rows = splat_ref[pl.ds(r, sections, stride=strips), :]
-        tile, start = divmod(r * BAND, LANES)
+    grid = [jnp.zeros((sections, LANES), jnp.float32)] * 3
+    for k in range(-2, 2):
+        at = strip + k
+        first = jnp.minimum(jnp.maximum(at, 0), strips - 1)
+        rows = splat_ref[pl.ds(first, sections, stride=strips), :]
+        base = (k + 1) * BAND
+        inside = (lane >= base) & (lane < base + SPLAT) & (at >= 0) & (at < strips)
         for q in range(3):
-            moved = pltpu.roll(rows, (start - q * SPLAT) % LANES, 1)
-            here = (lane >= start) & (lane < start + SPLAT)
-            grid[q][tile] = grid[q][tile] + jnp.where(here, moved, 0.0)
-            if start + SPLAT > LANES and tile + 1 < tiles:
-                spill = lane < start + SPLAT - LANES
-                grid[q][tile + 1] = grid[q][tile + 1] + jnp.where(spill, moved, 0.0)
+            moved = pltpu.roll(rows, (base - q * SPLAT) % LANES, 1)
+            grid[q] = grid[q] + jnp.where(inside, moved, 0.0)
     below = (iota((sections, LANES), 0) ^ 1) < section
     fixed = []
     for q in range(2):
-        parts = []
-        for tile in range(tiles):
-            target = jnp.where(below, grid[q][tile] / (1.0 + grid[2][tile]), 0.0)
-            part = jnp.sum(target, axis=0, keepdims=True)
-            parts.append(jnp.broadcast_to(part, (SUBLANES, LANES)))
-        fixed.append(parts[0] if tiles == 1 else jnp.concatenate(parts, axis=1))
-    width = tiles * LANES
-    node = iota((SUBLANES, width), 1)
-    col = node & (NODE_COLS - 1)
+        target = jnp.where(below, grid[q] / (1.0 + grid[2]), 0.0)
+        total = jnp.sum(target, axis=0, keepdims=True)
+        fixed.append(jnp.broadcast_to(total, (SUBLANES, LANES)))
+    reach = SPRING_STEPS
+    fields = {
+        o: tuple(
+            pltpu.roll(field, -NODE_COLS * o % LANES, 1, stride=1, stride_axis=0) for field in fixed
+        )
+        for o in range(-reach, reach + 1)
+    }
+    sub = iota((SUBLANES, LANES), 0)
+    row = strip * BAND_ROWS + (iota((SUBLANES, LANES), 1) >> 3) - BAND_ROWS
     one, none = 1.0, 0.0
-    springs = (
-        (NODE_COLS, jnp.where(node >= NODE_COLS, one, none), -rest_length, 0.0),
-        (width - NODE_COLS, jnp.where(node < length - NODE_COLS, one, none), rest_length, 0.0),
-        (1, jnp.where(col > 0, one, none), 0.0, -rest_length),
-        (width - 1, jnp.where(col < NODE_COLS - 1, one, none), 0.0, rest_length),
-    )
+    beside = jnp.where(sub > 0, one, none)
+    under = {
+        o: jnp.where((row + o >= 0) & (row + o + 1 < strips * BAND_ROWS), one, none)
+        for o in range(-reach, reach)
+    }
     rest_zero = math.sqrt(rest_length * rest_length + 1.0)
-    now_y, now_x = fixed
-    speed_y = speed_x = jnp.zeros((SUBLANES, width), jnp.float32)
-    for _ in range(SPRING_STEPS):
-        push_y = flow_stiff * (fixed[0] - now_y)
-        push_x = flow_stiff * (fixed[1] - now_x)
-        for turn, present, rest_y, rest_x in springs:
-            gap_y = rest_y + pltpu.roll(now_y, turn, 1) - now_y
-            gap_x = rest_x + pltpu.roll(now_x, turn, 1) - now_x
-            inverse = lax.rsqrt(gap_y * gap_y + gap_x * gap_x + 1.0)
-            tension = (1.0 - rest_zero * inverse) * present
-            push_y = push_y + tension * gap_y
-            push_x = push_x + tension * gap_x
-        speed_y = damping * speed_y + time_step * push_y
-        speed_x = damping * speed_x + time_step * push_x
-        now_y = now_y + time_step * speed_y
-        now_x = now_x + time_step * speed_x
-    for q, now in enumerate((now_y, now_x)):
+
+    def pull(gap_y, gap_x, present):
+        inverse = lax.rsqrt(gap_y * gap_y + gap_x * gap_x + 1.0)
+        tension = (1.0 - rest_zero * inverse) * present
+        return tension * gap_y, tension * gap_x
+
+    now = dict(fields)
+    speed = {}
+    for step in range(SPRING_STEPS):
+        reach = SPRING_STEPS - 1 - step
+        down = {}
+        for o in range(-reach - 1, reach + 1):
+            gap_y = (rest_length + now[o + 1][0]) - now[o][0]
+            down[o] = pull(gap_y, now[o + 1][1] - now[o][1], under[o])
+        later = {}
+        for o in range(-reach, reach + 1):
+            gap_x = (rest_length + pltpu.roll(now[o][1], 1, 0)) - now[o][1]
+            right = pull(pltpu.roll(now[o][0], 1, 0) - now[o][0], gap_x, beside)
+            moved = []
+            for q in range(2):
+                left = pltpu.roll(right[q], SUBLANES - 1, 0)
+                push = (down[o][q] - down[o - 1][q]) + (right[q] - left)
+                if step > 0:
+                    push = push + flow_stiff * (fields[o][q] - now[o][q])
+                rate = time_step * push
+                if step > 0:
+                    rate = damping * speed[o, q] + rate
+                speed[o, q] = rate
+                moved.append(now[o][q] + time_step * rate)
+            later[o] = tuple(moved)
+        now = later
+    place = iota((SUBLANES, NODE_COLS), 0) + iota((SUBLANES, NODE_COLS), 1) == NODE_COLS - 1
+    for q in range(2):
         for i in range(BAND_ROWS):
-            turn = lax.rem(2 * width - strip * BAND - i * NODE_COLS, width)
-            out_ref[q, 0, i : i + 1, :] = pltpu.roll(now, turn, 1)[:1, :NODE_COLS]
+            spot = BAND + (i + 1) * NODE_COLS - 1
+            column = jnp.where(place, now[0][q][:, spot : spot + 1], 0.0)
+            out_ref[q, 0, i : i + 1, :] = jnp.sum(column, axis=0, keepdims=True)
 
 
 def call(kernel, out_shape, in_specs, flops=0, **settings):

time: 24.6 us -> 24.5 us (level)
  no operation moved by 1% of the time
where the time goes in v5:
time: 24.5 us; the launch traced here: 24.3 us
  blocking collectives  11.8 us (48%)
  starting transfers between devices  5.84 us (24%)
  Pallas kernels  2.73 us (11%)
  waiting for transfers between devices  2.56 us (10%)
  other arithmetic  0.72 us (3%)
  between operations  0.68 us (3%)
    all_to_all x1, blocking collectives, on_device(): gathered = lax.all_to_all(splat, ('gz', 'xy'), 0, 0, tiled=True)  11.8 us
    ppermute x1, starting transfers between devices, on_device(): first = lax.ppermute(images, 'gz', pair)  3 us
    ppermute x1, waiting for transfers between devices, on_device(): codes = lax.ppermute(codes, 'gz', pair)  2.55 us
    ppermute x1, starting transfers between devices, on_device(): even = lax.ppermute(images, 'gz', two)  1.58 us
    pallas_call x1, Pallas kernels, on_device(): call(functools.partial(relax, strips), (jax.ShapeDtypeStruct((2, 1, 1, co...  0.99 us
    concatenate x1, other arithmetic, on_device(): jnp.concatenate([peak_code, cell_block, cell_offset, valid_patch], axis=1)  0.72 us
    ppermute x1, starting transfers between devices, on_device(): late = lax.ppermute(images, 'gz', late)  0.66 us
    pallas_call x1, Pallas kernels, on_device(): call(move, (pltpu.VMEM((3, size, breadth), jnp.float32), pltpu.VMEM((3, S...  0.66 us
  transfers between devices with their start and end apart: 4, of which 1 were waited for; matrix products, arithmetic and copies ran while one was open for 3% of the time, Pallas kernels for 5%

profile of v5, /device:TPU:0, one launch (start us, length us, event | category | flops | bytes accessed | tf_op | source)
XLA Modules:
  0.0 24.3 jit_solution(1398723869123236322)
XLA Ops:
  0.6 3.0 %collective-permute-start.1 = (bf16[1,160,640]{2,1,0:T(8,128)(2,1)}, bf16[1,160,640]{2,1,0:T(8,128)(2,1)S(1)}, u32[]{:S(2)}, u32[]{:S(2)}) collective-permute-start(bf16[1,160,640]{2,1,0:T(8,128)(2,1)} %own_ref.1), channel_id=1, source_target_pairs={{4,0},{0,4},{12,8},{8,12},{20,16},{16,20},{28,24},{24,28},{5,1},{1... | collective-permute-start | bytes 614408 | tf_op jit(solution)/shard_map/ppermute | solution.py:284
  3.6 1.6 %collective-permute-start.2 = (bf16[1,160,640]{2,1,0:T(8,128)(2,1)}, bf16[1,160,640]{2,1,0:T(8,128)(2,1)S(1)}, u32[]{:S(2)}, u32[]{:S(2)}) collective-permute-start(bf16[1,160,640]{2,1,0:T(8,128)(2,1)} %own_ref.1), channel_id=1, source_target_pairs={{8,0},{12,4},{0,8},{4,12},{24,16},{28,20},{16,24},{20,28},{9,1},{1... | collective-permute-start | bytes 614408 | tf_op jit(solution)/shard_map/ppermute | solution.py:286
  5.2 0.7 %collective-permute-start.3 = (bf16[1,160,640]{2,1,0:T(8,128)(2,1)}, bf16[1,160,640]{2,1,0:T(8,128)(2,1)S(1)}, u32[]{:S(2)}, u32[]{:S(2)}) collective-permute-start(bf16[1,160,640]{2,1,0:T(8,128)(2,1)} %own_ref.1), channel_id=1, source_target_pairs={{16,8},{17,9},{18,10},{19,11}} | collective-permute-start | bytes 614408 | tf_op jit(solution)/shard_map/ppermute | solution.py:287
  5.9 0.7 %pad_add_fusion = s32[1,4,4]{2,1,0:T(4,128)S(1)} fusion(s32[1,1,4]{2,1,0:T(1,128)} %param.9, s32[1,1,4]{2,1,0:T(1,128)} %param.8, s32[1,1,4]{2,1,0:T(1,128)} %param.7, s32[1,1,4]{2,1,0:T(1,128)} %param.6), kind=kLoop, calls=%fused_computation | loop fusion | flops 48 | bytes 128 | tf_op jit(solution)/shard_map/concatenate | solution.py:283
  6.6 0.0 copy-start
  6.6 0.6 %collective-permute-start = (s32[1,4,4]{2,1,0:T(4,128)S(1)}, s32[1,4,4]{2,1,0:T(4,128)S(1)}, u32[]{:S(2)}, u32[]{:S(2)}) collective-permute-start(s32[1,4,4]{2,1,0:T(4,128)S(1)} %pad_add_fusion), channel_id=1, source_target_pairs={{4,0},{0,4},{12,8},{8,12},{20,16},{16,20},{28,24},{24,28},{5,1},{1... | collective-permute-start | bytes 200 | tf_op jit(solution)/shard_map/ppermute | solution.py:285
  7.2 0.5 %bank.1 = (bf16[5,160,160]{2,1,0:T(8,128)(2,1)S(1)}, bf16[28,256,256]{2,1,0:T(8,128)(2,1)S(1)}) custom-call(), custom_call_target="tpu_custom_call" | custom-call | flops 1000000000 | bytes 4000000 | tf_op jit(solution)/shard_map/bank/pallas_call | solution.py:289
  7.7 2.5 %collective-permute-done.codes_ref = s32[1,4,4]{2,1,0:T(4,128)S(1)} collective-permute-done((s32[1,4,4]{2,1,0:T(4,128)S(1)}, s32[1,4,4]{2,1,0:T(4,128)S(1)}, u32[]{:S(2)}, u32[]{:S(2)}) %collective-permute-start) | collective-permute-done | bytes 96 | tf_op jit(solution)/shard_map/ppermute | solution.py:285
  10.3 0.0 collective-permute-done.1.first_ref
  10.3 0.7 %move.1 = (f32[3,160,640]{2,1,0:T(8,128)S(1)}, f32[3,8,128]{2,1,0:T(8,128)S(1)}) custom-call(s32[1,4,4]{2,1,0:T(4,128)S(1)} %collective-permute-done.codes_ref, bf16[5,160,160]{2,1,0:T(8,128)(2,1)S(1)} %get-tuple-element.6.rows_ref, bf16[28,256,256]{2,1,0:T(8,128)(2,1)S(1)} %get-tuple-element.7.across_ref, ...), custom_call_target="tpu_custom_call" | custom-call | flops 1000000000 | bytes 4000000 | tf_op jit(solution)/shard_map/move/pallas_call | solution.py:299
  10.9 0.0 collective-permute-done.2.even_ref
  10.9 0.0 collective-permute-done.3.late_ref
  10.9 0.0 copy-done
  11.0 0.6 %correlate.1 = f32[32,128]{1,0:T(8,128)S(1)} custom-call(f32[3,160,640]{2,1,0:T(8,128)S(1)} %get-tuple-element.8.moved_ref, f32[3,8,128]{2,1,0:T(8,128)S(1)} %get-tuple-element.9.aux_ref, bf16[1,160,640]{2,1,0:T(8,128)(2,1)S(1)} %copy-done, bf16[1,160,640]{2,1,0:T(8,128)(2,1)S(1)} %collective-permute-done.2.even_ref, ...), custom_call_target="tpu_custom_call" | custom-call | bytes 4000000 | tf_op jit(solution)/shard_map/correlate/pallas_call | solution.py:309
  11.5 11.8 %all_to_all.11 = f32[32,1,128]{2,1,0:T(1,128)S(1)} all-to-all(f32[32,1,128]{2,1,0:T(1,128)S(1)} %bitcast.4), channel_id=1, replica_groups=mesh['gz'=8,'xy'=4] {'gz','xy'}, dimensions={0} | all-to-all | bytes 32768 | tf_op jit(solution)/shard_map/all_to_all | solution.py:316
  23.3 1.0 %relax.1 = (f32[2,1,1,4]{3,2,1,0:T(1,128)}, f32[2,1,4,8]{3,2,1,0:T(4,128)}) custom-call(f32[32,128]{1,0:T(8,128)S(1)} %bitcast.5), custom_call_target="tpu_custom_call" | custom-call | bytes 4000000 | tf_op jit(solution)/shard_map/relax/pallas_call | solution.py:317
Async XLA Ops:
  0.6 9.6 %collective-permute-start.1 = (bf16[1,160,640]{2,1,0:T(8,128)(2,1)}, bf16[1,160,640]{2,1,0:T(8,128)(2,1)S(1)}, u32[]{:S(2)}, u32[]{:S(2)}) collective-permute-start(bf16[1,160,640]{2,1,0:T(8,128)(2,1)} %own_ref.1), channel_id=1, source_target_pairs={{4,0},{0,4},{12,8},{8,12},{20,16},{16,20},{28,24},{24,28},{5,1},{1... | collective-permute-start | bytes 614408 | tf_op jit(solution)/shard_map/ppermute | solution.py:284
  3.6 7.3 %collective-permute-start.2 = (bf16[1,160,640]{2,1,0:T(8,128)(2,1)}, bf16[1,160,640]{2,1,0:T(8,128)(2,1)S(1)}, u32[]{:S(2)}, u32[]{:S(2)}) collective-permute-start(bf16[1,160,640]{2,1,0:T(8,128)(2,1)} %own_ref.1), channel_id=1, source_target_pairs={{8,0},{12,4},{0,8},{4,12},{24,16},{28,20},{16,24},{20,28},{9,1},{1... | collective-permute-start | bytes 614408 | tf_op jit(solution)/shard_map/ppermute | solution.py:286
  5.2 5.7 %collective-permute-start.3 = (bf16[1,160,640]{2,1,0:T(8,128)(2,1)}, bf16[1,160,640]{2,1,0:T(8,128)(2,1)S(1)}, u32[]{:S(2)}, u32[]{:S(2)}) collective-permute-start(bf16[1,160,640]{2,1,0:T(8,128)(2,1)} %own_ref.1), channel_id=1, source_target_pairs={{16,8},{17,9},{18,10},{19,11}} | collective-permute-start | bytes 614408 | tf_op jit(solution)/shard_map/ppermute | solution.py:287
  6.6 4.3 %copy-start = (bf16[1,160,640]{2,1,0:T(8,128)(2,1)S(1)}, bf16[1,160,640]{2,1,0:T(8,128)(2,1)}, u32[]{:S(2)}) copy-start(bf16[1,160,640]{2,1,0:T(8,128)(2,1)} %own_ref.1) | copy-start | bytes 614404
  6.6 3.7 %collective-permute-start = (s32[1,4,4]{2,1,0:T(4,128)S(1)}, s32[1,4,4]{2,1,0:T(4,128)S(1)}, u32[]{:S(2)}, u32[]{:S(2)}) collective-permute-start(s32[1,4,4]{2,1,0:T(4,128)S(1)} %pad_add_fusion), channel_id=1, source_target_pairs={{4,0},{0,4},{12,8},{8,12},{20,16},{16,20},{28,24},{24,28},{5,1},{1... | collective-permute-start | bytes 200 | tf_op jit(solution)/shard_map/ppermute | solution.py:285

commit v6 on v5

--- a/solution.py
+++ b/solution.py
@@ -99,16 +99,16 @@
     aux_ref[2] = jnp.broadcast_to(shift_x, (SUBLANES, LANES))
 
 
-def move(codes_ref, rows_ref, across_ref, first_ref, moved_ref, aux_ref):
+def copy_codes(codes_ref, again_ref):
+    again_ref[...] = codes_ref[...]
+
+
+def move(peaks, rows_ref, across_ref, image_ref, moved_ref):
     size = PATCH_SIZE
-    cols = codes_ref.shape[2]
-    codes = codes_ref[0]
-    lane = iota((1, cols), 1)
-    peaks = [jnp.sum(jnp.where(lane == j, codes[:1], 0)) for j in range(cols)]
-    splat_weights(codes.astype(jnp.float32), aux_ref)
+    cols = len(peaks)
     downs = []
     for j, base, width, _ in windows(cols, size):
-        window = first_ref[0, :, base : base + width]
+        window = image_ref[0, :, base : base + width]
         down = jnp.dot(rows_ref[peaks[j] // 5], window, preferred_element_type=jnp.float32)
         downs.append(down.astype(jnp.bfloat16))
     for b in range(3):
@@ -123,31 +123,52 @@
             moved_ref[b, :, tile : tile + LANES] = part
 
 
-def correlate(moved_ref, aux_ref, own_ref, even_ref, late_ref, splat_ref, held_ref):
+def peaks_of(codes):
+    lane = iota((1, codes.shape[1]), 1)
+    return [jnp.sum(jnp.where(lane == j, codes[:1], 0)) for j in range(codes.shape[1])]
+
+
+def roles():
+    section = lax.axis_index("gz")
+    fourth = lax.rem(section, 4)
+    turned = (fourth == 1) & (section > 1)
+    return lax.rem(section, 2) == 0, fourth == 0, turned
+
+
+def move_own(codes_ref, rows_ref, across_ref, own_ref, moved_ref, aux_ref):
+    codes = codes_ref[0]
+    peaks = peaks_of(codes)
+    splat_weights(codes.astype(jnp.float32), aux_ref)
+    own, _, _ = roles()
+    pl.when(own)(lambda: move(peaks, rows_ref, across_ref, own_ref, moved_ref))
+
+
+def move_next(beside_ref, along_ref, rows_ref, across_ref, image_ref, _, moved_ref, aux_ref):
+    _, straight, turned = roles()
+    codes = jnp.where(straight, beside_ref[0], along_ref[0])
+    back = (2 * PEAK + 1) ** 2 - 1
+    peaks = [jnp.where(straight, peak, back - peak) for peak in peaks_of(codes)]
+    splat_weights(codes.astype(jnp.float32), aux_ref)
+    pl.when(straight | turned)(lambda: move(peaks, rows_ref, across_ref, image_ref, moved_ref))
+
+
+def lag_sums(moved_ref, second_ref, held_ref):
     size = PATCH_SIZE
-    cols = own_ref.shape[2] // size
-    section = lax.axis_index("gz")
-
-    def stage(second_ref):
-        for tile in range(cols * size // LANES):
-            lanes = slice(tile * LANES, (tile + 1) * LANES)
-            for top in range(0, size, 16):
-                later = second_ref[0, top : top + 16, lanes].astype(jnp.float32)
-                held_ref[tile, SUBLANES + top : SUBLANES + top + 16, :] = later
-                if top == 0:
-                    held_ref[tile, SUBLANES + size : 2 * SUBLANES + size, :] = later[:SUBLANES]
-                if top + 16 == size:
-                    held_ref[tile, :SUBLANES, :] = later[SUBLANES:]
-
-    odd = lax.rem(section, 2) == 1
-    four = lax.rem(section, 4) == 0
-    pl.when(odd)(lambda: stage(own_ref))
-    pl.when(four)(lambda: stage(even_ref))
-    pl.when(jnp.logical_not(jnp.logical_or(odd, four)))(lambda: stage(late_ref))
+    cols = second_ref.shape[2] // size
+    tiles = cols * size // LANES
+    for tile in range(tiles):
+        lanes = slice(tile * LANES, (tile + 1) * LANES)
+        for top in range(0, size, 16):
+            later = second_ref[0, top : top + 16, lanes].astype(jnp.float32)
+            held_ref[tile, SUBLANES + top : SUBLANES + top + 16, :] = later
+            if top == 0:
+                held_ref[tile, SUBLANES + size : 2 * SUBLANES + size, :] = later[:SUBLANES]
+            if top + 16 == size:
+                held_ref[tile, :SUBLANES, :] = later[SUBLANES:]
     sub = iota((SUBLANES, LANES), 0)
     lane = iota((SUBLANES, LANES), 1)
     total = [jnp.zeros((SUBLANES, LANES), jnp.float32) for _ in range(LAGS)]
-    for tile in range(cols * size // LANES):
+    for tile in range(tiles):
         base = tile * LANES
         sums = [None] * LAGS
         for top in range(0, size, SUBLANES):
@@ -165,46 +186,96 @@
             for step in (4, 2, 1):
                 part = part + pltpu.roll(part, step, 0)
             total[k] = total[k] + jnp.where(own, part, 0.0)
-    corr = [jnp.sum(t, axis=1, keepdims=True) / float(size) for t in total]
-    energy = 1.0
-    for value in corr:
-        energy = energy + value * value
+    return [jnp.sum(t, axis=1, keepdims=True) for t in total]
+
+
+def splat_row(corr, aux_ref, cols):
+    size = float(PATCH_SIZE)
+    sub = iota((SUBLANES, LANES), 0)
+    lane = iota((SUBLANES, LANES), 1)
+    squares = [value * value for value in corr]
+    energy = (squares[0] + squares[1]) + (squares[2] + squares[3])
+    energy = energy + ((squares[4] + squares[5]) + (squares[6] + squares[7])) + squares[8]
+    scale = size / (size * size + energy)
     num_y = (corr[6] - corr[0]) + (corr[7] - corr[1]) + (corr[8] - corr[2])
     num_x = (corr[2] - corr[0]) + (corr[5] - corr[3]) + (corr[8] - corr[6])
-    flow_y = aux_ref[1] + num_y / energy
-    flow_x = aux_ref[2] + num_x / energy
+    flow_y = aux_ref[1] + num_y * scale
+    flow_x = aux_ref[2] + num_x * scale
     value = jnp.where(lane < SPLAT, flow_y, jnp.where(lane < 2 * SPLAT, flow_x, 1.0))
     value = aux_ref[0] * value
     value = jnp.where(lane == 3 * SPLAT + sub, flow_y, value)
     value = jnp.where(lane == 3 * SPLAT + cols + sub, flow_x, value)
     row = jnp.sum(jnp.where(sub < cols, value, 0.0), axis=0, keepdims=True)
-    splat_ref[...] = jnp.broadcast_to(row, splat_ref.shape)
+    return jnp.broadcast_to(row, (SUBLANES, LANES))
+
+
+def correlate_own(moved_ref, aux_ref, second_ref, row_ref, held_ref):
+    cols = second_ref.shape[2] // PATCH_SIZE
+    own, _, _ = roles()
+
+    @pl.when(own)
+    def _():
+        row_ref[...] = splat_row(lag_sums(moved_ref, second_ref, held_ref), aux_ref, cols)
+
+    @pl.when(jnp.logical_not(own))
+    def _():
+        row = splat_row([jnp.zeros((SUBLANES, 1), jnp.float32)] * LAGS, aux_ref, cols)
+        row_ref[...] = jnp.where(iota((SUBLANES, LANES), 1) < 3 * SPLAT, 0.0, row)
+
+
+def correlate_next(moved_ref, aux_ref, second_ref, row_ref, splat_ref, held_ref):
+    cols = second_ref.shape[2] // PATCH_SIZE
+    _, straight, turned = roles()
+    some = straight | turned
+    even = lax.rem(iota(splat_ref.shape, 0), 2) == 0
+
+    def spread(row):
+        full = [jnp.broadcast_to(r[:1], splat_ref.shape) for r in (row_ref[...], row)]
+        splat_ref[...] = jnp.where(even, *full)
+
+    @pl.when(some)
+    def _():
+        corr = lag_sums(moved_ref, second_ref, held_ref)
+        corr = [jnp.where(straight, value, other) for value, other in zip(corr, corr[::-1])]
+        spread(splat_row(corr, aux_ref, cols))
+
+    @pl.when(jnp.logical_not(some))
+    def _():
+        spread(jnp.zeros((SUBLANES, LANES), jnp.float32))
 
 
 def relax(strips, splat_ref, flow_ref, out_ref):
-    sections = splat_ref.shape[0] // strips
+    sections = splat_ref.shape[0] // (2 * strips)
     section, strip = lax.axis_index("gz"), lax.axis_index("xy")
     cols = flow_ref.shape[3]
-    home = splat_ref[pl.ds((section ^ 1) * strips + strip, 1), :]
+    fourth = lax.rem(section, 4)
+    after = (fourth == 3) & (section + 2 < sections)
+    worker = jnp.where(fourth == 1, section - 1, jnp.where(after, section + 2, section))
+    second = jnp.where((fourth == 1) | after, 1, 0)
+    home = splat_ref[pl.ds(2 * (worker * strips + strip) + second, 1), :]
     for q in range(2):
         flow_ref[q, 0] = pltpu.roll(home, LANES - 3 * SPLAT - q * cols, 1)[:, :cols]
     lane = iota((sections, LANES), 1)
-    grid = [jnp.zeros((sections, LANES), jnp.float32)] * 3
-    for k in range(-2, 2):
-        at = strip + k
-        first = jnp.minimum(jnp.maximum(at, 0), strips - 1)
-        rows = splat_ref[pl.ds(first, sections, stride=strips), :]
-        base = (k + 1) * BAND
-        inside = (lane >= base) & (lane < base + SPLAT) & (at >= 0) & (at < strips)
-        for q in range(3):
-            moved = pltpu.roll(rows, (base - q * SPLAT) % LANES, 1)
-            grid[q] = grid[q] + jnp.where(inside, moved, 0.0)
-    below = (iota((sections, LANES), 0) ^ 1) < section
-    fixed = []
-    for q in range(2):
-        target = jnp.where(below, grid[q] / (1.0 + grid[2]), 0.0)
-        total = jnp.sum(target, axis=0, keepdims=True)
-        fixed.append(jnp.broadcast_to(total, (SUBLANES, LANES)))
+    place = iota((sections, LANES), 0)
+    which = (place, jnp.where((place & 3) == 0, place + 1, place - 2))
+    sums = [jnp.zeros((sections, LANES), jnp.float32)] * 2
+    for kind in range(2):
+        grid = [jnp.zeros((sections, LANES), jnp.float32)] * 3
+        for k in range(-2, 2):
+            at = strip + k
+            first = jnp.minimum(jnp.maximum(at, 0), strips - 1)
+            rows = splat_ref[pl.ds(2 * first + kind, sections, stride=2 * strips), :]
+            base = (k + 1) * BAND
+            inside = (lane >= base) & (lane < base + SPLAT) & (at >= 0) & (at < strips)
+            for q in range(3):
+                moved = pltpu.roll(rows, (base - q * SPLAT) % LANES, 1)
+                grid[q] = grid[q] + jnp.where(inside, moved, 0.0)
+        inverse = 1.0 / (1.0 + grid[2])
+        below = which[kind] < section
+        sums = [sums[q] + jnp.where(below, grid[q] * inverse, 0.0) for q in range(2)]
+    fixed = [
+        jnp.broadcast_to(jnp.sum(total, axis=0, keepdims=True), (SUBLANES, LANES)) for total in sums
+    ]
     reach = SPRING_STEPS
     fields = {
         o: tuple(
@@ -222,10 +293,13 @@
     }
     rest_zero = math.sqrt(rest_length * rest_length + 1.0)
 
-    def pull(gap_y, gap_x, present):
-        inverse = lax.rsqrt(gap_y * gap_y + gap_x * gap_x + 1.0)
-        tension = (1.0 - rest_zero * inverse) * present
+    def pull(gap_y, gap_x, present, rest):
+        inverse = lax.rsqrt((gap_y * gap_y + 1.0) + gap_x * gap_x)
+        tension = present - rest * inverse
         return tension * gap_y, tension * gap_x
+
+    rest_beside = rest_zero * beside
+    rest_under = {o: rest_zero * present for o, present in under.items()}
 
     now = dict(fields)
     speed = {}
@@ -234,22 +308,21 @@
         down = {}
         for o in range(-reach - 1, reach + 1):
             gap_y = (rest_length + now[o + 1][0]) - now[o][0]
-            down[o] = pull(gap_y, now[o + 1][1] - now[o][1], under[o])
+            down[o] = pull(gap_y, now[o + 1][1] - now[o][1], under[o], rest_under[o])
         later = {}
         for o in range(-reach, reach + 1):
             gap_x = (rest_length + pltpu.roll(now[o][1], 1, 0)) - now[o][1]
-            right = pull(pltpu.roll(now[o][0], 1, 0) - now[o][0], gap_x, beside)
+            right = pull(pltpu.roll(now[o][0], 1, 0) - now[o][0], gap_x, beside, rest_beside)
             moved = []
             for q in range(2):
                 left = pltpu.roll(right[q], SUBLANES - 1, 0)
                 push = (down[o][q] - down[o - 1][q]) + (right[q] - left)
+                rate = (time_step * time_step) * push
                 if step > 0:
-                    push = push + flow_stiff * (fields[o][q] - now[o][q])
-                rate = time_step * push
-                if step > 0:
-                    rate = damping * speed[o, q] + rate
+                    pulled = (time_step * time_step * flow_stiff) * (fields[o][q] - now[o][q])
+                    rate = (damping * speed[o, q] + pulled) + rate
                 speed[o, q] = rate
-                moved.append(now[o][q] + time_step * rate)
+                moved.append(now[o][q] + rate)
             later[o] = tuple(moved)
         now = later
     place = iota((SUBLANES, NODE_COLS), 0) + iota((SUBLANES, NODE_COLS), 1) == NODE_COLS - 1
@@ -267,7 +340,7 @@
         in_specs=in_specs,
         out_specs=jax.tree.map(lambda _: VMEM, out_shape),
         compiler_params=pltpu.CompilerParams(vmem_limit_bytes=24 << 20),
-        cost_estimate=pl.CostEstimate(flops=flops, bytes_accessed=4_000_000, transcendentals=0),
+        cost_estimate=pl.CostEstimate(flops=flops, bytes_accessed=1_000, transcendentals=0),
         **settings,
     )
 
@@ -277,14 +350,17 @@
     cols = breadth // PATCH_SIZE
     sections, strips = lax.axis_size("gz"), lax.axis_size("xy")
     devices = sections * strips
-    pair = [(i ^ 1, i) for i in range(sections)]
-    two = [(i ^ 2, i) for i in range(sections)]
-    late = [(i + 2, i) for i in range(2, sections - 2, 4)]
+    beside = [(i ^ 1, i) for i in range(sections)]
+    along = []
+    for i in range(sections):
+        other = i ^ 2 if i % 2 == 0 else i + 2 if i % 4 == 3 else i - 2
+        for r in range(strips):
+            mate = other * strips + r if 0 <= other < sections else i * strips + (r ^ 1)
+            along.append((mate, i * strips + r))
     codes = jnp.concatenate([peak_code, cell_block, cell_offset, valid_patch], axis=1)
-    first = lax.ppermute(images, "gz", pair)
-    codes = lax.ppermute(codes, "gz", pair)
-    even = lax.ppermute(images, "gz", two)
-    late = lax.ppermute(images, "gz", late)
+    image_beside = lax.ppermute(images, "gz", beside)
+    image_along = lax.ppermute(images, ("gz", "xy"), along)
+    codes_along = lax.ppermute(codes, ("gz", "xy"), along)
     width = max(w for _, _, w, _ in windows(cols, PATCH_SIZE))
     rows, across = call(
         bank,
@@ -293,26 +369,36 @@
             pltpu.VMEM((cols * (2 * PEAK + 3), width, width), jnp.bfloat16),
         ),
         [],
-        flops=1_000_000_000,
+        flops=1_000,
         name="bank",
     )()
+    again = call(copy_codes, pltpu.VMEM(codes.shape, codes.dtype), [VMEM], name="copy_codes")
+    codes_beside = lax.ppermute(again(codes), "gz", beside)
+    moved_shape = (
+        pltpu.VMEM((3, size, breadth), jnp.float32),
+        pltpu.VMEM((3, SUBLANES, LANES), jnp.float32),
+    )
+    held = [pltpu.VMEM((breadth // LANES, size + 2 * SUBLANES, LANES), jnp.float32)]
     moved, aux = call(
-        move,
-        (
-            pltpu.VMEM((3, size, breadth), jnp.float32),
-            pltpu.VMEM((3, SUBLANES, LANES), jnp.float32),
-        ),
+        move_own, moved_shape, [VMEM] * 4, flops=1_000, name="move_own"
+    )(codes, rows, across, images)
+    row = call(
+        correlate_own,
+        pltpu.VMEM((SUBLANES, LANES), jnp.float32),
+        [VMEM] * 3,
+        scratch_shapes=held,
+        name="correlate_own",
+    )(moved, aux, image_beside)
+    moved, aux = call(
+        move_next, moved_shape, [VMEM] * 6, flops=1_000, name="move_next"
+    )(codes_beside, codes_along, rows, across, image_beside, row)
+    splat = call(
+        correlate_next,
+        pltpu.VMEM((2 * devices, LANES), jnp.float32),
         [VMEM] * 4,
-        flops=1_000_000_000,
-        name="move",
-    )(codes, rows, across, first)
-    splat = call(
-        correlate,
-        pltpu.VMEM((devices, LANES), jnp.float32),
-        [VMEM] * 5,
-        scratch_shapes=[pltpu.VMEM((breadth // LANES, size + 2 * SUBLANES, LANES), jnp.float32)],
-        name="correlate",
-    )(moved, aux, images, even, late)
+        scratch_shapes=held,
+        name="correlate_next",
+    )(moved, aux, image_along, row)
     gathered = lax.all_to_all(splat, ("gz", "xy"), 0, 0, tiled=True)
     flow, node_shift = call(
         functools.partial(relax, strips),

time: 24.5 us -> 23.8 us (0.971)
  Pallas kernels: 2.73 us -> 3.98 us
  waiting for transfers between devices: 2.56 us -> 1.31 us
  local copies, waits for them, and re-layouts: 0.01 us -> 0.93 us
  blocking collectives: 11.8 us -> 11 us
  starting transfers between devices: 5.84 us -> 5.09 us
    pallas_call x2 -> x5, Pallas kernels: 1.24 us -> 2.5 us  [the longest x1 0.69 us: on_device(): call(move_next, moved_shape, [VMEM] * 6, flops=1000, name='move_next')]
    ppermute x4, waiting for transfers between devices: 2.56 us -> 1.31 us  [the longest x1 0.51 us: on_device(): codes_beside = lax.ppermute(again(codes), 'gz', beside)]
    unnamed x2, local copies, waits for them, and re-layouts: 0.01 us -> 0.93 us
    all_to_all x1, blocking collectives: 11.8 us -> 11 us  [on_device(): gathered = lax.all_to_all(splat, ('gz', 'xy'), 0, 0, tiled=True)]
    ppermute x4, starting transfers between devices: 5.84 us -> 5.09 us  [the longest x1 3 us: on_device(): image_beside = lax.ppermute(images, 'gz', beside)]
  transfers between devices with their start and end apart: 4 -> 4, of which waited for: 1 -> 3; matrix products, arithmetic and copies ran while one was open for 3% -> 3% of each run, Pallas kernels for 5% -> 10%
where the time goes in v6:
time: 23.8 us; the launch traced here: 23.7 us
  blocking collectives  11 us (46%)
  starting transfers between devices  5.09 us (21%)
  Pallas kernels  3.98 us (17%)
  waiting for transfers between devices  1.31 us (6%)
  local copies, waits for them, and re-layouts  0.93 us (4%)
  other arithmetic  0.71 us (3%)
  between operations  0.68 us (3%)
    all_to_all x1, blocking collectives, on_device(): gathered = lax.all_to_all(splat, ('gz', 'xy'), 0, 0, tiled=True)  11 us
    ppermute x1, starting transfers between devices, on_device(): image_beside = lax.ppermute(images, 'gz', beside)  3 us
    ppermute x1, starting transfers between devices, on_device(): image_along = lax.ppermute(images, ('gz', 'xy'), along)  1.58 us
    pallas_call x1, Pallas kernels, on_device(): call(functools.partial(relax, strips), (jax.ShapeDtypeStruct((2, 1, 1, co...  0.98 us
    unnamed x2, local copies, waits for them, and re-layouts  0.93 us
    concatenate x1, other arithmetic, on_device(): jnp.concatenate([peak_code, cell_block, cell_offset, valid_patch], axis=1)  0.71 us
    pallas_call x1, Pallas kernels, on_device(): call(move_next, moved_shape, [VMEM] * 6, flops=1000, name='move_next')  0.69 us
    pallas_call x1, Pallas kernels, on_device(): call(move_own, moved_shape, [VMEM] * 4, flops=1000, name='move_own')  0.68 us
  transfers between devices with their start and end apart: 4, of which 3 were waited for; matrix products, arithmetic and copies ran while one was open for 3% of the time, Pallas kernels for 10%

profile of v6, /device:TPU:0, one launch (start us, length us, event | category | flops | bytes accessed | tf_op | source)
XLA Modules:
  0.0 23.7 jit_solution(6231147835794863321)
XLA Ops:
  0.6 3.0 %collective-permute-start.2 = (bf16[1,160,640]{2,1,0:T(8,128)(2,1)}, bf16[1,160,640]{2,1,0:T(8,128)(2,1)S(1)}, u32[]{:S(2)}, u32[]{:S(2)}) collective-permute-start(bf16[1,160,640]{2,1,0:T(8,128)(2,1)} %own_ref.1), channel_id=1, source_target_pairs={{4,0},{0,4},{12,8},{8,12},{20,16},{16,20},{28,24},{24,28},{5,1},{1... | collective-permute-start | bytes 614408 | tf_op jit(solution)/shard_map/ppermute | solution.py:361
  3.6 1.6 %collective-permute-start.3 = (bf16[1,160,640]{2,1,0:T(8,128)(2,1)}, bf16[1,160,640]{2,1,0:T(8,128)(2,1)S(1)}, u32[]{:S(2)}, u32[]{:S(2)}) collective-permute-start(bf16[1,160,640]{2,1,0:T(8,128)(2,1)} %own_ref.1), channel_id=1, source_target_pairs={{8,0},{9,1},{10,2},{11,3},{5,4},{4,5},{7,6},{6,7},{0,8},{1,9},{2,1... | collective-permute-start | bytes 614408 | tf_op jit(solution)/shard_map/ppermute | solution.py:362
  5.2 0.7 %pad_add_fusion.codes_ref = s32[1,4,4]{2,1,0:T(4,128)S(1)} fusion(s32[1,1,4]{2,1,0:T(1,128)} %param.9, s32[1,1,4]{2,1,0:T(1,128)} %param.8, s32[1,1,4]{2,1,0:T(1,128)} %param.7, s32[1,1,4]{2,1,0:T(1,128)} %param.6), kind=kLoop, calls=%fused_computation | loop fusion | flops 48 | bytes 128 | tf_op jit(solution)/shard_map/concatenate | solution.py:360
  5.9 0.5 %collective-permute-start.1 = (s32[1,4,4]{2,1,0:T(4,128)S(1)}, s32[1,4,4]{2,1,0:T(4,128)S(1)}, u32[]{:S(2)}, u32[]{:S(2)}) collective-permute-start(s32[1,4,4]{2,1,0:T(4,128)S(1)} %pad_add_fusion.codes_ref), channel_id=1, source_target_pairs={{8,0},{9,1},{10,2},{11,3},{5,4},{4,5},{7,6},{6,7},{0,8},{1,9},{2,1... | collective-permute-start | bytes 200 | tf_op jit(solution)/shard_map/ppermute | solution.py:363
  6.4 0.0 collective-permute-start
  6.4 0.5 %bank.1 = (bf16[5,160,160]{2,1,0:T(8,128)(2,1)S(1)}, bf16[28,256,256]{2,1,0:T(8,128)(2,1)S(1)}) custom-call(), custom_call_target="tpu_custom_call" | custom-call | flops 1000 | bytes 1000 | tf_op jit(solution)/shard_map/bank/pallas_call | solution.py:365
  6.9 0.0 copy-start
  7.0 0.9 %copy-done = bf16[1,160,640]{2,1,0:T(8,128)(2,1)S(1)} copy-done((bf16[1,160,640]{2,1,0:T(8,128)(2,1)S(1)}, bf16[1,160,640]{2,1,0:T(8,128)(2,1)}, u32[]{:S(2)}) %copy-start) | copy-done | bytes 204824
  7.9 0.7 %move_own.1 = (f32[3,160,640]{2,1,0:T(8,128)S(1)}, f32[3,8,128]{2,1,0:T(8,128)S(1)}) custom-call(s32[1,4,4]{2,1,0:T(4,128)S(1)} %pad_add_fusion.codes_ref, bf16[5,160,160]{2,1,0:T(8,128)(2,1)S(1)} %get-tuple-element.8.rows_ref, bf16[28,256,256]{2,1,0:T(8,128)(2,1)S(1)} %get-tuple-element.9.across_ref, bf16[1,160,640]{2,1,0:T(8,128)(2,1)S(1)} %copy-done), custom_call_target="tpu_custom_call" | custom-call | flops 1000 | bytes 1000 | tf_op jit(solution)/shard_map/move_own/pallas_call | solution.py:382
  8.6 0.4 %collective-permute-done.2.second_ref.image_ref = bf16[1,160,640]{2,1,0:T(8,128)(2,1)S(1)} collective-permute-done((bf16[1,160,640]{2,1,0:T(8,128)(2,1)}, bf16[1,160,640]{2,1,0:T(8,128)(2,1)S(1)}, u32[]{:S(2)}, u32[]{:S(2)}) %collective-permute-start.2) | collective-permute-done | bytes 204832 | tf_op jit(solution)/shard_map/ppermute | solution.py:361
  8.9 0.6 %correlate_own.1._.row_ref = f32[8,128]{1,0:T(8,128)S(1)} custom-call(f32[3,160,640]{2,1,0:T(8,128)S(1)} %get-tuple-element.10.moved_ref, f32[3,8,128]{2,1,0:T(8,128)S(1)} %get-tuple-element.11.aux_ref, bf16[1,160,640]{2,1,0:T(8,128)(2,1)S(1)} %collective-permute-done.2.second_ref.image_ref), custom_call_target="tpu_custom_call" | custom-call | bytes 1000 | tf_op jit(solution)/shard_map/correlate_own/pallas_call | solution.py:385
  9.5 0.5 %collective-permute-done.beside_ref = s32[1,4,4]{2,1,0:T(4,128)S(1)} collective-permute-done((s32[1,4,4]{2,1,0:T(4,128)S(1)}, s32[1,4,4]{2,1,0:T(4,128)S(1)}, u32[]{:S(2)}, u32[]{:S(2)}) %collective-permute-start) | collective-permute-done | bytes 96 | tf_op jit(solution)/shard_map/ppermute | solution.py:376
  10.0 0.4 %collective-permute-done.1.along_ref = s32[1,4,4]{2,1,0:T(4,128)S(1)} collective-permute-done((s32[1,4,4]{2,1,0:T(4,128)S(1)}, s32[1,4,4]{2,1,0:T(4,128)S(1)}, u32[]{:S(2)}, u32[]{:S(2)}) %collective-permute-start.1) | collective-permute-done | bytes 96 | tf_op jit(solution)/shard_map/ppermute | solution.py:363
  10.4 0.7 %move_next.1 = (f32[3,160,640]{2,1,0:T(8,128)S(1)}, f32[3,8,128]{2,1,0:T(8,128)S(1)}) custom-call(s32[1,4,4]{2,1,0:T(4,128)S(1)} %collective-permute-done.beside_ref, s32[1,4,4]{2,1,0:T(4,128)S(1)} %collective-permute-done.1.along_ref, bf16[5,160,160]{2,1,0:T(8,128)(2,1)S(1)} %get-tuple-element.8.rows_ref, ...), custom_call_target="tpu_custom_call" | custom-call | flops 1000 | bytes 1000 | tf_op jit(solution)/shard_map/move_next/pallas_call | solution.py:392
  11.1 0.0 collective-permute-done.3.second_ref
  11.1 0.6 %correlate_next.1 = f32[64,128]{1,0:T(8,128)S(1)} custom-call(f32[3,160,640]{2,1,0:T(8,128)S(1)} %get-tuple-element.12.moved_ref, f32[3,8,128]{2,1,0:T(8,128)S(1)} %get-tuple-element.13.aux_ref, bf16[1,160,640]{2,1,0:T(8,128)(2,1)S(1)} %collective-permute-done.3.second_ref, f32[8,128]{1,0:T(8,128)S(1)} %correlate_own.1._.row_ref), custom_call_target="tpu_custom_call" | custom-call | bytes 1000 | tf_op jit(solution)/shard_map/correlate_next/pallas_call | solution.py:395
  11.7 11.0 %all_to_all.11 = f32[32,2,128]{2,1,0:T(2,128)S(1)} all-to-all(f32[32,2,128]{2,1,0:T(2,128)S(1)} %bitcast.2), channel_id=1, replica_groups=mesh['gz'=8,'xy'=4] {'gz','xy'}, dimensions={0} | all-to-all | bytes 65536 | tf_op jit(solution)/shard_map/all_to_all | solution.py:402
  22.7 1.0 %relax.1 = (f32[2,1,1,4]{3,2,1,0:T(1,128)}, f32[2,1,4,8]{3,2,1,0:T(4,128)}) custom-call(f32[64,128]{1,0:T(8,128)S(1)} %bitcast.3), custom_call_target="tpu_custom_call" | custom-call | bytes 1000 | tf_op jit(solution)/shard_map/relax/pallas_call | solution.py:403
  (1 shorter events, 0.0 us)
Async XLA Ops:
  0.6 8.3 %collective-permute-start.2 = (bf16[1,160,640]{2,1,0:T(8,128)(2,1)}, bf16[1,160,640]{2,1,0:T(8,128)(2,1)S(1)}, u32[]{:S(2)}, u32[]{:S(2)}) collective-permute-start(bf16[1,160,640]{2,1,0:T(8,128)(2,1)} %own_ref.1), channel_id=1, source_target_pairs={{4,0},{0,4},{12,8},{8,12},{20,16},{16,20},{28,24},{24,28},{5,1},{1... | collective-permute-start | bytes 614408 | tf_op jit(solution)/shard_map/ppermute | solution.py:361
  3.6 7.5 %collective-permute-start.3 = (bf16[1,160,640]{2,1,0:T(8,128)(2,1)}, bf16[1,160,640]{2,1,0:T(8,128)(2,1)S(1)}, u32[]{:S(2)}, u32[]{:S(2)}) collective-permute-start(bf16[1,160,640]{2,1,0:T(8,128)(2,1)} %own_ref.1), channel_id=1, source_target_pairs={{8,0},{9,1},{10,2},{11,3},{5,4},{4,5},{7,6},{6,7},{0,8},{1,9},{2,1... | collective-permute-start | bytes 614408 | tf_op jit(solution)/shard_map/ppermute | solution.py:362
  5.9 4.5 %collective-permute-start.1 = (s32[1,4,4]{2,1,0:T(4,128)S(1)}, s32[1,4,4]{2,1,0:T(4,128)S(1)}, u32[]{:S(2)}, u32[]{:S(2)}) collective-permute-start(s32[1,4,4]{2,1,0:T(4,128)S(1)} %pad_add_fusion.codes_ref), channel_id=1, source_target_pairs={{8,0},{9,1},{10,2},{11,3},{5,4},{4,5},{7,6},{6,7},{0,8},{1,9},{2,1... | collective-permute-start | bytes 200 | tf_op jit(solution)/shard_map/ppermute | solution.py:363
  6.4 3.6 %collective-permute-start = (s32[1,4,4]{2,1,0:T(4,128)S(1)}, s32[1,4,4]{2,1,0:T(4,128)S(1)}, u32[]{:S(2)}, u32[]{:S(2)}) collective-permute-start(s32[1,4,4]{2,1,0:T(4,128)S(1)} %copy_codes.1), channel_id=1, source_target_pairs={{4,0},{0,4},{12,8},{8,12},{20,16},{16,20},{28,24},{24,28},{5,1},{1... | collective-permute-start | bytes 200 | tf_op jit(solution)/shard_map/ppermute | solution.py:376
  6.9 0.9 %copy-start = (bf16[1,160,640]{2,1,0:T(8,128)(2,1)S(1)}, bf16[1,160,640]{2,1,0:T(8,128)(2,1)}, u32[]{:S(2)}) copy-start(bf16[1,160,640]{2,1,0:T(8,128)(2,1)} %own_ref.1) | copy-start | bytes 614404

commit v7 on v6

--- a/solution.py
+++ b/solution.py
@@ -103,7 +103,7 @@
     again_ref[...] = codes_ref[...]
 
 
-def move(peaks, rows_ref, across_ref, image_ref, moved_ref):
+def move(peaks, rows_ref, across_ref, image_ref, moved_ref, ready=None):
     size = PATCH_SIZE
     cols = len(peaks)
     downs = []
@@ -111,16 +111,24 @@
         window = image_ref[0, :, base : base + width]
         down = jnp.dot(rows_ref[peaks[j] // 5], window, preferred_element_type=jnp.float32)
         downs.append(down.astype(jnp.bfloat16))
-    for b in range(3):
-        kept = {}
-        for j, base, width, _ in windows(cols, size):
+    kept = [{} for _ in range(3)]
+    tiles = cols * size // LANES
+    done = 0
+    for j, base, width, _ in windows(cols, size):
+        for b in range(3):
             pick = across_ref[j * (2 * PEAK + 3) + peaks[j] % 5 + b]
             across = jnp.dot(downs[j], pick, preferred_element_type=jnp.float32)
-            for tile in range(0, width, LANES):
-                part = across[:, tile : tile + LANES]
-                kept[base + tile] = kept[base + tile] + part if base + tile in kept else part
-        for tile, part in kept.items():
-            moved_ref[b, :, tile : tile + LANES] = part
+            for k in range(width // LANES):
+                tile = base // LANES + k
+                part = across[:, k * LANES : (k + 1) * LANES]
+                kept[b][tile] = kept[b][tile] + part if tile in kept[b] else part
+        until = (j + 1) * size // LANES if j + 1 < cols else tiles
+        for tile in range(done, until):
+            for b in range(3):
+                moved_ref[b, :, tile * LANES : (tile + 1) * LANES] = kept[b].pop(tile)
+            if ready is not None:
+                ready(tile)
+        done = until
 
 
 def peaks_of(codes):
@@ -143,20 +151,9 @@
     pl.when(own)(lambda: move(peaks, rows_ref, across_ref, own_ref, moved_ref))
 
 
-def move_next(beside_ref, along_ref, rows_ref, across_ref, image_ref, _, moved_ref, aux_ref):
-    _, straight, turned = roles()
-    codes = jnp.where(straight, beside_ref[0], along_ref[0])
-    back = (2 * PEAK + 1) ** 2 - 1
-    peaks = [jnp.where(straight, peak, back - peak) for peak in peaks_of(codes)]
-    splat_weights(codes.astype(jnp.float32), aux_ref)
-    pl.when(straight | turned)(lambda: move(peaks, rows_ref, across_ref, image_ref, moved_ref))
-
-
-def lag_sums(moved_ref, second_ref, held_ref):
+def stage(second_ref, held_ref):
     size = PATCH_SIZE
-    cols = second_ref.shape[2] // size
-    tiles = cols * size // LANES
-    for tile in range(tiles):
+    for tile in range(second_ref.shape[2] // LANES):
         lanes = slice(tile * LANES, (tile + 1) * LANES)
         for top in range(0, size, 16):
             later = second_ref[0, top : top + 16, lanes].astype(jnp.float32)
@@ -165,27 +162,36 @@
                 held_ref[tile, SUBLANES + size : 2 * SUBLANES + size, :] = later[:SUBLANES]
             if top + 16 == size:
                 held_ref[tile, :SUBLANES, :] = later[SUBLANES:]
+
+
+def add_tile(tile, moved_ref, held_ref, total):
+    size = PATCH_SIZE
     sub = iota((SUBLANES, LANES), 0)
     lane = iota((SUBLANES, LANES), 1)
-    total = [jnp.zeros((SUBLANES, LANES), jnp.float32) for _ in range(LAGS)]
-    for tile in range(tiles):
-        base = tile * LANES
-        sums = [None] * LAGS
-        for top in range(0, size, SUBLANES):
-            first = [moved_ref[b, top : top + SUBLANES, base : base + LANES] for b in range(3)]
-            for a in range(3):
-                start = SUBLANES + top + a - 1
-                later = held_ref[tile, start : start + SUBLANES, :]
-                for b in range(3):
-                    part = first[b] * later
-                    k = a * 3 + b
-                    sums[k] = part if sums[k] is None else sums[k] + part
-        own = (lane + base >= sub * size) & (lane + base < (sub + 1) * size)
-        for k in range(LAGS):
-            part = sums[k]
-            for step in (4, 2, 1):
-                part = part + pltpu.roll(part, step, 0)
-            total[k] = total[k] + jnp.where(own, part, 0.0)
+    base = tile * LANES
+    sums = [None] * LAGS
+    for top in range(0, size, SUBLANES):
+        first = [moved_ref[b, top : top + SUBLANES, base : base + LANES] for b in range(3)]
+        for a in range(3):
+            start = SUBLANES + top + a - 1
+            later = held_ref[tile, start : start + SUBLANES, :]
+            for b in range(3):
+                part = first[b] * later
+                k = a * 3 + b
+                sums[k] = part if sums[k] is None else sums[k] + part
+    own = (lane + base >= sub * size) & (lane + base < (sub + 1) * size)
+    for k in range(LAGS):
+        part = sums[k]
+        for step in (4, 2, 1):
+            part = part + pltpu.roll(part, step, 0)
+        total[k] = total[k] + jnp.where(own, part, 0.0)
+
+
+def no_sums():
+    return [jnp.zeros((SUBLANES, LANES), jnp.float32) for _ in range(LAGS)]
+
+
+def over_lanes(total):
     return [jnp.sum(t, axis=1, keepdims=True) for t in total]
 
 
@@ -215,7 +221,11 @@
 
     @pl.when(own)
     def _():
-        row_ref[...] = splat_row(lag_sums(moved_ref, second_ref, held_ref), aux_ref, cols)
+        stage(second_ref, held_ref)
+        total = no_sums()
+        for tile in range(second_ref.shape[2] // LANES):
+            add_tile(tile, moved_ref, held_ref, total)
+        row_ref[...] = splat_row(over_lanes(total), aux_ref, cols)
 
     @pl.when(jnp.logical_not(own))
     def _():
@@ -223,8 +233,10 @@
         row_ref[...] = jnp.where(iota((SUBLANES, LANES), 1) < 3 * SPLAT, 0.0, row)
 
 
-def correlate_next(moved_ref, aux_ref, second_ref, row_ref, splat_ref, held_ref):
-    cols = second_ref.shape[2] // PATCH_SIZE
+def neighbours(
+    beside_ref, along_ref, rows_ref, across_ref, image_ref, second_ref, row_ref,
+    splat_ref, moved_ref, held_ref, aux_ref,
+):
     _, straight, turned = roles()
     some = straight | turned
     even = lax.rem(iota(splat_ref.shape, 0), 2) == 0
@@ -235,9 +247,19 @@
 
     @pl.when(some)
     def _():
-        corr = lag_sums(moved_ref, second_ref, held_ref)
+        codes = jnp.where(straight, beside_ref[0], along_ref[0])
+        back = (2 * PEAK + 1) ** 2 - 1
+        peaks = [jnp.where(straight, peak, back - peak) for peak in peaks_of(codes)]
+        splat_weights(codes.astype(jnp.float32), aux_ref)
+        stage(second_ref, held_ref)
+        total = no_sums()
+        move(
+            peaks, rows_ref, across_ref, image_ref, moved_ref,
+            lambda tile: add_tile(tile, moved_ref, held_ref, total),
+        )
+        corr = over_lanes(total)
         corr = [jnp.where(straight, value, other) for value, other in zip(corr, corr[::-1])]
-        spread(splat_row(corr, aux_ref, cols))
+        spread(splat_row(corr, aux_ref, len(peaks)))
 
     @pl.when(jnp.logical_not(some))
     def _():
@@ -350,17 +372,26 @@
     cols = breadth // PATCH_SIZE
     sections, strips = lax.axis_size("gz"), lax.axis_size("xy")
     devices = sections * strips
-    beside = [(i ^ 1, i) for i in range(sections)]
-    along = []
-    for i in range(sections):
-        other = i ^ 2 if i % 2 == 0 else i + 2 if i % 4 == 3 else i - 2
-        for r in range(strips):
-            mate = other * strips + r if 0 <= other < sections else i * strips + (r ^ 1)
-            along.append((mate, i * strips + r))
+
+    def pairing(other):
+        route = []
+        for i in range(sections):
+            j = other(i)
+            for r in range(strips):
+                mate = j * strips + r if 0 <= j < sections else i * strips + (r ^ 1)
+                route.append((mate, i * strips + r))
+        return route
+
+    beside = pairing(lambda i: i ^ 1)
+    along = pairing(lambda i: i ^ 2 if i % 2 == 0 else i + 2 if i % 4 == 3 else i - 2)
+    codes_routes = (
+        pairing(lambda i: i ^ 1 if i % 4 < 2 else -1),
+        pairing(lambda i: -1 if i % 2 == 0 else i + 2 if i % 4 == 3 else i - 2),
+    )
     codes = jnp.concatenate([peak_code, cell_block, cell_offset, valid_patch], axis=1)
-    image_beside = lax.ppermute(images, "gz", beside)
+    image_beside = lax.ppermute(images, ("gz", "xy"), beside)
     image_along = lax.ppermute(images, ("gz", "xy"), along)
-    codes_along = lax.ppermute(codes, ("gz", "xy"), along)
+    codes_along = lax.ppermute(codes, ("gz", "xy"), codes_routes[1])
     width = max(w for _, _, w, _ in windows(cols, PATCH_SIZE))
     rows, across = call(
         bank,
@@ -373,7 +404,7 @@
         name="bank",
     )()
     again = call(copy_codes, pltpu.VMEM(codes.shape, codes.dtype), [VMEM], name="copy_codes")
-    codes_beside = lax.ppermute(again(codes), "gz", beside)
+    codes_beside = lax.ppermute(again(codes), ("gz", "xy"), codes_routes[0])
     moved_shape = (
         pltpu.VMEM((3, size, breadth), jnp.float32),
         pltpu.VMEM((3, SUBLANES, LANES), jnp.float32),
@@ -389,16 +420,15 @@
         scratch_shapes=held,
         name="correlate_own",
     )(moved, aux, image_beside)
-    moved, aux = call(
-        move_next, moved_shape, [VMEM] * 6, flops=1_000, name="move_next"
-    )(codes_beside, codes_along, rows, across, image_beside, row)
     splat = call(
-        correlate_next,
+        neighbours,
         pltpu.VMEM((2 * devices, LANES), jnp.float32),
-        [VMEM] * 4,
-        scratch_shapes=held,
-        name="correlate_next",
-    )(moved, aux, image_along, row)
+        [VMEM] * 7,
+        scratch_shapes=[pltpu.VMEM(shape.shape, jnp.float32) for shape in moved_shape[:1]]
+        + held
+        + [pltpu.VMEM((3, SUBLANES, LANES), jnp.float32)],
+        name="neighbours",
+    )(codes_beside, codes_along, rows, across, image_beside, image_along, row)
     gathered = lax.all_to_all(splat, ("gz", "xy"), 0, 0, tiled=True)
     flow, node_shift = call(
         functools.partial(relax, strips),

time: 23.8 us -> 23.5 us (0.987)
  Pallas kernels: 3.98 us -> 3.6 us
  starting transfers between devices: 5.09 us -> 4.71 us
  waiting for transfers between devices: 1.31 us -> 1.63 us
    ppermute x1, waiting for transfers between devices: 0.01 us -> 0.72 us  [on_device(): image_along = lax.ppermute(images, ('gz', 'xy'), along)]
    ppermute x3, waiting for transfers between devices: 1.31 us -> 0.91 us  [the longest x1 0.73 us: on_device(): image_beside = lax.ppermute(images, ('gz', 'xy'), beside)]
    ppermute x3, starting transfers between devices: 3.51 us -> 3.14 us  [the longest x1 3 us: on_device(): image_beside = lax.ppermute(images, ('gz', 'xy'), beside)]
    pallas_call x3 -> x2, Pallas kernels: 1.27 us -> 0.9 us  [the longest x1 0.9 us: on_device(): call(neighbours, pltpu.VMEM((2 * devices, LANES), jnp.float32), [VMEM] *...]
  transfers between devices with their start and end apart: 4 -> 4, of which waited for: 3 -> 3; matrix products, arithmetic and copies ran while one was open for 3% -> 3% of each run, Pallas kernels for 10% -> 7%
where the time goes in v7:
time: 23.5 us; the launch traced here: 23.4 us
  blocking collectives  11.1 us (47%)
  starting transfers between devices  4.71 us (20%)
  Pallas kernels  3.6 us (15%)
  waiting for transfers between devices  1.63 us (7%)
  local copies, waits for them, and re-layouts  0.93 us (4%)
  other arithmetic  0.71 us (3%)
  between operations  0.69 us (3%)
    all_to_all x1, blocking collectives, on_device(): gathered = lax.all_to_all(splat, ('gz', 'xy'), 0, 0, tiled=True)  11.1 us
    ppermute x1, starting transfers between devices, on_device(): image_beside = lax.ppermute(images, ('gz', 'xy'), beside)  3 us
    ppermute x1, starting transfers between devices, on_device(): image_along = lax.ppermute(images, ('gz', 'xy'), along)  1.58 us
    pallas_call x1, Pallas kernels, on_device(): call(functools.partial(relax, strips), (jax.ShapeDtypeStruct((2, 1, 1, co...  0.98 us
    unnamed x2, local copies, waits for them, and re-layouts  0.93 us
    pallas_call x1, Pallas kernels, on_device(): call(neighbours, pltpu.VMEM((2 * devices, LANES), jnp.float32), [VMEM] *...  0.9 us
    ppermute x1, waiting for transfers between devices, on_device(): image_beside = lax.ppermute(images, ('gz', 'xy'), beside)  0.73 us
    ppermute x1, waiting for transfers between devices, on_device(): image_along = lax.ppermute(images, ('gz', 'xy'), along)  0.72 us
  transfers between devices with their start and end apart: 4, of which 3 were waited for; matrix products, arithmetic and copies ran while one was open for 3% of the time, Pallas kernels for 7%

profile of v7, /device:TPU:0, one launch (start us, length us, event | category | flops | bytes accessed | tf_op | source)
XLA Modules:
  0.0 23.4 jit_solution(1586950075354063617)
XLA Ops:
  0.6 3.0 %collective-permute-start.2 = (bf16[1,160,640]{2,1,0:T(8,128)(2,1)}, bf16[1,160,640]{2,1,0:T(8,128)(2,1)S(1)}, u32[]{:S(2)}, u32[]{:S(2)}) collective-permute-start(bf16[1,160,640]{2,1,0:T(8,128)(2,1)} %own_ref.1), channel_id=1, source_target_pairs={{4,0},{5,1},{6,2},{7,3},{0,4},{1,5},{2,6},{3,7},{12,8},{13,9},{14,... | collective-permute-start | bytes 614408 | tf_op jit(solution)/shard_map/ppermute | solution.py:392
  3.6 1.6 %collective-permute-start.3 = (bf16[1,160,640]{2,1,0:T(8,128)(2,1)}, bf16[1,160,640]{2,1,0:T(8,128)(2,1)S(1)}, u32[]{:S(2)}, u32[]{:S(2)}) collective-permute-start(bf16[1,160,640]{2,1,0:T(8,128)(2,1)} %own_ref.1), channel_id=1, source_target_pairs={{8,0},{9,1},{10,2},{11,3},{5,4},{4,5},{7,6},{6,7},{0,8},{1,9},{2,1... | collective-permute-start | bytes 614408 | tf_op jit(solution)/shard_map/ppermute | solution.py:393
  5.2 0.7 %pad_add_fusion.codes_ref = s32[1,4,4]{2,1,0:T(4,128)S(1)} fusion(s32[1,1,4]{2,1,0:T(1,128)} %param.9, s32[1,1,4]{2,1,0:T(1,128)} %param.8, s32[1,1,4]{2,1,0:T(1,128)} %param.7, s32[1,1,4]{2,1,0:T(1,128)} %param.6), kind=kLoop, calls=%fused_computation | loop fusion | flops 48 | bytes 128 | tf_op jit(solution)/shard_map/concatenate | solution.py:391
  5.9 0.1 collective-permute-start.1
  6.0 0.1 collective-permute-start
  6.1 0.5 %bank.1 = (bf16[5,160,160]{2,1,0:T(8,128)(2,1)S(1)}, bf16[28,256,256]{2,1,0:T(8,128)(2,1)S(1)}) custom-call(), custom_call_target="tpu_custom_call" | custom-call | flops 1000 | bytes 1000 | tf_op jit(solution)/shard_map/bank/pallas_call | solution.py:396
  6.6 0.0 copy-start
  6.6 0.9 %copy-done = bf16[1,160,640]{2,1,0:T(8,128)(2,1)S(1)} copy-done((bf16[1,160,640]{2,1,0:T(8,128)(2,1)S(1)}, bf16[1,160,640]{2,1,0:T(8,128)(2,1)}, u32[]{:S(2)}) %copy-start) | copy-done | bytes 204824
  7.5 0.7 %move_own.1 = (f32[3,160,640]{2,1,0:T(8,128)S(1)}, f32[3,8,128]{2,1,0:T(8,128)S(1)}) custom-call(s32[1,4,4]{2,1,0:T(4,128)S(1)} %pad_add_fusion.codes_ref, bf16[5,160,160]{2,1,0:T(8,128)(2,1)S(1)} %get-tuple-element.6.rows_ref, bf16[28,256,256]{2,1,0:T(8,128)(2,1)S(1)} %get-tuple-element.7.across_ref, bf16[1,160,640]{2,1,0:T(8,128)(2,1)S(1)} %copy-done), custom_call_target="tpu_custom_call" | custom-call | flops 1000 | bytes 1000 | tf_op jit(solution)/shard_map/move_own/pallas_call | solution.py:413
  8.2 0.7 %collective-permute-done.2.second_ref.image_ref = bf16[1,160,640]{2,1,0:T(8,128)(2,1)S(1)} collective-permute-done((bf16[1,160,640]{2,1,0:T(8,128)(2,1)}, bf16[1,160,640]{2,1,0:T(8,128)(2,1)S(1)}, u32[]{:S(2)}, u32[]{:S(2)}) %collective-permute-start.2) | collective-permute-done | bytes 204832 | tf_op jit(solution)/shard_map/ppermute | solution.py:392
  8.9 0.6 %correlate_own.1.row_ref = f32[8,128]{1,0:T(8,128)S(1)} custom-call(f32[3,160,640]{2,1,0:T(8,128)S(1)} %get-tuple-element.8.moved_ref, f32[3,8,128]{2,1,0:T(8,128)S(1)} %get-tuple-element.9.aux_ref, bf16[1,160,640]{2,1,0:T(8,128)(2,1)S(1)} %collective-permute-done.2.second_ref.image_ref), custom_call_target="tpu_custom_call" | custom-call | bytes 1000 | tf_op jit(solution)/shard_map/correlate_own/pallas_call | solution.py:416
  9.5 0.2 collective-permute-done.beside_ref
  9.7 0.0 collective-permute-done.1.along_ref
  9.7 0.7 %collective-permute-done.3.second_ref = bf16[1,160,640]{2,1,0:T(8,128)(2,1)S(1)} collective-permute-done((bf16[1,160,640]{2,1,0:T(8,128)(2,1)}, bf16[1,160,640]{2,1,0:T(8,128)(2,1)S(1)}, u32[]{:S(2)}, u32[]{:S(2)}) %collective-permute-start.3) | collective-permute-done | bytes 204832 | tf_op jit(solution)/shard_map/ppermute | solution.py:393
  10.4 0.9 %neighbours.1 = f32[64,128]{1,0:T(8,128)S(1)} custom-call(s32[1,4,4]{2,1,0:T(4,128)S(1)} %collective-permute-done.beside_ref, s32[1,4,4]{2,1,0:T(4,128)S(1)} %collective-permute-done.1.along_ref, bf16[5,160,160]{2,1,0:T(8,128)(2,1)S(1)} %get-tuple-element.6.rows_ref, bf16[28,256,256]{2,1,0:T(8,128)(2,1)S(1)} %get-tuple-element.7.across_ref, ...), custom_call_target="tpu_custom_call" | custom-call | bytes 1000 | tf_op jit(solution)/shard_map/neighbours/pallas_call | solution.py:423
  11.3 11.1 %all_to_all.11 = f32[32,2,128]{2,1,0:T(2,128)S(1)} all-to-all(f32[32,2,128]{2,1,0:T(2,128)S(1)} %bitcast.2), channel_id=1, replica_groups=mesh['gz'=8,'xy'=4] {'gz','xy'}, dimensions={0} | all-to-all | bytes 65536 | tf_op jit(solution)/shard_map/all_to_all | solution.py:432
  22.4 1.0 %relax.1 = (f32[2,1,1,4]{3,2,1,0:T(1,128)}, f32[2,1,4,8]{3,2,1,0:T(4,128)}) custom-call(f32[64,128]{1,0:T(8,128)S(1)} %bitcast.3), custom_call_target="tpu_custom_call" | custom-call | bytes 1000 | tf_op jit(solution)/shard_map/relax/pallas_call | solution.py:433
  (1 shorter events, 0.0 us)
Async XLA Ops:
  0.6 8.3 %collective-permute-start.2 = (bf16[1,160,640]{2,1,0:T(8,128)(2,1)}, bf16[1,160,640]{2,1,0:T(8,128)(2,1)S(1)}, u32[]{:S(2)}, u32[]{:S(2)}) collective-permute-start(bf16[1,160,640]{2,1,0:T(8,128)(2,1)} %own_ref.1), channel_id=1, source_target_pairs={{4,0},{5,1},{6,2},{7,3},{0,4},{1,5},{2,6},{3,7},{12,8},{13,9},{14,... | collective-permute-start | bytes 614408 | tf_op jit(solution)/shard_map/ppermute | solution.py:392
  3.6 6.7 %collective-permute-start.3 = (bf16[1,160,640]{2,1,0:T(8,128)(2,1)}, bf16[1,160,640]{2,1,0:T(8,128)(2,1)S(1)}, u32[]{:S(2)}, u32[]{:S(2)}) collective-permute-start(bf16[1,160,640]{2,1,0:T(8,128)(2,1)} %own_ref.1), channel_id=1, source_target_pairs={{8,0},{9,1},{10,2},{11,3},{5,4},{4,5},{7,6},{6,7},{0,8},{1,9},{2,1... | collective-permute-start | bytes 614408 | tf_op jit(solution)/shard_map/ppermute | solution.py:393
  5.9 3.7 %collective-permute-start.1 = (s32[1,4,4]{2,1,0:T(4,128)S(1)}, s32[1,4,4]{2,1,0:T(4,128)S(1)}, u32[]{:S(2)}, u32[]{:S(2)}) collective-permute-start(s32[1,4,4]{2,1,0:T(4,128)S(1)} %pad_add_fusion.codes_ref), channel_id=1, source_target_pairs={{1,0},{0,1},{3,2},{2,3},{5,4},{4,5},{7,6},{6,7},{9,8},{8,9},{11,10... | collective-permute-start | bytes 200 | tf_op jit(solution)/shard_map/ppermute | solution.py:394
  6.0 3.7 %collective-permute-start = (s32[1,4,4]{2,1,0:T(4,128)S(1)}, s32[1,4,4]{2,1,0:T(4,128)S(1)}, u32[]{:S(2)}, u32[]{:S(2)}) collective-permute-start(s32[1,4,4]{2,1,0:T(4,128)S(1)} %copy_codes.1), channel_id=1, source_target_pairs={{4,0},{5,1},{6,2},{7,3},{0,4},{1,5},{2,6},{3,7},{9,8},{8,9},{11,10... | collective-permute-start | bytes 200 | tf_op jit(solution)/shard_map/ppermute | solution.py:407
  6.6 0.9 %copy-start = (bf16[1,160,640]{2,1,0:T(8,128)(2,1)S(1)}, bf16[1,160,640]{2,1,0:T(8,128)(2,1)}, u32[]{:S(2)}) copy-start(bf16[1,160,640]{2,1,0:T(8,128)(2,1)} %own_ref.1) | copy-start | bytes 614404

commit v8 on v7

--- a/solution.py
+++ b/solution.py
@@ -137,10 +137,11 @@
 
 
 def roles():
-    section = lax.axis_index("gz")
-    fourth = lax.rem(section, 4)
-    turned = (fourth == 1) & (section > 1)
-    return lax.rem(section, 2) == 0, fourth == 0, turned
+    section, strip = lax.axis_index("gz"), lax.axis_index("xy")
+    place = lax.rem(section + 2 * lax.rem(strip, 2), 4)
+    straight = (place == 0) & (section + 2 < lax.axis_size("gz"))
+    turned = (place == 1) & (section > 1)
+    return lax.rem(section, 2) == 0, straight, turned
 
 
 def move_own(codes_ref, rows_ref, across_ref, own_ref, moved_ref, aux_ref):
@@ -270,34 +271,35 @@
     sections = splat_ref.shape[0] // (2 * strips)
     section, strip = lax.axis_index("gz"), lax.axis_index("xy")
     cols = flow_ref.shape[3]
-    fourth = lax.rem(section, 4)
-    after = (fourth == 3) & (section + 2 < sections)
-    worker = jnp.where(fourth == 1, section - 1, jnp.where(after, section + 2, section))
-    second = jnp.where((fourth == 1) | after, 1, 0)
-    home = splat_ref[pl.ds(2 * (worker * strips + strip) + second, 1), :]
+    below = lax.rem(section + 2 * lax.rem(strip, 2), 4) == 1
+    other = (lax.rem(section, 2) == 1) & (section + 1 < sections)
+    worker = jnp.where(other, jnp.where(below, section - 1, section + 2), section)
+    home = splat_ref[pl.ds(2 * (worker * strips + strip) + jnp.where(other, 1, 0), 1), :]
     for q in range(2):
         flow_ref[q, 0] = pltpu.roll(home, LANES - 3 * SPLAT - q * cols, 1)[:, :cols]
     lane = iota((sections, LANES), 1)
     place = iota((sections, LANES), 0)
-    which = (place, jnp.where((place & 3) == 0, place + 1, place - 2))
-    sums = [jnp.zeros((sections, LANES), jnp.float32)] * 2
-    for kind in range(2):
-        grid = [jnp.zeros((sections, LANES), jnp.float32)] * 3
-        for k in range(-2, 2):
-            at = strip + k
-            first = jnp.minimum(jnp.maximum(at, 0), strips - 1)
-            rows = splat_ref[pl.ds(2 * first + kind, sections, stride=2 * strips), :]
-            base = (k + 1) * BAND
-            inside = (lane >= base) & (lane < base + SPLAT) & (at >= 0) & (at < strips)
-            for q in range(3):
-                moved = pltpu.roll(rows, (base - q * SPLAT) % LANES, 1)
-                grid[q] = grid[q] + jnp.where(inside, moved, 0.0)
-        inverse = 1.0 / (1.0 + grid[2])
-        below = which[kind] < section
-        sums = [sums[q] + jnp.where(below, grid[q] * inverse, 0.0) for q in range(2)]
-    fixed = [
-        jnp.broadcast_to(jnp.sum(total, axis=0, keepdims=True), (SUBLANES, LANES)) for total in sums
-    ]
+    grid = [jnp.zeros((sections, LANES), jnp.float32)] * 3
+    for k in range(-2, 2):
+        at = strip + k
+        first = jnp.minimum(jnp.maximum(at, 0), strips - 1)
+        own, next_rows = (
+            splat_ref[pl.ds(2 * first + kind, sections, stride=2 * strips), :] for kind in range(2)
+        )
+        below = ((place + 2 * lax.rem(first, 2)) & 3) == 1
+        odd = jnp.where(below, pltpu.roll(next_rows, 1, 0), pltpu.roll(next_rows, sections - 2, 0))
+        rows = jnp.where((place & 1) == 0, own, odd)
+        base = (k + 1) * BAND
+        inside = (lane >= base) & (lane < base + SPLAT) & (at >= 0) & (at < strips)
+        for q in range(3):
+            moved = pltpu.roll(rows, (base - q * SPLAT) % LANES, 1)
+            grid[q] = grid[q] + jnp.where(inside, moved, 0.0)
+    inverse = 1.0 / (1.0 + grid[2])
+    fixed = []
+    for q in range(2):
+        target = jnp.where(place < section, grid[q] * inverse, 0.0)
+        total = jnp.sum(target, axis=0, keepdims=True)
+        fixed.append(jnp.broadcast_to(total, (SUBLANES, LANES)))
     reach = SPRING_STEPS
     fields = {
         o: tuple(
@@ -374,19 +376,26 @@
     devices = sections * strips
 
     def pairing(other):
+        mates = {(i, r): other(i, r % 2) for i in range(sections) for r in range(strips)}
+        free = {(i, r) for (i, r), j in mates.items() if not 0 <= j < sections}
         route = []
-        for i in range(sections):
-            j = other(i)
-            for r in range(strips):
-                mate = j * strips + r if 0 <= j < sections else i * strips + (r ^ 1)
-                route.append((mate, i * strips + r))
+        for (i, r), j in mates.items():
+            if (i, r) in free:
+                j, mate = i, r ^ 1 if (i, r ^ 1) in free else r ^ 2
+            else:
+                mate = r
+            route.append((j * strips + mate, i * strips + r))
         return route
 
-    beside = pairing(lambda i: i ^ 1)
-    along = pairing(lambda i: i ^ 2 if i % 2 == 0 else i + 2 if i % 4 == 3 else i - 2)
+    def two_away(i, p):
+        step = 2 if (i + 2 * p) % 4 in (0, 3) else -2
+        return i + step
+
+    beside = pairing(lambda i, p: i ^ 1)
+    along = pairing(two_away)
     codes_routes = (
-        pairing(lambda i: i ^ 1 if i % 4 < 2 else -1),
-        pairing(lambda i: -1 if i % 2 == 0 else i + 2 if i % 4 == 3 else i - 2),
+        pairing(lambda i, p: i ^ 1 if (i + 2 * p) % 4 < 2 else -1),
+        pairing(lambda i, p: two_away(i, p) if i % 2 else -1),
     )
     codes = jnp.concatenate([peak_code, cell_block, cell_offset, valid_patch], axis=1)
     image_beside = lax.ppermute(images, ("gz", "xy"), beside)

time: 23.5 us -> 23.3 us (level)
  waiting for transfers between devices: 1.63 us -> 0.45 us
  blocking collectives: 11.1 us -> 11.6 us
  starting transfers between devices: 4.71 us -> 5.19 us
    ppermute x1, waiting for transfers between devices: 0.72 us -> 0.01 us  [on_device(): image_along = lax.ppermute(images, ('gz', 'xy'), along)]
    all_to_all x1, blocking collectives: 11.1 us -> 11.6 us  [on_device(): gathered = lax.all_to_all(splat, ('gz', 'xy'), 0, 0, tiled=True)]
    ppermute x1, starting transfers between devices: 0.07 us -> 0.54 us  [on_device(): codes_beside = lax.ppermute(again(codes), ('gz', 'xy'), codes_routes[0])]
    ppermute x1, waiting for transfers between devices: 0.73 us -> 0.27 us  [on_device(): image_beside = lax.ppermute(images, ('gz', 'xy'), beside)]
  transfers between devices with their start and end apart: 4 -> 4, of which waited for: 3 -> 2; matrix products, arithmetic and copies ran while one was open for 3% -> 3% of each run, Pallas kernels for 7% -> 7%
where the time goes in v8:
time: 23.3 us; the launch traced here: 23.2 us
  blocking collectives  11.6 us (50%)
  starting transfers between devices  5.19 us (22%)
  Pallas kernels  3.61 us (15%)
  local copies, waits for them, and re-layouts  0.93 us (4%)
  other arithmetic  0.71 us (3%)
  between operations  0.68 us (3%)
  waiting for transfers between devices  0.45 us (2%)
    all_to_all x1, blocking collectives, on_device(): gathered = lax.all_to_all(splat, ('gz', 'xy'), 0, 0, tiled=True)  11.6 us
    ppermute x1, starting transfers between devices, on_device(): image_beside = lax.ppermute(images, ('gz', 'xy'), beside)  3 us
    ppermute x1, starting transfers between devices, on_device(): image_along = lax.ppermute(images, ('gz', 'xy'), along)  1.58 us
    pallas_call x1, Pallas kernels, on_device(): call(functools.partial(relax, strips), (jax.ShapeDtypeStruct((2, 1, 1, co...  0.98 us
    unnamed x2, local copies, waits for them, and re-layouts  0.93 us
    pallas_call x1, Pallas kernels, on_device(): call(neighbours, pltpu.VMEM((2 * devices, LANES), jnp.float32), [VMEM] *...  0.91 us
    concatenate x1, other arithmetic, on_device(): jnp.concatenate([peak_code, cell_block, cell_offset, valid_patch], axis=1)  0.71 us
    pallas_call x1, Pallas kernels, on_device(): call(move_own, moved_shape, [VMEM] * 4, flops=1000, name='move_own')  0.66 us
  transfers between devices with their start and end apart: 4, of which 2 were waited for; matrix products, arithmetic and copies ran while one was open for 3% of the time, Pallas kernels for 7%

profile of v8, /device:TPU:0, one launch (start us, length us, event | category | flops | bytes accessed | tf_op | source)
XLA Modules:
  0.0 23.2 jit_solution(8445514781561507696)
XLA Ops:
  0.6 3.0 %collective-permute-start.2 = (bf16[1,160,640]{2,1,0:T(8,128)(2,1)}, bf16[1,160,640]{2,1,0:T(8,128)(2,1)S(1)}, u32[]{:S(2)}, u32[]{:S(2)}) collective-permute-start(bf16[1,160,640]{2,1,0:T(8,128)(2,1)} %own_ref.1), channel_id=1, source_target_pairs={{4,0},{5,1},{6,2},{7,3},{0,4},{1,5},{2,6},{3,7},{12,8},{13,9},{14,... | collective-permute-start | bytes 614408 | tf_op jit(solution)/shard_map/ppermute | solution.py:401
  3.6 1.6 %collective-permute-start.3 = (bf16[1,160,640]{2,1,0:T(8,128)(2,1)}, bf16[1,160,640]{2,1,0:T(8,128)(2,1)S(1)}, u32[]{:S(2)}, u32[]{:S(2)}) collective-permute-start(bf16[1,160,640]{2,1,0:T(8,128)(2,1)} %own_ref.1), channel_id=1, source_target_pairs={{8,0},{3,1},{10,2},{1,3},{6,4},{13,5},{4,6},{15,7},{0,8},{17,9},{2... | collective-permute-start | bytes 614408 | tf_op jit(solution)/shard_map/ppermute | solution.py:402
  5.2 0.7 %pad_add_fusion.codes_ref = s32[1,4,4]{2,1,0:T(4,128)S(1)} fusion(s32[1,1,4]{2,1,0:T(1,128)} %param.9, s32[1,1,4]{2,1,0:T(1,128)} %param.8, s32[1,1,4]{2,1,0:T(1,128)} %param.7, s32[1,1,4]{2,1,0:T(1,128)} %param.6), kind=kLoop, calls=%fused_computation | loop fusion | flops 48 | bytes 128 | tf_op jit(solution)/shard_map/concatenate | solution.py:400
  5.9 0.1 collective-permute-start.1
  6.0 0.5 %collective-permute-start = (s32[1,4,4]{2,1,0:T(4,128)S(1)}, s32[1,4,4]{2,1,0:T(4,128)S(1)}, u32[]{:S(2)}, u32[]{:S(2)}) collective-permute-start(s32[1,4,4]{2,1,0:T(4,128)S(1)} %copy_codes.1), channel_id=1, source_target_pairs={{4,0},{3,1},{6,2},{1,3},{0,4},{7,5},{2,6},{5,7},{10,8},{13,9},{8,1... | collective-permute-start | bytes 200 | tf_op jit(solution)/shard_map/ppermute | solution.py:416
  6.6 0.5 %bank.1 = (bf16[5,160,160]{2,1,0:T(8,128)(2,1)S(1)}, bf16[28,256,256]{2,1,0:T(8,128)(2,1)S(1)}) custom-call(), custom_call_target="tpu_custom_call" | custom-call | flops 1000 | bytes 1000 | tf_op jit(solution)/shard_map/bank/pallas_call | solution.py:405
  7.1 0.0 copy-start
  7.1 0.9 %copy-done = bf16[1,160,640]{2,1,0:T(8,128)(2,1)S(1)} copy-done((bf16[1,160,640]{2,1,0:T(8,128)(2,1)S(1)}, bf16[1,160,640]{2,1,0:T(8,128)(2,1)}, u32[]{:S(2)}) %copy-start) | copy-done | bytes 204824
  8.0 0.7 %move_own.1 = (f32[3,160,640]{2,1,0:T(8,128)S(1)}, f32[3,8,128]{2,1,0:T(8,128)S(1)}) custom-call(s32[1,4,4]{2,1,0:T(4,128)S(1)} %pad_add_fusion.codes_ref, bf16[5,160,160]{2,1,0:T(8,128)(2,1)S(1)} %get-tuple-element.6.rows_ref, bf16[28,256,256]{2,1,0:T(8,128)(2,1)S(1)} %get-tuple-element.7.across_ref, bf16[1,160,640]{2,1,0:T(8,128)(2,1)S(1)} %copy-done), custom_call_target="tpu_custom_call" | custom-call | flops 1000 | bytes 1000 | tf_op jit(solution)/shard_map/move_own/pallas_call | solution.py:422
  8.7 0.3 %collective-permute-done.2.second_ref.image_ref = bf16[1,160,640]{2,1,0:T(8,128)(2,1)S(1)} collective-permute-done((bf16[1,160,640]{2,1,0:T(8,128)(2,1)}, bf16[1,160,640]{2,1,0:T(8,128)(2,1)S(1)}, u32[]{:S(2)}, u32[]{:S(2)}) %collective-permute-start.2) | collective-permute-done | bytes 204832 | tf_op jit(solution)/shard_map/ppermute | solution.py:401
  8.9 0.6 %correlate_own.1.row_ref = f32[8,128]{1,0:T(8,128)S(1)} custom-call(f32[3,160,640]{2,1,0:T(8,128)S(1)} %get-tuple-element.8.moved_ref, f32[3,8,128]{2,1,0:T(8,128)S(1)} %get-tuple-element.9.aux_ref, bf16[1,160,640]{2,1,0:T(8,128)(2,1)S(1)} %collective-permute-done.2.second_ref.image_ref), custom_call_target="tpu_custom_call" | custom-call | bytes 1000 | tf_op jit(solution)/shard_map/correlate_own/pallas_call | solution.py:425
  9.5 0.2 collective-permute-done.beside_ref
  9.7 0.0 collective-permute-done.1.along_ref
  9.7 0.0 collective-permute-done.3.second_ref
  9.7 0.9 %neighbours.1 = f32[64,128]{1,0:T(8,128)S(1)} custom-call(s32[1,4,4]{2,1,0:T(4,128)S(1)} %collective-permute-done.beside_ref, s32[1,4,4]{2,1,0:T(4,128)S(1)} %collective-permute-done.1.along_ref, bf16[5,160,160]{2,1,0:T(8,128)(2,1)S(1)} %get-tuple-element.6.rows_ref, bf16[28,256,256]{2,1,0:T(8,128)(2,1)S(1)} %get-tuple-element.7.across_ref, ...), custom_call_target="tpu_custom_call" | custom-call | bytes 1000 | tf_op jit(solution)/shard_map/neighbours/pallas_call | solution.py:432
  10.6 11.6 %all_to_all.11 = f32[32,2,128]{2,1,0:T(2,128)S(1)} all-to-all(f32[32,2,128]{2,1,0:T(2,128)S(1)} %bitcast.2), channel_id=1, replica_groups=mesh['gz'=8,'xy'=4] {'gz','xy'}, dimensions={0} | all-to-all | bytes 65536 | tf_op jit(solution)/shard_map/all_to_all | solution.py:441
  22.2 1.0 %relax.1 = (f32[2,1,1,4]{3,2,1,0:T(1,128)}, f32[2,1,4,8]{3,2,1,0:T(4,128)}) custom-call(f32[64,128]{1,0:T(8,128)S(1)} %bitcast.3), custom_call_target="tpu_custom_call" | custom-call | bytes 1000 | tf_op jit(solution)/shard_map/relax/pallas_call | solution.py:442
  (1 shorter events, 0.0 us)
Async XLA Ops:
  0.6 8.3 %collective-permute-start.2 = (bf16[1,160,640]{2,1,0:T(8,128)(2,1)}, bf16[1,160,640]{2,1,0:T(8,128)(2,1)S(1)}, u32[]{:S(2)}, u32[]{:S(2)}) collective-permute-start(bf16[1,160,640]{2,1,0:T(8,128)(2,1)} %own_ref.1), channel_id=1, source_target_pairs={{4,0},{5,1},{6,2},{7,3},{0,4},{1,5},{2,6},{3,7},{12,8},{13,9},{14,... | collective-permute-start | bytes 614408 | tf_op jit(solution)/shard_map/ppermute | solution.py:401
  3.6 6.0 %collective-permute-start.3 = (bf16[1,160,640]{2,1,0:T(8,128)(2,1)}, bf16[1,160,640]{2,1,0:T(8,128)(2,1)S(1)}, u32[]{:S(2)}, u32[]{:S(2)}) collective-permute-start(bf16[1,160,640]{2,1,0:T(8,128)(2,1)} %own_ref.1), channel_id=1, source_target_pairs={{8,0},{3,1},{10,2},{1,3},{6,4},{13,5},{4,6},{15,7},{0,8},{17,9},{2... | collective-permute-start | bytes 614408 | tf_op jit(solution)/shard_map/ppermute | solution.py:402
  5.9 3.7 %collective-permute-start.1 = (s32[1,4,4]{2,1,0:T(4,128)S(1)}, s32[1,4,4]{2,1,0:T(4,128)S(1)}, u32[]{:S(2)}, u32[]{:S(2)}) collective-permute-start(s32[1,4,4]{2,1,0:T(4,128)S(1)} %pad_add_fusion.codes_ref), channel_id=1, source_target_pairs={{1,0},{0,1},{3,2},{2,3},{6,4},{13,5},{4,6},{15,7},{9,8},{8,9},{11,... | collective-permute-start | bytes 200 | tf_op jit(solution)/shard_map/ppermute | solution.py:403
  6.0 3.7 %collective-permute-start = (s32[1,4,4]{2,1,0:T(4,128)S(1)}, s32[1,4,4]{2,1,0:T(4,128)S(1)}, u32[]{:S(2)}, u32[]{:S(2)}) collective-permute-start(s32[1,4,4]{2,1,0:T(4,128)S(1)} %copy_codes.1), channel_id=1, source_target_pairs={{4,0},{3,1},{6,2},{1,3},{0,4},{7,5},{2,6},{5,7},{10,8},{13,9},{8,1... | collective-permute-start | bytes 200 | tf_op jit(solution)/shard_map/ppermute | solution.py:416
  7.1 0.9 %copy-start = (bf16[1,160,640]{2,1,0:T(8,128)(2,1)S(1)}, bf16[1,160,640]{2,1,0:T(8,128)(2,1)}, u32[]{:S(2)}) copy-start(bf16[1,160,640]{2,1,0:T(8,128)(2,1)} %own_ref.1) | copy-start | bytes 614404

commit v9 on v8

--- a/solution.py
+++ b/solution.py
@@ -137,19 +137,20 @@
 
 
 def roles():
-    section, strip = lax.axis_index("gz"), lax.axis_index("xy")
-    place = lax.rem(section + 2 * lax.rem(strip, 2), 4)
-    straight = (place == 0) & (section + 2 < lax.axis_size("gz"))
-    turned = (place == 1) & (section > 1)
-    return lax.rem(section, 2) == 0, straight, turned
+    section = lax.axis_index("gz")
+    odd_strip = lax.rem(lax.axis_index("xy"), 2) == 1
+    odd = lax.rem(section, 2) == 1
+    down = jnp.logical_not(odd_strip) & jnp.logical_not(odd)
+    up = odd_strip & odd
+    return down, up, down & (section + 2 < lax.axis_size("gz")), up & (section > 1)
 
 
 def move_own(codes_ref, rows_ref, across_ref, own_ref, moved_ref, aux_ref):
     codes = codes_ref[0]
     peaks = peaks_of(codes)
     splat_weights(codes.astype(jnp.float32), aux_ref)
-    own, _, _ = roles()
-    pl.when(own)(lambda: move(peaks, rows_ref, across_ref, own_ref, moved_ref))
+    down, _, _, _ = roles()
+    pl.when(down)(lambda: move(peaks, rows_ref, across_ref, own_ref, moved_ref))
 
 
 def stage(second_ref, held_ref):
@@ -216,29 +217,48 @@
     return jnp.broadcast_to(row, (SUBLANES, LANES))
 
 
-def correlate_own(moved_ref, aux_ref, second_ref, row_ref, held_ref):
-    cols = second_ref.shape[2] // PATCH_SIZE
-    own, _, _ = roles()
-
-    @pl.when(own)
+def moved_sums(peaks, rows_ref, across_ref, image_ref, second_ref, moved_ref, held_ref):
+    stage(second_ref, held_ref)
+    total = no_sums()
+    move(
+        peaks, rows_ref, across_ref, image_ref, moved_ref,
+        lambda tile: add_tile(tile, moved_ref, held_ref, total),
+    )
+    return over_lanes(total)
+
+
+def pairs(
+    own_moved_ref, own_aux_ref, beside_ref, rows_ref, across_ref, image_ref, own_ref,
+    row_ref, moved_ref, held_ref, aux_ref,
+):
+    cols = own_ref.shape[2] // PATCH_SIZE
+    down, up, _, _ = roles()
+
+    @pl.when(down)
     def _():
-        stage(second_ref, held_ref)
+        stage(image_ref, held_ref)
         total = no_sums()
-        for tile in range(second_ref.shape[2] // LANES):
-            add_tile(tile, moved_ref, held_ref, total)
-        row_ref[...] = splat_row(over_lanes(total), aux_ref, cols)
-
-    @pl.when(jnp.logical_not(own))
+        for tile in range(own_ref.shape[2] // LANES):
+            add_tile(tile, own_moved_ref, held_ref, total)
+        row_ref[...] = splat_row(over_lanes(total), own_aux_ref, cols)
+
+    @pl.when(up)
     def _():
-        row = splat_row([jnp.zeros((SUBLANES, 1), jnp.float32)] * LAGS, aux_ref, cols)
-        row_ref[...] = jnp.where(iota((SUBLANES, LANES), 1) < 3 * SPLAT, 0.0, row)
+        splat_weights(beside_ref[0].astype(jnp.float32), aux_ref)
+        peaks = peaks_of(beside_ref[0])
+        corr = moved_sums(peaks, rows_ref, across_ref, image_ref, own_ref, moved_ref, held_ref)
+        row_ref[...] = splat_row(corr, aux_ref, cols)
+
+    @pl.when(jnp.logical_not(down | up))
+    def _():
+        row_ref[...] = jnp.zeros((SUBLANES, LANES), jnp.float32)
 
 
 def neighbours(
     beside_ref, along_ref, rows_ref, across_ref, image_ref, second_ref, row_ref,
     splat_ref, moved_ref, held_ref, aux_ref,
 ):
-    _, straight, turned = roles()
+    _, _, straight, turned = roles()
     some = straight | turned
     even = lax.rem(iota(splat_ref.shape, 0), 2) == 0
 
@@ -252,13 +272,7 @@
         back = (2 * PEAK + 1) ** 2 - 1
         peaks = [jnp.where(straight, peak, back - peak) for peak in peaks_of(codes)]
         splat_weights(codes.astype(jnp.float32), aux_ref)
-        stage(second_ref, held_ref)
-        total = no_sums()
-        move(
-            peaks, rows_ref, across_ref, image_ref, moved_ref,
-            lambda tile: add_tile(tile, moved_ref, held_ref, total),
-        )
-        corr = over_lanes(total)
+        corr = moved_sums(peaks, rows_ref, across_ref, image_ref, second_ref, moved_ref, held_ref)
         corr = [jnp.where(straight, value, other) for value, other in zip(corr, corr[::-1])]
         spread(splat_row(corr, aux_ref, len(peaks)))
 
@@ -267,28 +281,33 @@
         spread(jnp.zeros((SUBLANES, LANES), jnp.float32))
 
 
-def relax(strips, splat_ref, flow_ref, out_ref):
+def relax(strips, splat_ref, own_aux_ref, flow_ref, out_ref):
     sections = splat_ref.shape[0] // (2 * strips)
     section, strip = lax.axis_index("gz"), lax.axis_index("xy")
     cols = flow_ref.shape[3]
-    below = lax.rem(section + 2 * lax.rem(strip, 2), 4) == 1
-    other = (lax.rem(section, 2) == 1) & (section + 1 < sections)
-    worker = jnp.where(other, jnp.where(below, section - 1, section + 2), section)
-    home = splat_ref[pl.ds(2 * (worker * strips + strip) + jnp.where(other, 1, 0), 1), :]
+    odd, odd_strip = lax.rem(section, 2), lax.rem(strip, 2)
+    worker = section + jnp.where(odd_strip == 1, 1 + odd, -odd)
+    last = section + 1 == sections
+    worker = jnp.where(last, section, worker)
+    home = splat_ref[pl.ds(2 * (worker * strips + strip) + odd, 1), :]
+    diagonal = iota((SUBLANES, LANES), 0) == iota((SUBLANES, LANES), 1)
     for q in range(2):
-        flow_ref[q, 0] = pltpu.roll(home, LANES - 3 * SPLAT - q * cols, 1)[:, :cols]
+        peak = jnp.sum(jnp.where(diagonal, own_aux_ref[1 + q], 0.0), axis=0, keepdims=True)
+        flow = pltpu.roll(home, LANES - 3 * SPLAT - q * cols, 1)
+        flow_ref[q, 0] = jnp.where(last, peak, flow)[:, :cols]
     lane = iota((sections, LANES), 1)
     place = iota((sections, LANES), 0)
     grid = [jnp.zeros((sections, LANES), jnp.float32)] * 3
     for k in range(-2, 2):
         at = strip + k
         first = jnp.minimum(jnp.maximum(at, 0), strips - 1)
-        own, next_rows = (
+        pair, after = (
             splat_ref[pl.ds(2 * first + kind, sections, stride=2 * strips), :] for kind in range(2)
         )
-        below = ((place + 2 * lax.rem(first, 2)) & 3) == 1
-        odd = jnp.where(below, pltpu.roll(next_rows, 1, 0), pltpu.roll(next_rows, sections - 2, 0))
-        rows = jnp.where((place & 1) == 0, own, odd)
+        odd_strip = lax.rem(first, 2) == 1
+        pair = jnp.where(odd_strip, pltpu.roll(pair, sections - 1, 0), pair)
+        after = jnp.where(odd_strip, pltpu.roll(after, sections - 2, 0), pltpu.roll(after, 1, 0))
+        rows = jnp.where((place & 1) == 0, pair, after)
         base = (k + 1) * BAND
         inside = (lane >= base) & (lane < base + SPLAT) & (at >= 0) & (at < strips)
         for q in range(3):
@@ -375,32 +394,21 @@
     sections, strips = lax.axis_size("gz"), lax.axis_size("xy")
     devices = sections * strips
 
-    def pairing(other):
-        mates = {(i, r): other(i, r % 2) for i in range(sections) for r in range(strips)}
-        free = {(i, r) for (i, r), j in mates.items() if not 0 <= j < sections}
-        route = []
-        for (i, r), j in mates.items():
-            if (i, r) in free:
-                j, mate = i, r ^ 1 if (i, r ^ 1) in free else r ^ 2
-            else:
-                mate = r
-            route.append((j * strips + mate, i * strips + r))
-        return route
-
-    def two_away(i, p):
-        step = 2 if (i + 2 * p) % 4 in (0, 3) else -2
-        return i + step
-
-    beside = pairing(lambda i, p: i ^ 1)
-    along = pairing(two_away)
-    codes_routes = (
-        pairing(lambda i, p: i ^ 1 if (i + 2 * p) % 4 < 2 else -1),
-        pairing(lambda i, p: two_away(i, p) if i % 2 else -1),
-    )
+    def ring(devices):
+        places = [i * strips + r for i, r in devices]
+        return list(zip(places, places[1:] + places[:1]))
+
+    beside, along = [], []
+    for r in range(0, strips, 2):
+        for i in range(0, sections, 2):
+            beside += ring([(i + 1, r), (i, r), (i, r + 1), (i + 1, r + 1)])
+        for start in range(2):
+            column = range(start, sections, 2)
+            along += ring([(i, r + 1) for i in column] + [(i, r) for i in reversed(column)])
     codes = jnp.concatenate([peak_code, cell_block, cell_offset, valid_patch], axis=1)
     image_beside = lax.ppermute(images, ("gz", "xy"), beside)
     image_along = lax.ppermute(images, ("gz", "xy"), along)
-    codes_along = lax.ppermute(codes, ("gz", "xy"), codes_routes[1])
+    codes_along = lax.ppermute(codes, ("gz", "xy"), along)
     width = max(w for _, _, w, _ in windows(cols, PATCH_SIZE))
     rows, across = call(
         bank,
@@ -413,29 +421,29 @@
         name="bank",
     )()
     again = call(copy_codes, pltpu.VMEM(codes.shape, codes.dtype), [VMEM], name="copy_codes")
-    codes_beside = lax.ppermute(again(codes), ("gz", "xy"), codes_routes[0])
+    codes_beside = lax.ppermute(again(codes), ("gz", "xy"), beside)
     moved_shape = (
         pltpu.VMEM((3, size, breadth), jnp.float32),
         pltpu.VMEM((3, SUBLANES, LANES), jnp.float32),
     )
     held = [pltpu.VMEM((breadth // LANES, size + 2 * SUBLANES, LANES), jnp.float32)]
+    work = [pltpu.VMEM(moved_shape[0].shape, jnp.float32)] + held
+    work += [pltpu.VMEM(moved_shape[1].shape, jnp.float32)]
     moved, aux = call(
         move_own, moved_shape, [VMEM] * 4, flops=1_000, name="move_own"
     )(codes, rows, across, images)
     row = call(
-        correlate_own,
+        pairs,
         pltpu.VMEM((SUBLANES, LANES), jnp.float32),
-        [VMEM] * 3,
-        scratch_shapes=held,
-        name="correlate_own",
-    )(moved, aux, image_beside)
+        [VMEM] * 7,
+        scratch_shapes=work,
+        name="pairs",
+    )(moved, aux, codes_beside, rows, across, image_beside, images)
     splat = call(
         neighbours,
         pltpu.VMEM((2 * devices, LANES), jnp.float32),
         [VMEM] * 7,
-        scratch_shapes=[pltpu.VMEM(shape.shape, jnp.float32) for shape in moved_shape[:1]]
-        + held
-        + [pltpu.VMEM((3, SUBLANES, LANES), jnp.float32)],
+        scratch_shapes=work,
         name="neighbours",
     )(codes_beside, codes_along, rows, across, image_beside, image_along, row)
     gathered = lax.all_to_all(splat, ("gz", "xy"), 0, 0, tiled=True)
@@ -445,9 +453,9 @@
             jax.ShapeDtypeStruct((2, 1, 1, cols), jnp.float32),
             jax.ShapeDtypeStruct((2, 1, BAND_ROWS, NODE_COLS), jnp.float32),
         ),
-        [VMEM],
+        [VMEM] * 2,
         name="relax",
-    )(gathered)
+    )(gathered, aux)
     return (flow, node_shift)
 
 

time: 23.3 us -> 22.4 us (0.961)
  blocking collectives: 11.6 us -> 11.1 us
  waiting for transfers between devices: 0.45 us -> 0.19 us
    ppermute x1, starting transfers between devices: 3 us -> 0.47 us  [on_device(): image_beside = lax.ppermute(images, ('gz', 'xy'), beside)]
    ppermute x2, starting transfers between devices: 0.61 us -> 2.6 us  [the longest x1 1.31 us: on_device(): codes_along = lax.ppermute(codes, ('gz', 'xy'), along)]
    all_to_all x1, blocking collectives: 11.6 us -> 11.1 us  [on_device(): gathered = lax.all_to_all(splat, ('gz', 'xy'), 0, 0, tiled=True)]
    ppermute x1, starting transfers between devices: 1.58 us -> 2.04 us  [on_device(): image_along = lax.ppermute(images, ('gz', 'xy'), along)]
    ppermute x1, waiting for transfers between devices: 0.27 us -> 0.01 us  [on_device(): image_beside = lax.ppermute(images, ('gz', 'xy'), beside)]
  transfers between devices with their start and end apart: 4 -> 4, of which waited for: 2 -> 1; matrix products, arithmetic and copies ran while one was open for 3% -> 3% of each run, Pallas kernels for 7% -> 7%
where the time goes in v9:
time: 22.4 us; the launch traced here: 22.2 us
  blocking collectives  11.1 us (50%)
  starting transfers between devices  5.11 us (23%)
  Pallas kernels  3.48 us (16%)
  local copies, waits for them, and re-layouts  0.93 us (4%)
  other arithmetic  0.71 us (3%)
  between operations  0.69 us (3%)
    all_to_all x1, blocking collectives, on_device(): gathered = lax.all_to_all(splat, ('gz', 'xy'), 0, 0, tiled=True)  11.1 us
    ppermute x1, starting transfers between devices, on_device(): image_along = lax.ppermute(images, ('gz', 'xy'), along)  2.04 us
    ppermute x1, starting transfers between devices, on_device(): codes_along = lax.ppermute(codes, ('gz', 'xy'), along)  1.31 us
    ppermute x1, starting transfers between devices, on_device(): codes_beside = lax.ppermute(again(codes), ('gz', 'xy'), beside)  1.3 us
    pallas_call x1, Pallas kernels, on_device(): call(functools.partial(relax, strips), (jax.ShapeDtypeStruct((2, 1, 1, co...  0.98 us
    unnamed x2, local copies, waits for them, and re-layouts  0.93 us
    pallas_call x1, Pallas kernels, on_device(): call(neighbours, pltpu.VMEM((2 * devices, LANES), jnp.float32), [VMEM] *...  0.9 us
    concatenate x1, other arithmetic, on_device(): jnp.concatenate([peak_code, cell_block, cell_offset, valid_patch], axis=1)  0.71 us
  transfers between devices with their start and end apart: 4, of which 1 were waited for; matrix products, arithmetic and copies ran while one was open for 3% of the time, Pallas kernels for 7%

profile of v9, /device:TPU:0, one launch (start us, length us, event | category | flops | bytes accessed | tf_op | source)
XLA Modules:
  0.0 22.2 jit_solution(7461523737130888416)
XLA Ops:
  0.6 0.5 %collective-permute-start.2 = (bf16[1,160,640]{2,1,0:T(8,128)(2,1)}, bf16[1,160,640]{2,1,0:T(8,128)(2,1)S(1)}, u32[]{:S(2)}, u32[]{:S(2)}) collective-permute-start(bf16[1,160,640]{2,1,0:T(8,128)(2,1)} %own_ref.3), channel_id=1, source_target_pairs={{4,0},{0,1},{1,5},{5,4},{12,8},{8,9},{9,13},{13,12},{20,16},{16,17... | collective-permute-start | bytes 614408 | tf_op jit(solution)/shard_map/ppermute | solution.py:409
  1.1 2.0 %collective-permute-start.3 = (bf16[1,160,640]{2,1,0:T(8,128)(2,1)}, bf16[1,160,640]{2,1,0:T(8,128)(2,1)S(1)}, u32[]{:S(2)}, u32[]{:S(2)}) collective-permute-start(bf16[1,160,640]{2,1,0:T(8,128)(2,1)} %own_ref.3), channel_id=1, source_target_pairs={{1,9},{9,17},{17,25},{25,24},{24,16},{16,8},{8,0},{0,1},{5,13},{13... | collective-permute-start | bytes 614408 | tf_op jit(solution)/shard_map/ppermute | solution.py:410
  3.1 0.7 %pad_add_fusion.codes_ref = s32[1,4,4]{2,1,0:T(4,128)S(1)} fusion(s32[1,1,4]{2,1,0:T(1,128)} %param.9, s32[1,1,4]{2,1,0:T(1,128)} %param.8, s32[1,1,4]{2,1,0:T(1,128)} %param.7, s32[1,1,4]{2,1,0:T(1,128)} %param.6), kind=kLoop, calls=%fused_computation | loop fusion | flops 48 | bytes 128 | tf_op jit(solution)/shard_map/concatenate | solution.py:408
  3.9 1.3 %collective-permute-start.1 = (s32[1,4,4]{2,1,0:T(4,128)S(1)}, s32[1,4,4]{2,1,0:T(4,128)S(1)}, u32[]{:S(2)}, u32[]{:S(2)}) collective-permute-start(s32[1,4,4]{2,1,0:T(4,128)S(1)} %pad_add_fusion.codes_ref), channel_id=1, source_target_pairs={{1,9},{9,17},{17,25},{25,24},{24,16},{16,8},{8,0},{0,1},{5,13},{13... | collective-permute-start | bytes 200 | tf_op jit(solution)/shard_map/ppermute | solution.py:411
  5.2 1.3 %collective-permute-start = (s32[1,4,4]{2,1,0:T(4,128)S(1)}, s32[1,4,4]{2,1,0:T(4,128)S(1)}, u32[]{:S(2)}, u32[]{:S(2)}) collective-permute-start(s32[1,4,4]{2,1,0:T(4,128)S(1)} %copy_codes.1), channel_id=1, source_target_pairs={{4,0},{0,1},{1,5},{5,4},{12,8},{8,9},{9,13},{13,12},{20,16},{16,17... | collective-permute-start | bytes 200 | tf_op jit(solution)/shard_map/ppermute | solution.py:424
  6.5 0.5 %bank.1 = (bf16[5,160,160]{2,1,0:T(8,128)(2,1)S(1)}, bf16[28,256,256]{2,1,0:T(8,128)(2,1)S(1)}) custom-call(), custom_call_target="tpu_custom_call" | custom-call | flops 1000 | bytes 1000 | tf_op jit(solution)/shard_map/bank/pallas_call | solution.py:413
  7.0 0.0 copy-start
  7.0 0.9 %copy-done = bf16[1,160,640]{2,1,0:T(8,128)(2,1)S(1)} copy-done((bf16[1,160,640]{2,1,0:T(8,128)(2,1)S(1)}, bf16[1,160,640]{2,1,0:T(8,128)(2,1)}, u32[]{:S(2)}) %copy-start) | copy-done | bytes 204824
  7.9 0.7 %move_own.1 = (f32[3,160,640]{2,1,0:T(8,128)S(1)}, f32[3,8,128]{2,1,0:T(8,128)S(1)}) custom-call(s32[1,4,4]{2,1,0:T(4,128)S(1)} %pad_add_fusion.codes_ref, bf16[5,160,160]{2,1,0:T(8,128)(2,1)S(1)} %get-tuple-element.6.rows_ref, bf16[28,256,256]{2,1,0:T(8,128)(2,1)S(1)} %get-tuple-element.7.across_ref, bf16[1,160,640]{2,1,0:T(8,128)(2,1)S(1)} %copy-done), custom_call_target="tpu_custom_call" | custom-call | flops 1000 | bytes 1000 | tf_op jit(solution)/shard_map/move_own/pallas_call | solution.py:432
  8.6 0.2 collective-permute-done.beside_ref
  8.7 0.0 collective-permute-done.2.image_ref
  8.8 0.4 %pairs.1.row_ref = f32[8,128]{1,0:T(8,128)S(1)} custom-call(f32[3,160,640]{2,1,0:T(8,128)S(1)} %get-tuple-element.8.own_moved_ref, f32[3,8,128]{2,1,0:T(8,128)S(1)} %get-tuple-element.9.own_aux_ref, s32[1,4,4]{2,1,0:T(4,128)S(1)} %collective-permute-done.beside_ref, bf16[5,160,160]{2,1,0:T(8,128)(2,1)S(1)} %get-tuple-element.6.rows_ref, ...), custom_call_target="tpu_custom_call" | custom-call | bytes 1000 | tf_op jit(solution)/shard_map/pairs/pallas_call | solution.py:435
  9.2 0.0 collective-permute-done.1.along_ref
  9.2 0.0 collective-permute-done.3.second_ref
  9.2 0.9 %neighbours.1 = f32[64,128]{1,0:T(8,128)S(1)} custom-call(s32[1,4,4]{2,1,0:T(4,128)S(1)} %collective-permute-done.beside_ref, s32[1,4,4]{2,1,0:T(4,128)S(1)} %collective-permute-done.1.along_ref, bf16[5,160,160]{2,1,0:T(8,128)(2,1)S(1)} %get-tuple-element.6.rows_ref, bf16[28,256,256]{2,1,0:T(8,128)(2,1)S(1)} %get-tuple-element.7.across_ref, ...), custom_call_target="tpu_custom_call" | custom-call | bytes 1000 | tf_op jit(solution)/shard_map/neighbours/pallas_call | solution.py:442
  10.1 11.1 %all_to_all.11 = f32[32,2,128]{2,1,0:T(2,128)S(1)} all-to-all(f32[32,2,128]{2,1,0:T(2,128)S(1)} %bitcast.2), channel_id=1, replica_groups=mesh['gz'=8,'xy'=4] {'gz','xy'}, dimensions={0} | all-to-all | bytes 65536 | tf_op jit(solution)/shard_map/all_to_all | solution.py:449
  21.2 1.0 %relax.1 = (f32[2,1,1,4]{3,2,1,0:T(1,128)}, f32[2,1,4,8]{3,2,1,0:T(4,128)}) custom-call(f32[64,128]{1,0:T(8,128)S(1)} %bitcast.3, f32[3,8,128]{2,1,0:T(8,128)S(1)} %get-tuple-element.9.own_aux_ref), custom_call_target="tpu_custom_call" | custom-call | bytes 1000 | tf_op jit(solution)/shard_map/relax/pallas_call | solution.py:450
  (1 shorter events, 0.0 us)
Async XLA Ops:
  0.6 8.1 %collective-permute-start.2 = (bf16[1,160,640]{2,1,0:T(8,128)(2,1)}, bf16[1,160,640]{2,1,0:T(8,128)(2,1)S(1)}, u32[]{:S(2)}, u32[]{:S(2)}) collective-permute-start(bf16[1,160,640]{2,1,0:T(8,128)(2,1)} %own_ref.3), channel_id=1, source_target_pairs={{4,0},{0,1},{1,5},{5,4},{12,8},{8,9},{9,13},{13,12},{20,16},{16,17... | collective-permute-start | bytes 614408 | tf_op jit(solution)/shard_map/ppermute | solution.py:409
  1.1 8.1 %collective-permute-start.3 = (bf16[1,160,640]{2,1,0:T(8,128)(2,1)}, bf16[1,160,640]{2,1,0:T(8,128)(2,1)S(1)}, u32[]{:S(2)}, u32[]{:S(2)}) collective-permute-start(bf16[1,160,640]{2,1,0:T(8,128)(2,1)} %own_ref.3), channel_id=1, source_target_pairs={{1,9},{9,17},{17,25},{25,24},{24,16},{16,8},{8,0},{0,1},{5,13},{13... | collective-permute-start | bytes 614408 | tf_op jit(solution)/shard_map/ppermute | solution.py:410
  3.9 5.3 %collective-permute-start.1 = (s32[1,4,4]{2,1,0:T(4,128)S(1)}, s32[1,4,4]{2,1,0:T(4,128)S(1)}, u32[]{:S(2)}, u32[]{:S(2)}) collective-permute-start(s32[1,4,4]{2,1,0:T(4,128)S(1)} %pad_add_fusion.codes_ref), channel_id=1, source_target_pairs={{1,9},{9,17},{17,25},{25,24},{24,16},{16,8},{8,0},{0,1},{5,13},{13... | collective-permute-start | bytes 200 | tf_op jit(solution)/shard_map/ppermute | solution.py:411
  5.2 3.6 %collective-permute-start = (s32[1,4,4]{2,1,0:T(4,128)S(1)}, s32[1,4,4]{2,1,0:T(4,128)S(1)}, u32[]{:S(2)}, u32[]{:S(2)}) collective-permute-start(s32[1,4,4]{2,1,0:T(4,128)S(1)} %copy_codes.1), channel_id=1, source_target_pairs={{4,0},{0,1},{1,5},{5,4},{12,8},{8,9},{9,13},{13,12},{20,16},{16,17... | collective-permute-start | bytes 200 | tf_op jit(solution)/shard_map/ppermute | solution.py:424
  7.0 0.9 %copy-start = (bf16[1,160,640]{2,1,0:T(8,128)(2,1)S(1)}, bf16[1,160,640]{2,1,0:T(8,128)(2,1)}, u32[]{:S(2)}) copy-start(bf16[1,160,640]{2,1,0:T(8,128)(2,1)} %own_ref.3) | copy-start | bytes 614404

commit v10 on v9

--- a/solution.py
+++ b/solution.py
@@ -103,11 +103,14 @@
     again_ref[...] = codes_ref[...]
 
 
-def move(peaks, rows_ref, across_ref, image_ref, moved_ref, ready=None):
+def move(peaks, rows_ref, across_ref, image_ref, moved_ref, ready=None, downs_ref=None):
     size = PATCH_SIZE
     cols = len(peaks)
     downs = []
     for j, base, width, _ in windows(cols, size):
+        if downs_ref is not None:
+            downs.append(downs_ref[peaks[j] // 5 * cols + j])
+            continue
         window = image_ref[0, :, base : base + width]
         down = jnp.dot(rows_ref[peaks[j] // 5], window, preferred_element_type=jnp.float32)
         downs.append(down.astype(jnp.bfloat16))
@@ -145,12 +148,21 @@
     return down, up, down & (section + 2 < lax.axis_size("gz")), up & (section > 1)
 
 
-def move_own(codes_ref, rows_ref, across_ref, own_ref, moved_ref, aux_ref):
+def move_own(codes_ref, rows_ref, across_ref, own_ref, moved_ref, aux_ref, downs_ref):
     codes = codes_ref[0]
+    cols = codes.shape[1]
     peaks = peaks_of(codes)
     splat_weights(codes.astype(jnp.float32), aux_ref)
-    down, _, _, _ = roles()
+    down, up, _, _ = roles()
     pl.when(down)(lambda: move(peaks, rows_ref, across_ref, own_ref, moved_ref))
+
+    @pl.when(up)
+    def _():
+        for j, base, width, _ in windows(cols, PATCH_SIZE):
+            window = own_ref[0, :, base : base + width]
+            for k in range(2 * PEAK + 1):
+                moved = jnp.dot(rows_ref[k], window, preferred_element_type=jnp.float32)
+                downs_ref[k * cols + j] = moved.astype(jnp.bfloat16)
 
 
 def stage(second_ref, held_ref):
@@ -217,37 +229,41 @@
     return jnp.broadcast_to(row, (SUBLANES, LANES))
 
 
-def moved_sums(peaks, rows_ref, across_ref, image_ref, second_ref, moved_ref, held_ref):
+def moved_sums(
+    peaks, rows_ref, across_ref, image_ref, second_ref, moved_ref, held_ref, downs_ref=None
+):
     stage(second_ref, held_ref)
     total = no_sums()
     move(
         peaks, rows_ref, across_ref, image_ref, moved_ref,
-        lambda tile: add_tile(tile, moved_ref, held_ref, total),
+        lambda tile: add_tile(tile, moved_ref, held_ref, total), downs_ref,
     )
     return over_lanes(total)
 
 
 def pairs(
-    own_moved_ref, own_aux_ref, beside_ref, rows_ref, across_ref, image_ref, own_ref,
+    own_moved_ref, own_aux_ref, downs_ref, beside_ref, rows_ref, across_ref, image_ref,
     row_ref, moved_ref, held_ref, aux_ref,
 ):
-    cols = own_ref.shape[2] // PATCH_SIZE
+    cols = image_ref.shape[2] // PATCH_SIZE
     down, up, _, _ = roles()
 
     @pl.when(down)
     def _():
         stage(image_ref, held_ref)
         total = no_sums()
-        for tile in range(own_ref.shape[2] // LANES):
+        for tile in range(image_ref.shape[2] // LANES):
             add_tile(tile, own_moved_ref, held_ref, total)
         row_ref[...] = splat_row(over_lanes(total), own_aux_ref, cols)
 
     @pl.when(up)
     def _():
         splat_weights(beside_ref[0].astype(jnp.float32), aux_ref)
-        peaks = peaks_of(beside_ref[0])
-        corr = moved_sums(peaks, rows_ref, across_ref, image_ref, own_ref, moved_ref, held_ref)
-        row_ref[...] = splat_row(corr, aux_ref, cols)
+        back = [(2 * PEAK + 1) ** 2 - 1 - peak for peak in peaks_of(beside_ref[0])]
+        corr = moved_sums(
+            back, rows_ref, across_ref, None, image_ref, moved_ref, held_ref, downs_ref
+        )
+        row_ref[...] = splat_row(corr[::-1], aux_ref, cols)
 
     @pl.when(jnp.logical_not(down | up))
     def _():
@@ -408,7 +424,7 @@
     codes = jnp.concatenate([peak_code, cell_block, cell_offset, valid_patch], axis=1)
     image_beside = lax.ppermute(images, ("gz", "xy"), beside)
     image_along = lax.ppermute(images, ("gz", "xy"), along)
-    codes_along = lax.ppermute(codes, ("gz", "xy"), along)
+    codes_beside = lax.ppermute(codes, ("gz", "xy"), beside)
     width = max(w for _, _, w, _ in windows(cols, PATCH_SIZE))
     rows, across = call(
         bank,
@@ -417,11 +433,11 @@
             pltpu.VMEM((cols * (2 * PEAK + 3), width, width), jnp.bfloat16),
         ),
         [],
-        flops=1_000,
+        flops=1_000_000_000,
         name="bank",
     )()
     again = call(copy_codes, pltpu.VMEM(codes.shape, codes.dtype), [VMEM], name="copy_codes")
-    codes_beside = lax.ppermute(again(codes), ("gz", "xy"), beside)
+    codes_along = lax.ppermute(again(codes), ("gz", "xy"), along)
     moved_shape = (
         pltpu.VMEM((3, size, breadth), jnp.float32),
         pltpu.VMEM((3, SUBLANES, LANES), jnp.float32),
@@ -429,8 +445,9 @@
     held = [pltpu.VMEM((breadth // LANES, size + 2 * SUBLANES, LANES), jnp.float32)]
     work = [pltpu.VMEM(moved_shape[0].shape, jnp.float32)] + held
     work += [pltpu.VMEM(moved_shape[1].shape, jnp.float32)]
-    moved, aux = call(
-        move_own, moved_shape, [VMEM] * 4, flops=1_000, name="move_own"
+    downs = pltpu.VMEM(((2 * PEAK + 1) * cols, size, width), jnp.bfloat16)
+    moved, aux, downs = call(
+        move_own, moved_shape + (downs,), [VMEM] * 4, flops=1_000, name="move_own"
     )(codes, rows, across, images)
     row = call(
         pairs,
@@ -438,7 +455,7 @@
         [VMEM] * 7,
         scratch_shapes=work,
         name="pairs",
-    )(moved, aux, codes_beside, rows, across, image_beside, images)
+    )(moved, aux, downs, codes_beside, rows, across, image_beside)
     splat = call(
         neighbours,
         pltpu.VMEM((2 * devices, LANES), jnp.float32),

time: 22.4 us -> 22.1 us (0.987)
  waiting for transfers between devices: 0.19 us -> 1.14 us
  local copies, waits for them, and re-layouts: 0.93 us -> 0.01 us
  starting transfers between devices: 5.11 us -> 4.49 us
  blocking collectives: 11.1 us -> 11.4 us
    ppermute x2, waiting for transfers between devices: 0.19 us -> 1.14 us  [the longest x1 0.6 us: on_device(): codes_along = lax.ppermute(again(codes), ('gz', 'xy'), along)]
    unnamed x2, local copies, waits for them, and re-layouts: 0.93 us -> 0.01 us
    ppermute x2, starting transfers between devices: 2.6 us -> 1.98 us  [the longest x1 1.3 us: on_device(): codes_beside = lax.ppermute(codes, ('gz', 'xy'), beside)]
    all_to_all x1, blocking collectives: 11.1 us -> 11.4 us  [on_device(): gathered = lax.all_to_all(splat, ('gz', 'xy'), 0, 0, tiled=True)]
  transfers between devices with their start and end apart: 4 -> 4, of which waited for: 1 -> 2; matrix products, arithmetic and copies ran while one was open for 3% -> 3% of each run, Pallas kernels for 7% -> 8%
where the time goes in v10:
time: 22.1 us; the launch traced here: 22 us
  blocking collectives  11.4 us (52%)
  starting transfers between devices  4.49 us (20%)
  Pallas kernels  3.6 us (16%)
  waiting for transfers between devices  1.14 us (5%)
  other arithmetic  0.71 us (3%)
  between operations  0.67 us (3%)
    all_to_all x1, blocking collectives, on_device(): gathered = lax.all_to_all(splat, ('gz', 'xy'), 0, 0, tiled=True)  11.4 us
    ppermute x1, starting transfers between devices, on_device(): image_along = lax.ppermute(images, ('gz', 'xy'), along)  2.04 us
    ppermute x1, starting transfers between devices, on_device(): codes_beside = lax.ppermute(codes, ('gz', 'xy'), beside)  1.3 us
    pallas_call x1, Pallas kernels, on_device(): call(functools.partial(relax, strips), (jax.ShapeDtypeStruct((2, 1, 1, co...  0.98 us
    pallas_call x1, Pallas kernels, on_device(): call(neighbours, pltpu.VMEM((2 * devices, LANES), jnp.float32), [VMEM] *...  0.88 us
    concatenate x1, other arithmetic, on_device(): jnp.concatenate([peak_code, cell_block, cell_offset, valid_patch], axis=1)  0.71 us
    ppermute x1, starting transfers between devices, on_device(): codes_along = lax.ppermute(again(codes), ('gz', 'xy'), along)  0.68 us
    pallas_call x1, Pallas kernels, on_device(): call(move_own, moved_shape + (downs,), [VMEM] * 4, flops=1000, name='move...  0.66 us
  transfers between devices with their start and end apart: 4, of which 2 were waited for; matrix products, arithmetic and copies ran while one was open for 3% of the time, Pallas kernels for 8%

profile of v10, /device:TPU:0, one launch (start us, length us, event | category | flops | bytes accessed | tf_op | source)
XLA Modules:
  0.0 22.0 jit_solution(13694404830320706930)
XLA Ops:
  0.6 0.5 %collective-permute-start.2 = (bf16[1,160,640]{2,1,0:T(8,128)(2,1)}, bf16[1,160,640]{2,1,0:T(8,128)(2,1)S(1)}, u32[]{:S(2)}, u32[]{:S(2)}) collective-permute-start(bf16[1,160,640]{2,1,0:T(8,128)(2,1)} %own_ref.1), channel_id=1, source_target_pairs={{4,0},{0,1},{1,5},{5,4},{12,8},{8,9},{9,13},{13,12},{20,16},{16,17... | collective-permute-start | bytes 614408 | tf_op jit(solution)/shard_map/ppermute | solution.py:425
  1.1 2.0 %collective-permute-start.3 = (bf16[1,160,640]{2,1,0:T(8,128)(2,1)}, bf16[1,160,640]{2,1,0:T(8,128)(2,1)S(1)}, u32[]{:S(2)}, u32[]{:S(2)}) collective-permute-start(bf16[1,160,640]{2,1,0:T(8,128)(2,1)} %own_ref.1), channel_id=1, source_target_pairs={{1,9},{9,17},{17,25},{25,24},{24,16},{16,8},{8,0},{0,1},{5,13},{13... | collective-permute-start | bytes 614408 | tf_op jit(solution)/shard_map/ppermute | solution.py:426
  3.1 0.7 %pad_add_fusion.codes_ref = s32[1,4,4]{2,1,0:T(4,128)S(1)} fusion(s32[1,1,4]{2,1,0:T(1,128)} %param.9, s32[1,1,4]{2,1,0:T(1,128)} %param.8, s32[1,1,4]{2,1,0:T(1,128)} %param.7, s32[1,1,4]{2,1,0:T(1,128)} %param.6), kind=kLoop, calls=%fused_computation | loop fusion | flops 48 | bytes 128 | tf_op jit(solution)/shard_map/concatenate | solution.py:424
  3.9 1.3 %collective-permute-start = (s32[1,4,4]{2,1,0:T(4,128)S(1)}, s32[1,4,4]{2,1,0:T(4,128)S(1)}, u32[]{:S(2)}, u32[]{:S(2)}) collective-permute-start(s32[1,4,4]{2,1,0:T(4,128)S(1)} %pad_add_fusion.codes_ref), channel_id=1, source_target_pairs={{4,0},{0,1},{1,5},{5,4},{12,8},{8,9},{9,13},{13,12},{20,16},{16,17... | collective-permute-start | bytes 200 | tf_op jit(solution)/shard_map/ppermute | solution.py:427
  5.2 0.0 copy-start
  5.2 0.7 %collective-permute-start.1 = (s32[1,4,4]{2,1,0:T(4,128)S(1)}, s32[1,4,4]{2,1,0:T(4,128)S(1)}, u32[]{:S(2)}, u32[]{:S(2)}) collective-permute-start(s32[1,4,4]{2,1,0:T(4,128)S(1)} %copy_codes.1), channel_id=1, source_target_pairs={{1,9},{9,17},{17,25},{25,24},{24,16},{16,8},{8,0},{0,1},{5,13},{13... | collective-permute-start | bytes 200 | tf_op jit(solution)/shard_map/ppermute | solution.py:440
  5.8 0.5 %bank.1 = (bf16[5,160,160]{2,1,0:T(8,128)(2,1)S(1)}, bf16[28,256,256]{2,1,0:T(8,128)(2,1)S(1)}) custom-call(), custom_call_target="tpu_custom_call" | custom-call | flops 1000000000 | bytes 1000 | tf_op jit(solution)/shard_map/bank/pallas_call | solution.py:429
  6.3 0.0 copy-done
  6.3 0.7 %move_own.1 = (f32[3,160,640]{2,1,0:T(8,128)S(1)}, f32[3,8,128]{2,1,0:T(8,128)S(1)}, bf16[20,160,256]{2,1,0:T(8,128)(2,1)S(1)}) custom-call(s32[1,4,4]{2,1,0:T(4,128)S(1)} %pad_add_fusion.codes_ref, bf16[5,160,160]{2,1,0:T(8,128)(2,1)S(1)} %get-tuple-element.7.rows_ref, bf16[28,256,256]{2,1,0:T(8,128)(2,1)S(1)} %get-tuple-element.8.across_ref, ...), custom_call_target="tpu_custom_call" | custom-call | flops 1000 | bytes 1000 | tf_op jit(solution)/shard_map/move_own/pallas_call | solution.py:449
  7.0 0.5 %collective-permute-done.beside_ref = s32[1,4,4]{2,1,0:T(4,128)S(1)} collective-permute-done((s32[1,4,4]{2,1,0:T(4,128)S(1)}, s32[1,4,4]{2,1,0:T(4,128)S(1)}, u32[]{:S(2)}, u32[]{:S(2)}) %collective-permute-start) | collective-permute-done | bytes 96 | tf_op jit(solution)/shard_map/ppermute | solution.py:427
  7.6 0.0 collective-permute-done.2.image_ref
  7.6 0.6 %pairs.1.row_ref = f32[8,128]{1,0:T(8,128)S(1)} custom-call(f32[3,160,640]{2,1,0:T(8,128)S(1)} %get-tuple-element.9.own_moved_ref, f32[3,8,128]{2,1,0:T(8,128)S(1)} %get-tuple-element.10.own_aux_ref, bf16[20,160,256]{2,1,0:T(8,128)(2,1)S(1)} %get-tuple-element.11.downs_ref, s32[1,4,4]{2,1,0:T(4,128)S(1)} %collective-permute-done.beside_ref, ...), custom_call_target="tpu_custom_call" | custom-call | bytes 1000 | tf_op jit(solution)/shard_map/pairs/pallas_call | solution.py:452
  8.1 0.6 %collective-permute-done.1.along_ref = s32[1,4,4]{2,1,0:T(4,128)S(1)} collective-permute-done((s32[1,4,4]{2,1,0:T(4,128)S(1)}, s32[1,4,4]{2,1,0:T(4,128)S(1)}, u32[]{:S(2)}, u32[]{:S(2)}) %collective-permute-start.1) | collective-permute-done | bytes 96 | tf_op jit(solution)/shard_map/ppermute | solution.py:440
  8.7 0.0 collective-permute-done.3.second_ref
  8.8 0.9 %neighbours.1 = f32[64,128]{1,0:T(8,128)S(1)} custom-call(s32[1,4,4]{2,1,0:T(4,128)S(1)} %collective-permute-done.beside_ref, s32[1,4,4]{2,1,0:T(4,128)S(1)} %collective-permute-done.1.along_ref, bf16[5,160,160]{2,1,0:T(8,128)(2,1)S(1)} %get-tuple-element.7.rows_ref, bf16[28,256,256]{2,1,0:T(8,128)(2,1)S(1)} %get-tuple-element.8.across_ref, ...), custom_call_target="tpu_custom_call" | custom-call | bytes 1000 | tf_op jit(solution)/shard_map/neighbours/pallas_call | solution.py:459
  9.6 11.4 %all_to_all.11 = f32[32,2,128]{2,1,0:T(2,128)S(1)} all-to-all(f32[32,2,128]{2,1,0:T(2,128)S(1)} %bitcast.2), channel_id=1, replica_groups=mesh['gz'=8,'xy'=4] {'gz','xy'}, dimensions={0} | all-to-all | bytes 65536 | tf_op jit(solution)/shard_map/all_to_all | solution.py:466
  21.0 1.0 %relax.1 = (f32[2,1,1,4]{3,2,1,0:T(1,128)}, f32[2,1,4,8]{3,2,1,0:T(4,128)}) custom-call(f32[64,128]{1,0:T(8,128)S(1)} %bitcast.3, f32[3,8,128]{2,1,0:T(8,128)S(1)} %get-tuple-element.10.own_aux_ref), custom_call_target="tpu_custom_call" | custom-call | bytes 1000 | tf_op jit(solution)/shard_map/relax/pallas_call | solution.py:467
  (1 shorter events, 0.0 us)
Async XLA Ops:
  0.6 6.9 %collective-permute-start.2 = (bf16[1,160,640]{2,1,0:T(8,128)(2,1)}, bf16[1,160,640]{2,1,0:T(8,128)(2,1)S(1)}, u32[]{:S(2)}, u32[]{:S(2)}) collective-permute-start(bf16[1,160,640]{2,1,0:T(8,128)(2,1)} %own_ref.1), channel_id=1, source_target_pairs={{4,0},{0,1},{1,5},{5,4},{12,8},{8,9},{9,13},{13,12},{20,16},{16,17... | collective-permute-start | bytes 614408 | tf_op jit(solution)/shard_map/ppermute | solution.py:425
  1.1 7.7 %collective-permute-start.3 = (bf16[1,160,640]{2,1,0:T(8,128)(2,1)}, bf16[1,160,640]{2,1,0:T(8,128)(2,1)S(1)}, u32[]{:S(2)}, u32[]{:S(2)}) collective-permute-start(bf16[1,160,640]{2,1,0:T(8,128)(2,1)} %own_ref.1), channel_id=1, source_target_pairs={{1,9},{9,17},{17,25},{25,24},{24,16},{16,8},{8,0},{0,1},{5,13},{13... | collective-permute-start | bytes 614408 | tf_op jit(solution)/shard_map/ppermute | solution.py:426
  3.9 3.7 %collective-permute-start = (s32[1,4,4]{2,1,0:T(4,128)S(1)}, s32[1,4,4]{2,1,0:T(4,128)S(1)}, u32[]{:S(2)}, u32[]{:S(2)}) collective-permute-start(s32[1,4,4]{2,1,0:T(4,128)S(1)} %pad_add_fusion.codes_ref), channel_id=1, source_target_pairs={{4,0},{0,1},{1,5},{5,4},{12,8},{8,9},{9,13},{13,12},{20,16},{16,17... | collective-permute-start | bytes 200 | tf_op jit(solution)/shard_map/ppermute | solution.py:427
  5.2 1.2 %copy-start = (bf16[1,160,640]{2,1,0:T(8,128)(2,1)S(1)}, bf16[1,160,640]{2,1,0:T(8,128)(2,1)}, u32[]{:S(2)}) copy-start(bf16[1,160,640]{2,1,0:T(8,128)(2,1)} %own_ref.1) | copy-start | bytes 614404
  5.2 3.6 %collective-permute-start.1 = (s32[1,4,4]{2,1,0:T(4,128)S(1)}, s32[1,4,4]{2,1,0:T(4,128)S(1)}, u32[]{:S(2)}, u32[]{:S(2)}) collective-permute-start(s32[1,4,4]{2,1,0:T(4,128)S(1)} %copy_codes.1), channel_id=1, source_target_pairs={{1,9},{9,17},{17,25},{25,24},{24,16},{16,8},{8,0},{0,1},{5,13},{13... | collective-permute-start | bytes 200 | tf_op jit(solution)/shard_map/ppermute | solution.py:440

commit v11 on v10

--- a/solution.py
+++ b/solution.py
@@ -182,10 +182,10 @@
     size = PATCH_SIZE
     sub = iota((SUBLANES, LANES), 0)
     lane = iota((SUBLANES, LANES), 1)
-    base = tile * LANES
+    base = tile * LANES if isinstance(tile, int) else pl.multiple_of(tile * LANES, LANES)
     sums = [None] * LAGS
     for top in range(0, size, SUBLANES):
-        first = [moved_ref[b, top : top + SUBLANES, base : base + LANES] for b in range(3)]
+        first = [moved_ref[b, top : top + SUBLANES, pl.ds(base, LANES)] for b in range(3)]
         for a in range(3):
             start = SUBLANES + top + a - 1
             later = held_ref[tile, start : start + SUBLANES, :]
@@ -238,48 +238,57 @@
         peaks, rows_ref, across_ref, image_ref, moved_ref,
         lambda tile: add_tile(tile, moved_ref, held_ref, total), downs_ref,
     )
-    return over_lanes(total)
+    return total
 
 
 def pairs(
     own_moved_ref, own_aux_ref, downs_ref, beside_ref, rows_ref, across_ref, image_ref,
-    row_ref, moved_ref, held_ref, aux_ref,
+    total_ref, used_ref, moved_ref, held_ref,
 ):
-    cols = image_ref.shape[2] // PATCH_SIZE
     down, up, _, _ = roles()
 
     @pl.when(down)
     def _():
         stage(image_ref, held_ref)
-        total = no_sums()
-        for tile in range(image_ref.shape[2] // LANES):
+
+        def body(tile, total):
+            total = list(total)
             add_tile(tile, own_moved_ref, held_ref, total)
-        row_ref[...] = splat_row(over_lanes(total), own_aux_ref, cols)
+            return tuple(total)
+
+        total = lax.fori_loop(0, image_ref.shape[2] // LANES, body, tuple(no_sums()))
+        for k in range(LAGS):
+            total_ref[k] = total[k]
+        used_ref[...] = own_aux_ref[...]
 
     @pl.when(up)
     def _():
-        splat_weights(beside_ref[0].astype(jnp.float32), aux_ref)
+        splat_weights(beside_ref[0].astype(jnp.float32), used_ref)
         back = [(2 * PEAK + 1) ** 2 - 1 - peak for peak in peaks_of(beside_ref[0])]
-        corr = moved_sums(
+        total = moved_sums(
             back, rows_ref, across_ref, None, image_ref, moved_ref, held_ref, downs_ref
         )
-        row_ref[...] = splat_row(corr[::-1], aux_ref, cols)
+        for k in range(LAGS):
+            total_ref[k] = total[LAGS - 1 - k]
 
     @pl.when(jnp.logical_not(down | up))
     def _():
-        row_ref[...] = jnp.zeros((SUBLANES, LANES), jnp.float32)
+        total_ref[...] = jnp.zeros(total_ref.shape, jnp.float32)
+        used_ref[...] = jnp.zeros(used_ref.shape, jnp.float32)
 
 
 def neighbours(
-    beside_ref, along_ref, rows_ref, across_ref, image_ref, second_ref, row_ref,
+    beside_ref, along_ref, rows_ref, across_ref, image_ref, second_ref, total_ref, used_ref,
     splat_ref, moved_ref, held_ref, aux_ref,
 ):
     _, _, straight, turned = roles()
     some = straight | turned
     even = lax.rem(iota(splat_ref.shape, 0), 2) == 0
+    cols = image_ref.shape[2] // PATCH_SIZE
 
     def spread(row):
-        full = [jnp.broadcast_to(r[:1], splat_ref.shape) for r in (row_ref[...], row)]
+        pair = splat_row(over_lanes([total_ref[k] for k in range(LAGS)]), used_ref, cols)
+        full = [jnp.broadcast_to(r[:1], splat_ref.shape) for r in (pair, row)]
         splat_ref[...] = jnp.where(even, *full)
 
     @pl.when(some)
@@ -288,7 +297,8 @@
         back = (2 * PEAK + 1) ** 2 - 1
         peaks = [jnp.where(straight, peak, back - peak) for peak in peaks_of(codes)]
         splat_weights(codes.astype(jnp.float32), aux_ref)
-        corr = moved_sums(peaks, rows_ref, across_ref, image_ref, second_ref, moved_ref, held_ref)
+        total = moved_sums(peaks, rows_ref, across_ref, image_ref, second_ref, moved_ref, held_ref)
+        corr = over_lanes(total)
         corr = [jnp.where(straight, value, other) for value, other in zip(corr, corr[::-1])]
         spread(splat_row(corr, aux_ref, len(peaks)))
 
@@ -449,20 +459,20 @@
     moved, aux, downs = call(
         move_own, moved_shape + (downs,), [VMEM] * 4, flops=1_000, name="move_own"
     )(codes, rows, across, images)
-    row = call(
+    total, used = call(
         pairs,
-        pltpu.VMEM((SUBLANES, LANES), jnp.float32),
+        (pltpu.VMEM((LAGS, SUBLANES, LANES), jnp.float32), moved_shape[1]),
         [VMEM] * 7,
-        scratch_shapes=work,
+        scratch_shapes=work[:2],
         name="pairs",
     )(moved, aux, downs, codes_beside, rows, across, image_beside)
     splat = call(
         neighbours,
         pltpu.VMEM((2 * devices, LANES), jnp.float32),
-        [VMEM] * 7,
+        [VMEM] * 8,
         scratch_shapes=work,
         name="neighbours",
-    )(codes_beside, codes_along, rows, across, image_beside, image_along, row)
+    )(codes_beside, codes_along, rows, across, image_beside, image_along, total, used)
     gathered = lax.all_to_all(splat, ("gz", "xy"), 0, 0, tiled=True)
     flow, node_shift = call(
         functools.partial(relax, strips),

time: 22.1 us -> 22.1 us (level)
  transfers between devices with their start and end apart: 4 -> 4, of which waited for: 2 -> 2; matrix products, arithmetic and copies ran while one was open for 3% -> 3% of each run, Pallas kernels for 8% -> 7%
where the time goes in v11:
time: 22.1 us; the launch traced here: 21.9 us
  blocking collectives  11.3 us (51%)
  starting transfers between devices  4.49 us (20%)
  Pallas kernels  3.44 us (16%)
  waiting for transfers between devices  1.33 us (6%)
  other arithmetic  0.71 us (3%)
  between operations  0.67 us (3%)
    all_to_all x1, blocking collectives, on_device(): gathered = lax.all_to_all(splat, ('gz', 'xy'), 0, 0, tiled=True)  11.3 us
    ppermute x1, starting transfers between devices, on_device(): image_along = lax.ppermute(images, ('gz', 'xy'), along)  2.04 us
    ppermute x1, starting transfers between devices, on_device(): codes_beside = lax.ppermute(codes, ('gz', 'xy'), beside)  1.3 us
    pallas_call x1, Pallas kernels, on_device(): call(functools.partial(relax, strips), (jax.ShapeDtypeStruct((2, 1, 1, co...  0.98 us
    pallas_call x1, Pallas kernels, on_device(): call(neighbours, pltpu.VMEM((2 * devices, LANES), jnp.float32), [VMEM] *...  0.9 us
    ppermute x1, waiting for transfers between devices, on_device(): codes_along = lax.ppermute(again(codes), ('gz', 'xy'), along)  0.79 us
    concatenate x1, other arithmetic, on_device(): jnp.concatenate([peak_code, cell_block, cell_offset, valid_patch], axis=1)  0.71 us
    ppermute x1, starting transfers between devices, on_device(): codes_along = lax.ppermute(again(codes), ('gz', 'xy'), along)  0.68 us
  transfers between devices with their start and end apart: 4, of which 2 were waited for; matrix products, arithmetic and copies ran while one was open for 3% of the time, Pallas kernels for 7%

profile of v11, /device:TPU:0, one launch (start us, length us, event | category | flops | bytes accessed | tf_op | source)
XLA Modules:
  0.0 21.9 jit_solution(2184857675635084470)
XLA Ops:
  0.6 0.5 %collective-permute-start.2 = (bf16[1,160,640]{2,1,0:T(8,128)(2,1)}, bf16[1,160,640]{2,1,0:T(8,128)(2,1)S(1)}, u32[]{:S(2)}, u32[]{:S(2)}) collective-permute-start(bf16[1,160,640]{2,1,0:T(8,128)(2,1)} %own_ref.1), channel_id=1, source_target_pairs={{4,0},{0,1},{1,5},{5,4},{12,8},{8,9},{9,13},{13,12},{20,16},{16,17... | collective-permute-start | bytes 614408 | tf_op jit(solution)/shard_map/ppermute | solution.py:435
  1.1 2.0 %collective-permute-start.3 = (bf16[1,160,640]{2,1,0:T(8,128)(2,1)}, bf16[1,160,640]{2,1,0:T(8,128)(2,1)S(1)}, u32[]{:S(2)}, u32[]{:S(2)}) collective-permute-start(bf16[1,160,640]{2,1,0:T(8,128)(2,1)} %own_ref.1), channel_id=1, source_target_pairs={{1,9},{9,17},{17,25},{25,24},{24,16},{16,8},{8,0},{0,1},{5,13},{13... | collective-permute-start | bytes 614408 | tf_op jit(solution)/shard_map/ppermute | solution.py:436
  3.1 0.7 %pad_add_fusion.codes_ref = s32[1,4,4]{2,1,0:T(4,128)S(1)} fusion(s32[1,1,4]{2,1,0:T(1,128)} %param.9, s32[1,1,4]{2,1,0:T(1,128)} %param.8, s32[1,1,4]{2,1,0:T(1,128)} %param.7, s32[1,1,4]{2,1,0:T(1,128)} %param.6), kind=kLoop, calls=%fused_computation | loop fusion | flops 48 | bytes 128 | tf_op jit(solution)/shard_map/concatenate | solution.py:434
  3.9 1.3 %collective-permute-start = (s32[1,4,4]{2,1,0:T(4,128)S(1)}, s32[1,4,4]{2,1,0:T(4,128)S(1)}, u32[]{:S(2)}, u32[]{:S(2)}) collective-permute-start(s32[1,4,4]{2,1,0:T(4,128)S(1)} %pad_add_fusion.codes_ref), channel_id=1, source_target_pairs={{4,0},{0,1},{1,5},{5,4},{12,8},{8,9},{9,13},{13,12},{20,16},{16,17... | collective-permute-start | bytes 200 | tf_op jit(solution)/shard_map/ppermute | solution.py:437
  5.2 0.0 copy-start
  5.2 0.7 %collective-permute-start.1 = (s32[1,4,4]{2,1,0:T(4,128)S(1)}, s32[1,4,4]{2,1,0:T(4,128)S(1)}, u32[]{:S(2)}, u32[]{:S(2)}) collective-permute-start(s32[1,4,4]{2,1,0:T(4,128)S(1)} %copy_codes.1), channel_id=1, source_target_pairs={{1,9},{9,17},{17,25},{25,24},{24,16},{16,8},{8,0},{0,1},{5,13},{13... | collective-permute-start | bytes 200 | tf_op jit(solution)/shard_map/ppermute | solution.py:450
  5.8 0.5 %bank.1 = (bf16[5,160,160]{2,1,0:T(8,128)(2,1)S(1)}, bf16[28,256,256]{2,1,0:T(8,128)(2,1)S(1)}) custom-call(), custom_call_target="tpu_custom_call" | custom-call | flops 1000000000 | bytes 1000 | tf_op jit(solution)/shard_map/bank/pallas_call | solution.py:439
  6.3 0.0 copy-done
  6.3 0.7 %move_own.1 = (f32[3,160,640]{2,1,0:T(8,128)S(1)}, f32[3,8,128]{2,1,0:T(8,128)S(1)}, bf16[20,160,256]{2,1,0:T(8,128)(2,1)S(1)}) custom-call(s32[1,4,4]{2,1,0:T(4,128)S(1)} %pad_add_fusion.codes_ref, bf16[5,160,160]{2,1,0:T(8,128)(2,1)S(1)} %get-tuple-element.9.rows_ref, bf16[28,256,256]{2,1,0:T(8,128)(2,1)S(1)} %get-tuple-element.10.across_ref, ...), custom_call_target="tpu_custom_call" | custom-call | flops 1000 | bytes 1000 | tf_op jit(solution)/shard_map/move_own/pallas_call | solution.py:459
  7.0 0.5 %collective-permute-done.beside_ref = s32[1,4,4]{2,1,0:T(4,128)S(1)} collective-permute-done((s32[1,4,4]{2,1,0:T(4,128)S(1)}, s32[1,4,4]{2,1,0:T(4,128)S(1)}, u32[]{:S(2)}, u32[]{:S(2)}) %collective-permute-start) | collective-permute-done | bytes 96 | tf_op jit(solution)/shard_map/ppermute | solution.py:437
  7.6 0.0 collective-permute-done.2.image_ref
  7.6 0.4 %pairs.1 = (f32[9,8,128]{2,1,0:T(8,128)S(1)}, f32[3,8,128]{2,1,0:T(8,128)S(1)}) custom-call(f32[3,160,640]{2,1,0:T(8,128)S(1)} %get-tuple-element.11.own_moved_ref, f32[3,8,128]{2,1,0:T(8,128)S(1)} %get-tuple-element.12.own_aux_ref, bf16[20,160,256]{2,1,0:T(8,128)(2,1)S(1)} %get-tuple-element.13.downs_ref, s32[1,4,4]{2,1,0:T(4,128)S(1)} %collective-permute-done.beside_ref, ...), custom_call_target="tpu_custom_call" | custom-call | bytes 1000 | tf_op jit(solution)/shard_map/pairs/pallas_call | solution.py:462
  8.0 0.8 %collective-permute-done.1.along_ref = s32[1,4,4]{2,1,0:T(4,128)S(1)} collective-permute-done((s32[1,4,4]{2,1,0:T(4,128)S(1)}, s32[1,4,4]{2,1,0:T(4,128)S(1)}, u32[]{:S(2)}, u32[]{:S(2)}) %collective-permute-start.1) | collective-permute-done | bytes 96 | tf_op jit(solution)/shard_map/ppermute | solution.py:450
  8.7 0.0 collective-permute-done.3.second_ref
  8.8 0.9 %neighbours.1 = f32[64,128]{1,0:T(8,128)S(1)} custom-call(s32[1,4,4]{2,1,0:T(4,128)S(1)} %collective-permute-done.beside_ref, s32[1,4,4]{2,1,0:T(4,128)S(1)} %collective-permute-done.1.along_ref, bf16[5,160,160]{2,1,0:T(8,128)(2,1)S(1)} %get-tuple-element.9.rows_ref, bf16[28,256,256]{2,1,0:T(8,128)(2,1)S(1)} %get-tuple-element.10.across_ref, ...), custom_call_target="tpu_custom_call" | custom-call | bytes 1000 | tf_op jit(solution)/shard_map/neighbours/pallas_call | solution.py:469
  9.7 11.3 %all_to_all.11 = f32[32,2,128]{2,1,0:T(2,128)S(1)} all-to-all(f32[32,2,128]{2,1,0:T(2,128)S(1)} %bitcast.2), channel_id=1, replica_groups=mesh['gz'=8,'xy'=4] {'gz','xy'}, dimensions={0} | all-to-all | bytes 65536 | tf_op jit(solution)/shard_map/all_to_all | solution.py:476
  21.0 1.0 %relax.1 = (f32[2,1,1,4]{3,2,1,0:T(1,128)}, f32[2,1,4,8]{3,2,1,0:T(4,128)}) custom-call(f32[64,128]{1,0:T(8,128)S(1)} %bitcast.3, f32[3,8,128]{2,1,0:T(8,128)S(1)} %get-tuple-element.12.own_aux_ref), custom_call_target="tpu_custom_call" | custom-call | bytes 1000 | tf_op jit(solution)/shard_map/relax/pallas_call | solution.py:477
  (1 shorter events, 0.0 us)
Async XLA Ops:
  0.6 6.9 %collective-permute-start.2 = (bf16[1,160,640]{2,1,0:T(8,128)(2,1)}, bf16[1,160,640]{2,1,0:T(8,128)(2,1)S(1)}, u32[]{:S(2)}, u32[]{:S(2)}) collective-permute-start(bf16[1,160,640]{2,1,0:T(8,128)(2,1)} %own_ref.1), channel_id=1, source_target_pairs={{4,0},{0,1},{1,5},{5,4},{12,8},{8,9},{9,13},{13,12},{20,16},{16,17... | collective-permute-start | bytes 614408 | tf_op jit(solution)/shard_map/ppermute | solution.py:435
  1.1 7.7 %collective-permute-start.3 = (bf16[1,160,640]{2,1,0:T(8,128)(2,1)}, bf16[1,160,640]{2,1,0:T(8,128)(2,1)S(1)}, u32[]{:S(2)}, u32[]{:S(2)}) collective-permute-start(bf16[1,160,640]{2,1,0:T(8,128)(2,1)} %own_ref.1), channel_id=1, source_target_pairs={{1,9},{9,17},{17,25},{25,24},{24,16},{16,8},{8,0},{0,1},{5,13},{13... | collective-permute-start | bytes 614408 | tf_op jit(solution)/shard_map/ppermute | solution.py:436
  3.9 3.7 %collective-permute-start = (s32[1,4,4]{2,1,0:T(4,128)S(1)}, s32[1,4,4]{2,1,0:T(4,128)S(1)}, u32[]{:S(2)}, u32[]{:S(2)}) collective-permute-start(s32[1,4,4]{2,1,0:T(4,128)S(1)} %pad_add_fusion.codes_ref), channel_id=1, source_target_pairs={{4,0},{0,1},{1,5},{5,4},{12,8},{8,9},{9,13},{13,12},{20,16},{16,17... | collective-permute-start | bytes 200 | tf_op jit(solution)/shard_map/ppermute | solution.py:437
  5.2 1.2 %copy-start = (bf16[1,160,640]{2,1,0:T(8,128)(2,1)S(1)}, bf16[1,160,640]{2,1,0:T(8,128)(2,1)}, u32[]{:S(2)}) copy-start(bf16[1,160,640]{2,1,0:T(8,128)(2,1)} %own_ref.1) | copy-start | bytes 614404
  5.2 3.6 %collective-permute-start.1 = (s32[1,4,4]{2,1,0:T(4,128)S(1)}, s32[1,4,4]{2,1,0:T(4,128)S(1)}, u32[]{:S(2)}, u32[]{:S(2)}) collective-permute-start(s32[1,4,4]{2,1,0:T(4,128)S(1)} %copy_codes.1), channel_id=1, source_target_pairs={{1,9},{9,17},{17,25},{25,24},{24,16},{16,8},{8,0},{0,1},{5,13},{13... | collective-permute-start | bytes 200 | tf_op jit(solution)/shard_map/ppermute | solution.py:450

commit v12 on v11

--- a/solution.py
+++ b/solution.py
@@ -232,7 +232,8 @@
 def moved_sums(
     peaks, rows_ref, across_ref, image_ref, second_ref, moved_ref, held_ref, downs_ref=None
 ):
-    stage(second_ref, held_ref)
+    if second_ref is not None:
+        stage(second_ref, held_ref)
     total = no_sums()
     move(
         peaks, rows_ref, across_ref, image_ref, moved_ref,
@@ -243,7 +244,7 @@
 
 def pairs(
     own_moved_ref, own_aux_ref, downs_ref, beside_ref, rows_ref, across_ref, image_ref,
-    total_ref, used_ref, moved_ref, held_ref,
+    total_ref, used_ref, held_ref, moved_ref,
 ):
     down, up, _, _ = roles()
 
@@ -278,8 +279,8 @@
 
 
 def neighbours(
-    beside_ref, along_ref, rows_ref, across_ref, image_ref, second_ref, total_ref, used_ref,
-    splat_ref, moved_ref, held_ref, aux_ref,
+    beside_ref, along_ref, rows_ref, across_ref, image_ref, held_ref, total_ref, used_ref,
+    splat_ref, moved_ref, aux_ref,
 ):
     _, _, straight, turned = roles()
     some = straight | turned
@@ -295,11 +296,11 @@
     def _():
         codes = jnp.where(straight, beside_ref[0], along_ref[0])
         back = (2 * PEAK + 1) ** 2 - 1
-        peaks = [jnp.where(straight, peak, back - peak) for peak in peaks_of(codes)]
+        peaks = [jnp.where(straight, back - peak, peak) for peak in peaks_of(codes)]
         splat_weights(codes.astype(jnp.float32), aux_ref)
-        total = moved_sums(peaks, rows_ref, across_ref, image_ref, second_ref, moved_ref, held_ref)
+        total = moved_sums(peaks, rows_ref, across_ref, image_ref, None, moved_ref, held_ref)
         corr = over_lanes(total)
-        corr = [jnp.where(straight, value, other) for value, other in zip(corr, corr[::-1])]
+        corr = [jnp.where(straight, other, value) for value, other in zip(corr, corr[::-1])]
         spread(splat_row(corr, aux_ref, len(peaks)))
 
     @pl.when(jnp.logical_not(some))
@@ -395,11 +396,14 @@
             later[o] = tuple(moved)
         now = later
     place = iota((SUBLANES, NODE_COLS), 0) + iota((SUBLANES, NODE_COLS), 1) == NODE_COLS - 1
+    line = iota((BAND_ROWS, NODE_COLS), 0)
     for q in range(2):
+        field = jnp.zeros((BAND_ROWS, NODE_COLS), jnp.float32)
         for i in range(BAND_ROWS):
             spot = BAND + (i + 1) * NODE_COLS - 1
             column = jnp.where(place, now[0][q][:, spot : spot + 1], 0.0)
-            out_ref[q, 0, i : i + 1, :] = jnp.sum(column, axis=0, keepdims=True)
+            field = jnp.where(line == i, jnp.sum(column, axis=0, keepdims=True), field)
+        out_ref[q, 0] = field
 
 
 def call(kernel, out_shape, in_specs, flops=0, **settings):
@@ -459,20 +463,20 @@
     moved, aux, downs = call(
         move_own, moved_shape + (downs,), [VMEM] * 4, flops=1_000, name="move_own"
     )(codes, rows, across, images)
-    total, used = call(
+    total, used, staged = call(
         pairs,
-        (pltpu.VMEM((LAGS, SUBLANES, LANES), jnp.float32), moved_shape[1]),
+        (pltpu.VMEM((LAGS, SUBLANES, LANES), jnp.float32), moved_shape[1], held[0]),
         [VMEM] * 7,
-        scratch_shapes=work[:2],
+        scratch_shapes=work[:1],
         name="pairs",
     )(moved, aux, downs, codes_beside, rows, across, image_beside)
     splat = call(
         neighbours,
         pltpu.VMEM((2 * devices, LANES), jnp.float32),
         [VMEM] * 8,
-        scratch_shapes=work,
+        scratch_shapes=[work[0], work[2]],
         name="neighbours",
-    )(codes_beside, codes_along, rows, across, image_beside, image_along, total, used)
+    )(codes_beside, codes_along, rows, across, image_along, staged, total, used)
     gathered = lax.all_to_all(splat, ("gz", "xy"), 0, 0, tiled=True)
     flow, node_shift = call(
         functools.partial(relax, strips),

time: 22.1 us -> 22.1 us (level)
  no operation moved by 1% of the time
where the time goes in v12:
time: 22.1 us; the launch traced here: 22 us
  blocking collectives  11.3 us (51%)
  starting transfers between devices  4.49 us (20%)
  Pallas kernels  3.44 us (16%)
  waiting for transfers between devices  1.32 us (6%)
  other arithmetic  0.71 us (3%)
  between operations  0.67 us (3%)
    all_to_all x1, blocking collectives, on_device(): gathered = lax.all_to_all(splat, ('gz', 'xy'), 0, 0, tiled=True)  11.3 us
    ppermute x1, starting transfers between devices, on_device(): image_along = lax.ppermute(images, ('gz', 'xy'), along)  2.04 us
    ppermute x1, starting transfers between devices, on_device(): codes_beside = lax.ppermute(codes, ('gz', 'xy'), beside)  1.3 us
    pallas_call x1, Pallas kernels, on_device(): call(functools.partial(relax, strips), (jax.ShapeDtypeStruct((2, 1, 1, co...  0.98 us
    pallas_call x1, Pallas kernels, on_device(): call(neighbours, pltpu.VMEM((2 * devices, LANES), jnp.float32), [VMEM] *...  0.9 us
    ppermute x1, waiting for transfers between devices, on_device(): codes_along = lax.ppermute(again(codes), ('gz', 'xy'), along)  0.78 us
    concatenate x1, other arithmetic, on_device(): jnp.concatenate([peak_code, cell_block, cell_offset, valid_patch], axis=1)  0.71 us
    ppermute x1, starting transfers between devices, on_device(): codes_along = lax.ppermute(again(codes), ('gz', 'xy'), along)  0.68 us
  transfers between devices with their start and end apart: 4, of which 2 were waited for; matrix products, arithmetic and copies ran while one was open for 3% of the time, Pallas kernels for 7%

profile of v12, /device:TPU:0, one launch (start us, length us, event | category | flops | bytes accessed | tf_op | source)
XLA Modules:
  0.0 22.0 jit_solution(18108983227080399500)
XLA Ops:
  0.6 0.5 %collective-permute-start.3 = (bf16[1,160,640]{2,1,0:T(8,128)(2,1)}, bf16[1,160,640]{2,1,0:T(8,128)(2,1)S(1)}, u32[]{:S(2)}, u32[]{:S(2)}) collective-permute-start(bf16[1,160,640]{2,1,0:T(8,128)(2,1)} %own_ref.1), channel_id=1, source_target_pairs={{4,0},{0,1},{1,5},{5,4},{12,8},{8,9},{9,13},{13,12},{20,16},{16,17... | collective-permute-start | bytes 614408 | tf_op jit(solution)/shard_map/ppermute | solution.py:439
  1.1 2.0 %collective-permute-start.2 = (bf16[1,160,640]{2,1,0:T(8,128)(2,1)}, bf16[1,160,640]{2,1,0:T(8,128)(2,1)S(1)}, u32[]{:S(2)}, u32[]{:S(2)}) collective-permute-start(bf16[1,160,640]{2,1,0:T(8,128)(2,1)} %own_ref.1), channel_id=1, source_target_pairs={{1,9},{9,17},{17,25},{25,24},{24,16},{16,8},{8,0},{0,1},{5,13},{13... | collective-permute-start | bytes 614408 | tf_op jit(solution)/shard_map/ppermute | solution.py:440
  3.1 0.7 %pad_add_fusion.codes_ref = s32[1,4,4]{2,1,0:T(4,128)S(1)} fusion(s32[1,1,4]{2,1,0:T(1,128)} %param.9, s32[1,1,4]{2,1,0:T(1,128)} %param.8, s32[1,1,4]{2,1,0:T(1,128)} %param.7, s32[1,1,4]{2,1,0:T(1,128)} %param.6), kind=kLoop, calls=%fused_computation | loop fusion | flops 48 | bytes 128 | tf_op jit(solution)/shard_map/concatenate | solution.py:438
  3.9 1.3 %collective-permute-start = (s32[1,4,4]{2,1,0:T(4,128)S(1)}, s32[1,4,4]{2,1,0:T(4,128)S(1)}, u32[]{:S(2)}, u32[]{:S(2)}) collective-permute-start(s32[1,4,4]{2,1,0:T(4,128)S(1)} %pad_add_fusion.codes_ref), channel_id=1, source_target_pairs={{4,0},{0,1},{1,5},{5,4},{12,8},{8,9},{9,13},{13,12},{20,16},{16,17... | collective-permute-start | bytes 200 | tf_op jit(solution)/shard_map/ppermute | solution.py:441
  5.2 0.0 copy-start
  5.2 0.7 %collective-permute-start.1 = (s32[1,4,4]{2,1,0:T(4,128)S(1)}, s32[1,4,4]{2,1,0:T(4,128)S(1)}, u32[]{:S(2)}, u32[]{:S(2)}) collective-permute-start(s32[1,4,4]{2,1,0:T(4,128)S(1)} %copy_codes.1), channel_id=1, source_target_pairs={{1,9},{9,17},{17,25},{25,24},{24,16},{16,8},{8,0},{0,1},{5,13},{13... | collective-permute-start | bytes 200 | tf_op jit(solution)/shard_map/ppermute | solution.py:454
  5.8 0.5 %bank.1 = (bf16[5,160,160]{2,1,0:T(8,128)(2,1)S(1)}, bf16[28,256,256]{2,1,0:T(8,128)(2,1)S(1)}) custom-call(), custom_call_target="tpu_custom_call" | custom-call | flops 1000000000 | bytes 1000 | tf_op jit(solution)/shard_map/bank/pallas_call | solution.py:443
  6.3 0.0 copy-done
  6.3 0.7 %move_own.1 = (f32[3,160,640]{2,1,0:T(8,128)S(1)}, f32[3,8,128]{2,1,0:T(8,128)S(1)}, bf16[20,160,256]{2,1,0:T(8,128)(2,1)S(1)}) custom-call(s32[1,4,4]{2,1,0:T(4,128)S(1)} %pad_add_fusion.codes_ref, bf16[5,160,160]{2,1,0:T(8,128)(2,1)S(1)} %get-tuple-element.10.rows_ref, bf16[28,256,256]{2,1,0:T(8,128)(2,1)S(1)} %get-tuple-element.11.across_ref, ...), custom_call_target="tpu_custom_call" | custom-call | flops 1000 | bytes 1000 | tf_op jit(solution)/shard_map/move_own/pallas_call | solution.py:463
  7.0 0.5 %collective-permute-done.beside_ref = s32[1,4,4]{2,1,0:T(4,128)S(1)} collective-permute-done((s32[1,4,4]{2,1,0:T(4,128)S(1)}, s32[1,4,4]{2,1,0:T(4,128)S(1)}, u32[]{:S(2)}, u32[]{:S(2)}) %collective-permute-start) | collective-permute-done | bytes 96 | tf_op jit(solution)/shard_map/ppermute | solution.py:441
  7.6 0.0 collective-permute-done.3.image_ref
  7.6 0.4 %pairs.1 = (f32[9,8,128]{2,1,0:T(8,128)S(1)}, f32[3,8,128]{2,1,0:T(8,128)S(1)}, f32[5,176,128]{2,1,0:T(8,128)S(1)}) custom-call(f32[3,160,640]{2,1,0:T(8,128)S(1)} %get-tuple-element.12.own_moved_ref, f32[3,8,128]{2,1,0:T(8,128)S(1)} %get-tuple-element.13.own_aux_ref, bf16[20,160,256]{2,1,0:T(8,128)(2,1)S(1)} %get-tuple-element.14.downs_ref, ...), custom_call_target="tpu_custom_call" | custom-call | bytes 1000 | tf_op jit(solution)/shard_map/pairs/pallas_call | solution.py:466
  8.0 0.8 %collective-permute-done.1.along_ref = s32[1,4,4]{2,1,0:T(4,128)S(1)} collective-permute-done((s32[1,4,4]{2,1,0:T(4,128)S(1)}, s32[1,4,4]{2,1,0:T(4,128)S(1)}, u32[]{:S(2)}, u32[]{:S(2)}) %collective-permute-start.1) | collective-permute-done | bytes 96 | tf_op jit(solution)/shard_map/ppermute | solution.py:454
  8.7 0.0 collective-permute-done.2.image_ref
  8.8 0.9 %neighbours.1 = f32[64,128]{1,0:T(8,128)S(1)} custom-call(s32[1,4,4]{2,1,0:T(4,128)S(1)} %collective-permute-done.beside_ref, s32[1,4,4]{2,1,0:T(4,128)S(1)} %collective-permute-done.1.along_ref, bf16[5,160,160]{2,1,0:T(8,128)(2,1)S(1)} %get-tuple-element.10.rows_ref, bf16[28,256,256]{2,1,0:T(8,128)(2,1)S(1)} %get-tuple-element.11.across_ref, ...), custom_call_target="tpu_custom_call" | custom-call | bytes 1000 | tf_op jit(solution)/shard_map/neighbours/pallas_call | solution.py:473
  9.7 11.3 %all_to_all.11 = f32[32,2,128]{2,1,0:T(2,128)S(1)} all-to-all(f32[32,2,128]{2,1,0:T(2,128)S(1)} %bitcast.2), channel_id=1, replica_groups=mesh['gz'=8,'xy'=4] {'gz','xy'}, dimensions={0} | all-to-all | bytes 65536 | tf_op jit(solution)/shard_map/all_to_all | solution.py:480
  21.0 1.0 %relax.1 = (f32[2,1,1,4]{3,2,1,0:T(1,128)}, f32[2,1,4,8]{3,2,1,0:T(4,128)}) custom-call(f32[64,128]{1,0:T(8,128)S(1)} %bitcast.3, f32[3,8,128]{2,1,0:T(8,128)S(1)} %get-tuple-element.13.own_aux_ref), custom_call_target="tpu_custom_call" | custom-call | bytes 1000 | tf_op jit(solution)/shard_map/relax/pallas_call | solution.py:481
  (1 shorter events, 0.0 us)
Async XLA Ops:
  0.6 6.9 %collective-permute-start.3 = (bf16[1,160,640]{2,1,0:T(8,128)(2,1)}, bf16[1,160,640]{2,1,0:T(8,128)(2,1)S(1)}, u32[]{:S(2)}, u32[]{:S(2)}) collective-permute-start(bf16[1,160,640]{2,1,0:T(8,128)(2,1)} %own_ref.1), channel_id=1, source_target_pairs={{4,0},{0,1},{1,5},{5,4},{12,8},{8,9},{9,13},{13,12},{20,16},{16,17... | collective-permute-start | bytes 614408 | tf_op jit(solution)/shard_map/ppermute | solution.py:439
  1.1 7.7 %collective-permute-start.2 = (bf16[1,160,640]{2,1,0:T(8,128)(2,1)}, bf16[1,160,640]{2,1,0:T(8,128)(2,1)S(1)}, u32[]{:S(2)}, u32[]{:S(2)}) collective-permute-start(bf16[1,160,640]{2,1,0:T(8,128)(2,1)} %own_ref.1), channel_id=1, source_target_pairs={{1,9},{9,17},{17,25},{25,24},{24,16},{16,8},{8,0},{0,1},{5,13},{13... | collective-permute-start | bytes 614408 | tf_op jit(solution)/shard_map/ppermute | solution.py:440
  3.9 3.7 %collective-permute-start = (s32[1,4,4]{2,1,0:T(4,128)S(1)}, s32[1,4,4]{2,1,0:T(4,128)S(1)}, u32[]{:S(2)}, u32[]{:S(2)}) collective-permute-start(s32[1,4,4]{2,1,0:T(4,128)S(1)} %pad_add_fusion.codes_ref), channel_id=1, source_target_pairs={{4,0},{0,1},{1,5},{5,4},{12,8},{8,9},{9,13},{13,12},{20,16},{16,17... | collective-permute-start | bytes 200 | tf_op jit(solution)/shard_map/ppermute | solution.py:441
  5.2 1.2 %copy-start = (bf16[1,160,640]{2,1,0:T(8,128)(2,1)S(1)}, bf16[1,160,640]{2,1,0:T(8,128)(2,1)}, u32[]{:S(2)}) copy-start(bf16[1,160,640]{2,1,0:T(8,128)(2,1)} %own_ref.1) | copy-start | bytes 614404
  5.2 3.6 %collective-permute-start.1 = (s32[1,4,4]{2,1,0:T(4,128)S(1)}, s32[1,4,4]{2,1,0:T(4,128)S(1)}, u32[]{:S(2)}, u32[]{:S(2)}) collective-permute-start(s32[1,4,4]{2,1,0:T(4,128)S(1)} %copy_codes.1), channel_id=1, source_target_pairs={{1,9},{9,17},{17,25},{25,24},{24,16},{16,8},{8,0},{0,1},{5,13},{13... | collective-permute-start | bytes 200 | tf_op jit(solution)/shard_map/ppermute | solution.py:454

commit v13 on v11

--- a/solution.py
+++ b/solution.py
@@ -395,11 +395,14 @@
             later[o] = tuple(moved)
         now = later
     place = iota((SUBLANES, NODE_COLS), 0) + iota((SUBLANES, NODE_COLS), 1) == NODE_COLS - 1
+    line = iota((BAND_ROWS, NODE_COLS), 0)
     for q in range(2):
+        field = jnp.zeros((BAND_ROWS, NODE_COLS), jnp.float32)
         for i in range(BAND_ROWS):
             spot = BAND + (i + 1) * NODE_COLS - 1
             column = jnp.where(place, now[0][q][:, spot : spot + 1], 0.0)
-            out_ref[q, 0, i : i + 1, :] = jnp.sum(column, axis=0, keepdims=True)
+            field = jnp.where(line == i, jnp.sum(column, axis=0, keepdims=True), field)
+        out_ref[q, 0] = field
 
 
 def call(kernel, out_shape, in_specs, flops=0, **settings):

time: 22.1 us -> 22.1 us (level)
  no operation moved by 1% of the time
where the time goes in v13:
time: 22.1 us; the launch traced here: 21.9 us
  blocking collectives  11.3 us (51%)
  starting transfers between devices  4.49 us (20%)
  Pallas kernels  3.44 us (16%)
  waiting for transfers between devices  1.33 us (6%)
  other arithmetic  0.71 us (3%)
  between operations  0.67 us (3%)
    all_to_all x1, blocking collectives, on_device(): gathered = lax.all_to_all(splat, ('gz', 'xy'), 0, 0, tiled=True)  11.3 us
    ppermute x1, starting transfers between devices, on_device(): image_along = lax.ppermute(images, ('gz', 'xy'), along)  2.04 us
    ppermute x1, starting transfers between devices, on_device(): codes_beside = lax.ppermute(codes, ('gz', 'xy'), beside)  1.3 us
    pallas_call x1, Pallas kernels, on_device(): call(functools.partial(relax, strips), (jax.ShapeDtypeStruct((2, 1, 1, co...  0.98 us
    pallas_call x1, Pallas kernels, on_device(): call(neighbours, pltpu.VMEM((2 * devices, LANES), jnp.float32), [VMEM] *...  0.9 us
    ppermute x1, waiting for transfers between devices, on_device(): codes_along = lax.ppermute(again(codes), ('gz', 'xy'), along)  0.79 us
    concatenate x1, other arithmetic, on_device(): jnp.concatenate([peak_code, cell_block, cell_offset, valid_patch], axis=1)  0.71 us
    ppermute x1, starting transfers between devices, on_device(): codes_along = lax.ppermute(again(codes), ('gz', 'xy'), along)  0.68 us
  transfers between devices with their start and end apart: 4, of which 2 were waited for; matrix products, arithmetic and copies ran while one was open for 3% of the time, Pallas kernels for 7%

profile of v13, /device:TPU:0, one launch (start us, length us, event | category | flops | bytes accessed | tf_op | source)
XLA Modules:
  0.0 21.9 jit_solution(17298103711842680653)
XLA Ops:
  0.6 0.5 %collective-permute-start.2 = (bf16[1,160,640]{2,1,0:T(8,128)(2,1)}, bf16[1,160,640]{2,1,0:T(8,128)(2,1)S(1)}, u32[]{:S(2)}, u32[]{:S(2)}) collective-permute-start(bf16[1,160,640]{2,1,0:T(8,128)(2,1)} %own_ref.1), channel_id=1, source_target_pairs={{4,0},{0,1},{1,5},{5,4},{12,8},{8,9},{9,13},{13,12},{20,16},{16,17... | collective-permute-start | bytes 614408 | tf_op jit(solution)/shard_map/ppermute | solution.py:438
  1.1 2.0 %collective-permute-start.3 = (bf16[1,160,640]{2,1,0:T(8,128)(2,1)}, bf16[1,160,640]{2,1,0:T(8,128)(2,1)S(1)}, u32[]{:S(2)}, u32[]{:S(2)}) collective-permute-start(bf16[1,160,640]{2,1,0:T(8,128)(2,1)} %own_ref.1), channel_id=1, source_target_pairs={{1,9},{9,17},{17,25},{25,24},{24,16},{16,8},{8,0},{0,1},{5,13},{13... | collective-permute-start | bytes 614408 | tf_op jit(solution)/shard_map/ppermute | solution.py:439
  3.1 0.7 %pad_add_fusion.codes_ref = s32[1,4,4]{2,1,0:T(4,128)S(1)} fusion(s32[1,1,4]{2,1,0:T(1,128)} %param.9, s32[1,1,4]{2,1,0:T(1,128)} %param.8, s32[1,1,4]{2,1,0:T(1,128)} %param.7, s32[1,1,4]{2,1,0:T(1,128)} %param.6), kind=kLoop, calls=%fused_computation | loop fusion | flops 48 | bytes 128 | tf_op jit(solution)/shard_map/concatenate | solution.py:437
  3.9 1.3 %collective-permute-start = (s32[1,4,4]{2,1,0:T(4,128)S(1)}, s32[1,4,4]{2,1,0:T(4,128)S(1)}, u32[]{:S(2)}, u32[]{:S(2)}) collective-permute-start(s32[1,4,4]{2,1,0:T(4,128)S(1)} %pad_add_fusion.codes_ref), channel_id=1, source_target_pairs={{4,0},{0,1},{1,5},{5,4},{12,8},{8,9},{9,13},{13,12},{20,16},{16,17... | collective-permute-start | bytes 200 | tf_op jit(solution)/shard_map/ppermute | solution.py:440
  5.2 0.0 copy-start
  5.2 0.7 %collective-permute-start.1 = (s32[1,4,4]{2,1,0:T(4,128)S(1)}, s32[1,4,4]{2,1,0:T(4,128)S(1)}, u32[]{:S(2)}, u32[]{:S(2)}) collective-permute-start(s32[1,4,4]{2,1,0:T(4,128)S(1)} %copy_codes.1), channel_id=1, source_target_pairs={{1,9},{9,17},{17,25},{25,24},{24,16},{16,8},{8,0},{0,1},{5,13},{13... | collective-permute-start | bytes 200 | tf_op jit(solution)/shard_map/ppermute | solution.py:453
  5.8 0.5 %bank.1 = (bf16[5,160,160]{2,1,0:T(8,128)(2,1)S(1)}, bf16[28,256,256]{2,1,0:T(8,128)(2,1)S(1)}) custom-call(), custom_call_target="tpu_custom_call" | custom-call | flops 1000000000 | bytes 1000 | tf_op jit(solution)/shard_map/bank/pallas_call | solution.py:442
  6.3 0.0 copy-done
  6.3 0.7 %move_own.1 = (f32[3,160,640]{2,1,0:T(8,128)S(1)}, f32[3,8,128]{2,1,0:T(8,128)S(1)}, bf16[20,160,256]{2,1,0:T(8,128)(2,1)S(1)}) custom-call(s32[1,4,4]{2,1,0:T(4,128)S(1)} %pad_add_fusion.codes_ref, bf16[5,160,160]{2,1,0:T(8,128)(2,1)S(1)} %get-tuple-element.9.rows_ref, bf16[28,256,256]{2,1,0:T(8,128)(2,1)S(1)} %get-tuple-element.10.across_ref, ...), custom_call_target="tpu_custom_call" | custom-call | flops 1000 | bytes 1000 | tf_op jit(solution)/shard_map/move_own/pallas_call | solution.py:462
  7.0 0.5 %collective-permute-done.beside_ref = s32[1,4,4]{2,1,0:T(4,128)S(1)} collective-permute-done((s32[1,4,4]{2,1,0:T(4,128)S(1)}, s32[1,4,4]{2,1,0:T(4,128)S(1)}, u32[]{:S(2)}, u32[]{:S(2)}) %collective-permute-start) | collective-permute-done | bytes 96 | tf_op jit(solution)/shard_map/ppermute | solution.py:440
  7.6 0.0 collective-permute-done.2.image_ref
  7.6 0.4 %pairs.1 = (f32[9,8,128]{2,1,0:T(8,128)S(1)}, f32[3,8,128]{2,1,0:T(8,128)S(1)}) custom-call(f32[3,160,640]{2,1,0:T(8,128)S(1)} %get-tuple-element.11.own_moved_ref, f32[3,8,128]{2,1,0:T(8,128)S(1)} %get-tuple-element.12.own_aux_ref, bf16[20,160,256]{2,1,0:T(8,128)(2,1)S(1)} %get-tuple-element.13.downs_ref, s32[1,4,4]{2,1,0:T(4,128)S(1)} %collective-permute-done.beside_ref, ...), custom_call_target="tpu_custom_call" | custom-call | bytes 1000 | tf_op jit(solution)/shard_map/pairs/pallas_call | solution.py:465
  8.0 0.8 %collective-permute-done.1.along_ref = s32[1,4,4]{2,1,0:T(4,128)S(1)} collective-permute-done((s32[1,4,4]{2,1,0:T(4,128)S(1)}, s32[1,4,4]{2,1,0:T(4,128)S(1)}, u32[]{:S(2)}, u32[]{:S(2)}) %collective-permute-start.1) | collective-permute-done | bytes 96 | tf_op jit(solution)/shard_map/ppermute | solution.py:453
  8.7 0.0 collective-permute-done.3.second_ref
  8.8 0.9 %neighbours.1 = f32[64,128]{1,0:T(8,128)S(1)} custom-call(s32[1,4,4]{2,1,0:T(4,128)S(1)} %collective-permute-done.beside_ref, s32[1,4,4]{2,1,0:T(4,128)S(1)} %collective-permute-done.1.along_ref, bf16[5,160,160]{2,1,0:T(8,128)(2,1)S(1)} %get-tuple-element.9.rows_ref, bf16[28,256,256]{2,1,0:T(8,128)(2,1)S(1)} %get-tuple-element.10.across_ref, ...), custom_call_target="tpu_custom_call" | custom-call | bytes 1000 | tf_op jit(solution)/shard_map/neighbours/pallas_call | solution.py:472
  9.7 11.3 %all_to_all.11 = f32[32,2,128]{2,1,0:T(2,128)S(1)} all-to-all(f32[32,2,128]{2,1,0:T(2,128)S(1)} %bitcast.2), channel_id=1, replica_groups=mesh['gz'=8,'xy'=4] {'gz','xy'}, dimensions={0} | all-to-all | bytes 65536 | tf_op jit(solution)/shard_map/all_to_all | solution.py:479
  21.0 1.0 %relax.1 = (f32[2,1,1,4]{3,2,1,0:T(1,128)}, f32[2,1,4,8]{3,2,1,0:T(4,128)}) custom-call(f32[64,128]{1,0:T(8,128)S(1)} %bitcast.3, f32[3,8,128]{2,1,0:T(8,128)S(1)} %get-tuple-element.12.own_aux_ref), custom_call_target="tpu_custom_call" | custom-call | bytes 1000 | tf_op jit(solution)/shard_map/relax/pallas_call | solution.py:480
  (1 shorter events, 0.0 us)
Async XLA Ops:
  0.6 6.9 %collective-permute-start.2 = (bf16[1,160,640]{2,1,0:T(8,128)(2,1)}, bf16[1,160,640]{2,1,0:T(8,128)(2,1)S(1)}, u32[]{:S(2)}, u32[]{:S(2)}) collective-permute-start(bf16[1,160,640]{2,1,0:T(8,128)(2,1)} %own_ref.1), channel_id=1, source_target_pairs={{4,0},{0,1},{1,5},{5,4},{12,8},{8,9},{9,13},{13,12},{20,16},{16,17... | collective-permute-start | bytes 614408 | tf_op jit(solution)/shard_map/ppermute | solution.py:438
  1.1 7.7 %collective-permute-start.3 = (bf16[1,160,640]{2,1,0:T(8,128)(2,1)}, bf16[1,160,640]{2,1,0:T(8,128)(2,1)S(1)}, u32[]{:S(2)}, u32[]{:S(2)}) collective-permute-start(bf16[1,160,640]{2,1,0:T(8,128)(2,1)} %own_ref.1), channel_id=1, source_target_pairs={{1,9},{9,17},{17,25},{25,24},{24,16},{16,8},{8,0},{0,1},{5,13},{13... | collective-permute-start | bytes 614408 | tf_op jit(solution)/shard_map/ppermute | solution.py:439
  3.9 3.7 %collective-permute-start = (s32[1,4,4]{2,1,0:T(4,128)S(1)}, s32[1,4,4]{2,1,0:T(4,128)S(1)}, u32[]{:S(2)}, u32[]{:S(2)}) collective-permute-start(s32[1,4,4]{2,1,0:T(4,128)S(1)} %pad_add_fusion.codes_ref), channel_id=1, source_target_pairs={{4,0},{0,1},{1,5},{5,4},{12,8},{8,9},{9,13},{13,12},{20,16},{16,17... | collective-permute-start | bytes 200 | tf_op jit(solution)/shard_map/ppermute | solution.py:440
  5.2 1.2 %copy-start = (bf16[1,160,640]{2,1,0:T(8,128)(2,1)S(1)}, bf16[1,160,640]{2,1,0:T(8,128)(2,1)}, u32[]{:S(2)}) copy-start(bf16[1,160,640]{2,1,0:T(8,128)(2,1)} %own_ref.1) | copy-start | bytes 614404
  5.2 3.6 %collective-permute-start.1 = (s32[1,4,4]{2,1,0:T(4,128)S(1)}, s32[1,4,4]{2,1,0:T(4,128)S(1)}, u32[]{:S(2)}, u32[]{:S(2)}) collective-permute-start(s32[1,4,4]{2,1,0:T(4,128)S(1)} %copy_codes.1), channel_id=1, source_target_pairs={{1,9},{9,17},{17,25},{25,24},{24,16},{16,8},{8,0},{0,1},{5,13},{13... | collective-permute-start | bytes 200 | tf_op jit(solution)/shard_map/ppermute | solution.py:453

commit v14 on v13

--- a/solution.py
+++ b/solution.py
@@ -136,7 +136,9 @@
 
 def peaks_of(codes):
     lane = iota((1, codes.shape[1]), 1)
-    return [jnp.sum(jnp.where(lane == j, codes[:1], 0)) for j in range(codes.shape[1])]
+    first = codes[:1].astype(jnp.float32)
+    picks = [jnp.sum(jnp.where(lane == j, first, 0.0)) for j in range(codes.shape[1])]
+    return [pick.astype(jnp.int32) for pick in picks]
 
 
 def roles():

time: 22.1 us -> 22.1 us (level)
  no operation moved by 1% of the time
where the time goes in v14:
time: 22.1 us; the launch traced here: 21.9 us
  blocking collectives  11.3 us (51%)
  starting transfers between devices  4.49 us (20%)
  Pallas kernels  3.45 us (16%)
  waiting for transfers between devices  1.33 us (6%)
  other arithmetic  0.71 us (3%)
  between operations  0.67 us (3%)
    all_to_all x1, blocking collectives, on_device(): gathered = lax.all_to_all(splat, ('gz', 'xy'), 0, 0, tiled=True)  11.3 us
    ppermute x1, starting transfers between devices, on_device(): image_along = lax.ppermute(images, ('gz', 'xy'), along)  2.04 us
    ppermute x1, starting transfers between devices, on_device(): codes_beside = lax.ppermute(codes, ('gz', 'xy'), beside)  1.3 us
    pallas_call x1, Pallas kernels, on_device(): call(functools.partial(relax, strips), (jax.ShapeDtypeStruct((2, 1, 1, co...  0.98 us
    pallas_call x1, Pallas kernels, on_device(): call(neighbours, pltpu.VMEM((2 * devices, LANES), jnp.float32), [VMEM] *...  0.91 us
    ppermute x1, waiting for transfers between devices, on_device(): codes_along = lax.ppermute(again(codes), ('gz', 'xy'), along)  0.79 us
    concatenate x1, other arithmetic, on_device(): jnp.concatenate([peak_code, cell_block, cell_offset, valid_patch], axis=1)  0.71 us
    ppermute x1, starting transfers between devices, on_device(): codes_along = lax.ppermute(again(codes), ('gz', 'xy'), along)  0.68 us
  transfers between devices with their start and end apart: 4, of which 2 were waited for; matrix products, arithmetic and copies ran while one was open for 3% of the time, Pallas kernels for 7%

profile of v14, /device:TPU:0, one launch (start us, length us, event | category | flops | bytes accessed | tf_op | source)
XLA Modules:
  0.0 21.9 jit_solution(18408031937982055564)
XLA Ops:
  0.6 0.5 %collective-permute-start.2 = (bf16[1,160,640]{2,1,0:T(8,128)(2,1)}, bf16[1,160,640]{2,1,0:T(8,128)(2,1)S(1)}, u32[]{:S(2)}, u32[]{:S(2)}) collective-permute-start(bf16[1,160,640]{2,1,0:T(8,128)(2,1)} %own_ref.1), channel_id=1, source_target_pairs={{4,0},{0,1},{1,5},{5,4},{12,8},{8,9},{9,13},{13,12},{20,16},{16,17... | collective-permute-start | bytes 614408 | tf_op jit(solution)/shard_map/ppermute | solution.py:440
  1.1 2.0 %collective-permute-start.3 = (bf16[1,160,640]{2,1,0:T(8,128)(2,1)}, bf16[1,160,640]{2,1,0:T(8,128)(2,1)S(1)}, u32[]{:S(2)}, u32[]{:S(2)}) collective-permute-start(bf16[1,160,640]{2,1,0:T(8,128)(2,1)} %own_ref.1), channel_id=1, source_target_pairs={{1,9},{9,17},{17,25},{25,24},{24,16},{16,8},{8,0},{0,1},{5,13},{13... | collective-permute-start | bytes 614408 | tf_op jit(solution)/shard_map/ppermute | solution.py:441
  3.1 0.7 %pad_add_fusion.codes_ref = s32[1,4,4]{2,1,0:T(4,128)S(1)} fusion(s32[1,1,4]{2,1,0:T(1,128)} %param.9, s32[1,1,4]{2,1,0:T(1,128)} %param.8, s32[1,1,4]{2,1,0:T(1,128)} %param.7, s32[1,1,4]{2,1,0:T(1,128)} %param.6), kind=kLoop, calls=%fused_computation | loop fusion | flops 48 | bytes 128 | tf_op jit(solution)/shard_map/concatenate | solution.py:439
  3.9 1.3 %collective-permute-start = (s32[1,4,4]{2,1,0:T(4,128)S(1)}, s32[1,4,4]{2,1,0:T(4,128)S(1)}, u32[]{:S(2)}, u32[]{:S(2)}) collective-permute-start(s32[1,4,4]{2,1,0:T(4,128)S(1)} %pad_add_fusion.codes_ref), channel_id=1, source_target_pairs={{4,0},{0,1},{1,5},{5,4},{12,8},{8,9},{9,13},{13,12},{20,16},{16,17... | collective-permute-start | bytes 200 | tf_op jit(solution)/shard_map/ppermute | solution.py:442
  5.2 0.0 copy-start
  5.2 0.7 %collective-permute-start.1 = (s32[1,4,4]{2,1,0:T(4,128)S(1)}, s32[1,4,4]{2,1,0:T(4,128)S(1)}, u32[]{:S(2)}, u32[]{:S(2)}) collective-permute-start(s32[1,4,4]{2,1,0:T(4,128)S(1)} %copy_codes.1), channel_id=1, source_target_pairs={{1,9},{9,17},{17,25},{25,24},{24,16},{16,8},{8,0},{0,1},{5,13},{13... | collective-permute-start | bytes 200 | tf_op jit(solution)/shard_map/ppermute | solution.py:455
  5.8 0.5 %bank.1 = (bf16[5,160,160]{2,1,0:T(8,128)(2,1)S(1)}, bf16[28,256,256]{2,1,0:T(8,128)(2,1)S(1)}) custom-call(), custom_call_target="tpu_custom_call" | custom-call | flops 1000000000 | bytes 1000 | tf_op jit(solution)/shard_map/bank/pallas_call | solution.py:444
  6.3 0.0 copy-done
  6.3 0.7 %move_own.1 = (f32[3,160,640]{2,1,0:T(8,128)S(1)}, f32[3,8,128]{2,1,0:T(8,128)S(1)}, bf16[20,160,256]{2,1,0:T(8,128)(2,1)S(1)}) custom-call(s32[1,4,4]{2,1,0:T(4,128)S(1)} %pad_add_fusion.codes_ref, bf16[5,160,160]{2,1,0:T(8,128)(2,1)S(1)} %get-tuple-element.9.rows_ref, bf16[28,256,256]{2,1,0:T(8,128)(2,1)S(1)} %get-tuple-element.10.across_ref, ...), custom_call_target="tpu_custom_call" | custom-call | flops 1000 | bytes 1000 | tf_op jit(solution)/shard_map/move_own/pallas_call | solution.py:464
  7.0 0.5 %collective-permute-done.beside_ref = s32[1,4,4]{2,1,0:T(4,128)S(1)} collective-permute-done((s32[1,4,4]{2,1,0:T(4,128)S(1)}, s32[1,4,4]{2,1,0:T(4,128)S(1)}, u32[]{:S(2)}, u32[]{:S(2)}) %collective-permute-start) | collective-permute-done | bytes 96 | tf_op jit(solution)/shard_map/ppermute | solution.py:442
  7.6 0.0 collective-permute-done.2.image_ref
  7.6 0.4 %pairs.1 = (f32[9,8,128]{2,1,0:T(8,128)S(1)}, f32[3,8,128]{2,1,0:T(8,128)S(1)}) custom-call(f32[3,160,640]{2,1,0:T(8,128)S(1)} %get-tuple-element.11.own_moved_ref, f32[3,8,128]{2,1,0:T(8,128)S(1)} %get-tuple-element.12.own_aux_ref, bf16[20,160,256]{2,1,0:T(8,128)(2,1)S(1)} %get-tuple-element.13.downs_ref, s32[1,4,4]{2,1,0:T(4,128)S(1)} %collective-permute-done.beside_ref, ...), custom_call_target="tpu_custom_call" | custom-call | bytes 1000 | tf_op jit(solution)/shard_map/pairs/pallas_call | solution.py:467
  8.0 0.8 %collective-permute-done.1.along_ref = s32[1,4,4]{2,1,0:T(4,128)S(1)} collective-permute-done((s32[1,4,4]{2,1,0:T(4,128)S(1)}, s32[1,4,4]{2,1,0:T(4,128)S(1)}, u32[]{:S(2)}, u32[]{:S(2)}) %collective-permute-start.1) | collective-permute-done | bytes 96 | tf_op jit(solution)/shard_map/ppermute | solution.py:455
  8.7 0.0 collective-permute-done.3.second_ref
  8.8 0.9 %neighbours.1 = f32[64,128]{1,0:T(8,128)S(1)} custom-call(s32[1,4,4]{2,1,0:T(4,128)S(1)} %collective-permute-done.beside_ref, s32[1,4,4]{2,1,0:T(4,128)S(1)} %collective-permute-done.1.along_ref, bf16[5,160,160]{2,1,0:T(8,128)(2,1)S(1)} %get-tuple-element.9.rows_ref, bf16[28,256,256]{2,1,0:T(8,128)(2,1)S(1)} %get-tuple-element.10.across_ref, ...), custom_call_target="tpu_custom_call" | custom-call | bytes 1000 | tf_op jit(solution)/shard_map/neighbours/pallas_call | solution.py:474
  9.7 11.3 %all_to_all.11 = f32[32,2,128]{2,1,0:T(2,128)S(1)} all-to-all(f32[32,2,128]{2,1,0:T(2,128)S(1)} %bitcast.2), channel_id=1, replica_groups=mesh['gz'=8,'xy'=4] {'gz','xy'}, dimensions={0} | all-to-all | bytes 65536 | tf_op jit(solution)/shard_map/all_to_all | solution.py:481
  21.0 1.0 %relax.1 = (f32[2,1,1,4]{3,2,1,0:T(1,128)}, f32[2,1,4,8]{3,2,1,0:T(4,128)}) custom-call(f32[64,128]{1,0:T(8,128)S(1)} %bitcast.3, f32[3,8,128]{2,1,0:T(8,128)S(1)} %get-tuple-element.12.own_aux_ref), custom_call_target="tpu_custom_call" | custom-call | bytes 1000 | tf_op jit(solution)/shard_map/relax/pallas_call | solution.py:482
  (1 shorter events, 0.0 us)
Async XLA Ops:
  0.6 6.9 %collective-permute-start.2 = (bf16[1,160,640]{2,1,0:T(8,128)(2,1)}, bf16[1,160,640]{2,1,0:T(8,128)(2,1)S(1)}, u32[]{:S(2)}, u32[]{:S(2)}) collective-permute-start(bf16[1,160,640]{2,1,0:T(8,128)(2,1)} %own_ref.1), channel_id=1, source_target_pairs={{4,0},{0,1},{1,5},{5,4},{12,8},{8,9},{9,13},{13,12},{20,16},{16,17... | collective-permute-start | bytes 614408 | tf_op jit(solution)/shard_map/ppermute | solution.py:440
  1.1 7.7 %collective-permute-start.3 = (bf16[1,160,640]{2,1,0:T(8,128)(2,1)}, bf16[1,160,640]{2,1,0:T(8,128)(2,1)S(1)}, u32[]{:S(2)}, u32[]{:S(2)}) collective-permute-start(bf16[1,160,640]{2,1,0:T(8,128)(2,1)} %own_ref.1), channel_id=1, source_target_pairs={{1,9},{9,17},{17,25},{25,24},{24,16},{16,8},{8,0},{0,1},{5,13},{13... | collective-permute-start | bytes 614408 | tf_op jit(solution)/shard_map/ppermute | solution.py:441
  3.9 3.7 %collective-permute-start = (s32[1,4,4]{2,1,0:T(4,128)S(1)}, s32[1,4,4]{2,1,0:T(4,128)S(1)}, u32[]{:S(2)}, u32[]{:S(2)}) collective-permute-start(s32[1,4,4]{2,1,0:T(4,128)S(1)} %pad_add_fusion.codes_ref), channel_id=1, source_target_pairs={{4,0},{0,1},{1,5},{5,4},{12,8},{8,9},{9,13},{13,12},{20,16},{16,17... | collective-permute-start | bytes 200 | tf_op jit(solution)/shard_map/ppermute | solution.py:442
  5.2 1.2 %copy-start = (bf16[1,160,640]{2,1,0:T(8,128)(2,1)S(1)}, bf16[1,160,640]{2,1,0:T(8,128)(2,1)}, u32[]{:S(2)}) copy-start(bf16[1,160,640]{2,1,0:T(8,128)(2,1)} %own_ref.1) | copy-start | bytes 614404
  5.2 3.6 %collective-permute-start.1 = (s32[1,4,4]{2,1,0:T(4,128)S(1)}, s32[1,4,4]{2,1,0:T(4,128)S(1)}, u32[]{:S(2)}, u32[]{:S(2)}) collective-permute-start(s32[1,4,4]{2,1,0:T(4,128)S(1)} %copy_codes.1), channel_id=1, source_target_pairs={{1,9},{9,17},{17,25},{25,24},{24,16},{16,8},{8,0},{0,1},{5,13},{13... | collective-permute-start | bytes 200 | tf_op jit(solution)/shard_map/ppermute | solution.py:455
